TPU v7x, 128 devices: a whole 4x4x4 slice. The times are simulated.
128 devices in a mesh: section: 2 (over core), expert: 4 (over x), seq: 16 (over z, y).
Axes of the slice: x: 4, y: 4, z: 4, core: 2. Of those that a mesh axis runs over, the one named last changes fastest.
Arguments:
- entry_rows: bfloat16 [4, 32, 2048], P('section', 'expert'), may hold values from -6 to 6
- cache_entries: bfloat16 [2, 32, 2, 4096, 512], P('section', 'expert', None, 'seq'), may hold values from -250 to 250
- cache_lengths: int32 [4, 32], P(None, 'expert'), may hold values from 1 to 4096, as said below
- norm_gains: float32 [2, 2, 2048], P('section'), may hold values from 0.1 to 1.9
- expert_ids: int32 [2, 4, 32, 8], P('section', None, 'expert'), may hold values from 0 to 63, all different within a row; in each aligned block of 8 rows (0 to 7, 8 to 15, ..., all dimensions but the last counted through in order) at most 2 rows name the same one
- gate_weights: float32 [2, 4, 32, 8], P('section', None, 'expert'), may hold values from 0.1 to 1
- gate_weight: bfloat16 [2, 64, 768, 2048], P('section', ('expert', 'seq')), may hold values from -0.125 to 0.125
- up_weight: bfloat16 [2, 64, 768, 2048], P('section', ('expert', 'seq')), may hold values from -0.125 to 0.125
- down_weight: bfloat16 [2, 64, 768, 2048], P('section', ('expert', 'seq')), may hold values from -0.21875 to 0.21875
- codebook_ids: int32 [4, 32], P(None, 'expert'), may hold values from 0 to 1023
- codec_table: bfloat16 [1024, 2048], P(('section', 'seq')), may hold values from -6 to 6
- final_gain: float32 [2048], replicated, may hold values from 0.1 to 1.9
Outputs:
- codec_logits: float32 [4, 32, 1024], P(None, 'expert', ('section', 'seq'))
Inputs may be any that keep to these rules, and one draw needn't show every extreme that they name: `expert_ids`: in each aligned block of 8 rows (one index of expert's rows of one layer and step) no expert is named by more than 2 rows, a bound that some block reaches. `cache_lengths`: at every step some row has seen all 4096 positions.
All inputs are finite; a program needn't handle non-finite values.
Results may differ from a plain program's by a relative error of at most 0.012.
The roundings to bfloat16 on the way count: a program that leaves them out, or rounds other values in their place, can miss the bound.
Values may be sent and summed in bfloat16 or wider, within the bound.
No kernel may reach another device: no remote copies, remote signals or barrier semaphores. Data moves between devices by JAX's collectives and lax.ppermute only.
A program may use at most 128 MiB of HBM per device.

v0:
```python
import jax
import jax.numpy as jnp
from jax import lax
from jax.sharding import PartitionSpec as P

HEAD_DIM = 128
KV_HEADS = 4
CAP = 2


epsilon = 1e-06


def passed_along(value, axis, steps):
    count = lax.axis_size(axis)
    leading, last = (max(0, -steps), min(count, count - steps))
    return lax.ppermute(value, axis, [(source, source + steps) for source in range(leading, last)])


def from_root(block, axis, owner):
    block = jnp.where(lax.axis_index(axis) == owner, block, jnp.zeros_like(block))
    return lax.psum(block, axis)


def normed(values_in, gain):
    return (
        values_in
        * lax.rsqrt(jnp.mean(values_in * values_in, axis=-1, keepdims=True) + epsilon)
        * gain
    )


def experts_apply(buffer, gate_part, up_part, down_part):
    gate_out = jnp.einsum("sxnd,xfd->sxnf", buffer, gate_part, preferred_element_type=jnp.float32)
    up_out = jnp.einsum("sxnd,xfd->sxnf", buffer, up_part, preferred_element_type=jnp.float32)
    activ = (jax.nn.silu(gate_out) * up_out).astype(jnp.bfloat16)
    return jnp.einsum(
        "sxnf,xfd->sxnd", activ, down_part, preferred_element_type=jnp.float32
    ).astype(jnp.bfloat16)


def slot_numbers(chosen_ids, capacity, expert_count):
    flat_ids = chosen_ids.reshape(-1)
    onehot = (flat_ids[:, None] == jnp.arange(expert_count, dtype=jnp.int32)[None, :]).astype(
        jnp.int32
    )
    before = jnp.cumsum(onehot, axis=0) - onehot
    slot_rank = jnp.sum(before * onehot, axis=1)
    return (flat_ids * capacity + slot_rank).reshape(chosen_ids.shape)


def per_device(
    entry_rows,
    cache_entries,
    cache_lengths,
    norm_gains,
    expert_ids,
    gate_weights,
    gate_weight,
    up_weight,
    down_weight,
    codebook_ids,
    codec_table,
    final_gain,
):
    segments = lax.axis_size("section")
    seq_count = lax.axis_size("seq")
    owners = lax.axis_size("expert")
    segment_at = lax.axis_index("section")
    seq_at = lax.axis_index("seq")
    steps = cache_lengths.shape[0]
    row_count = cache_lengths.shape[1]
    feature_count = entry_rows.shape[2]
    head_count = feature_count // HEAD_DIM
    groups = head_count // KV_HEADS
    local_experts = gate_weight.shape[1]
    expert_count = local_experts * owners * seq_count
    ctx_local = cache_entries.shape[3]
    codes_local = codec_table.shape[0]
    gate_part = gate_weight[0]
    up_part = up_weight[0]
    down_part = down_weight[0]
    inputs = lax.all_gather(entry_rows, "section", axis=0, tiled=True)
    code_start = (segment_at * seq_count + seq_at) * codes_local
    picked_codes = (
        codebook_ids.reshape(-1)[:, None] - code_start
        == jnp.arange(codes_local, dtype=jnp.int32)[None, :]
    ).astype(jnp.bfloat16)
    codec_part = jnp.dot(picked_codes, codec_table, preferred_element_type=jnp.float32).reshape(
        steps, row_count, feature_count
    )
    codec_rows = lax.psum(codec_part.astype(jnp.bfloat16), ("section", "seq")).astype(jnp.float32)
    cache_local = cache_entries[0]
    key_rows = cache_local[:, 0].reshape(row_count, ctx_local, KV_HEADS, HEAD_DIM)
    value_rows = (
        cache_local[:, 1].astype(jnp.float32).reshape(row_count, ctx_local, KV_HEADS, HEAD_DIM)
    )
    positions = seq_at * ctx_local + jnp.arange(ctx_local, dtype=jnp.int32)
    owner_range = jnp.arange(owners, dtype=jnp.int32)[:, None, None]
    expert_range = jnp.arange(local_experts, dtype=jnp.int32)[None, :, None]
    capacity_range = jnp.arange(CAP, dtype=jnp.int32)[None, None, :]
    column_slots = (
        ((owner_range * seq_count + seq_at) * local_experts + expert_range) * CAP + capacity_range
    ).reshape(-1)
    arriving = jnp.zeros((row_count, feature_count), jnp.bfloat16)
    finished = jnp.zeros((steps, row_count, feature_count), jnp.bfloat16)
    for clock_tick in range(steps + segments - 1):
        offset = clock_tick - segment_at
        step_at = jnp.clip(offset, 0, steps - 1)
        fresh_rows = inputs[min(clock_tick, steps - 1)].astype(jnp.float32)
        hidden_in = jnp.where(segment_at == 0, fresh_rows, arriving.astype(jnp.float32))
        codec_now = lax.dynamic_index_in_dim(codec_rows, step_at, 0, keepdims=False)
        hidden_in = hidden_in + jnp.where(segment_at == segments // 2, codec_now, 0.0)
        layer_lengths_now = lax.dynamic_index_in_dim(cache_lengths, step_at, 0, keepdims=False)
        layer_ids_now = lax.dynamic_index_in_dim(expert_ids[0], step_at, 0, keepdims=False)
        layer_gates_now = lax.dynamic_index_in_dim(gate_weights[0], step_at, 0, keepdims=False)
        queries = (
            normed(hidden_in, norm_gains[0, 0])
            .astype(jnp.bfloat16)
            .reshape(row_count, KV_HEADS, groups, HEAD_DIM)
        )
        scores = jnp.einsum(
            "rkgd,rpkd->rkgp", queries, key_rows, preferred_element_type=jnp.float32
        ) * HEAD_DIM ** (-0.5)
        live_mask = (positions[None, :] < layer_lengths_now[:, None])[:, None, None, :]
        scores = jnp.where(live_mask, scores, -1e30)
        live_float = live_mask.astype(jnp.float32)
        local_max = jnp.max(scores, axis=3)
        highest = lax.pmax(local_max, "seq")
        weights = jnp.exp(scores - highest[..., None]) * live_float
        totals, weighted = lax.psum(
            (jnp.sum(weights, axis=3), jnp.einsum("rkgp,rpkd->rkgd", weights, value_rows)), "seq"
        )
        middle = hidden_in + (weighted / totals[..., None]).reshape(row_count, feature_count)
        layer_moe_in = normed(middle, norm_gains[0, 1]).astype(jnp.bfloat16)
        slot_ids = slot_numbers(layer_ids_now, CAP, expert_count)
        slot_hits = (slot_ids[:, :, None] == column_slots[None, None, :]).astype(jnp.float32)
        gate_share = layer_gates_now / jnp.sum(layer_gates_now, axis=1, keepdims=True)
        mixing = jnp.sum(slot_hits * gate_share[:, :, None], axis=1)
        spread = jnp.sum(slot_hits, axis=1).astype(jnp.bfloat16)
        packed = lax.dot_general(
            spread, layer_moe_in, (((0,), (0,)), ((), ())), preferred_element_type=jnp.float32
        ).astype(jnp.bfloat16)
        packed = packed.reshape(owners, local_experts, CAP, feature_count)
        returned = lax.all_to_all(
            experts_apply(
                lax.all_to_all(packed, "expert", split_axis=0, concat_axis=0, tiled=True),
                gate_part,
                up_part,
                down_part,
            ),
            "expert",
            split_axis=0,
            concat_axis=0,
            tiled=True,
        )
        returned_rows = returned.reshape(owners * local_experts * CAP, feature_count).astype(
            jnp.float32
        )
        partial_value = jnp.dot(
            mixing,
            returned_rows,
            preferred_element_type=jnp.float32,
            precision=lax.Precision.HIGHEST,
        )
        out_rows = (middle + lax.psum(partial_value, "seq")).astype(jnp.bfloat16)
        keep_mask = (offset >= 0) & (offset < steps)
        current = lax.dynamic_index_in_dim(finished, step_at, 0, keepdims=False)
        finished = lax.dynamic_update_index_in_dim(
            finished, jnp.where(keep_mask, out_rows, current), step_at, 0
        )
        arriving = passed_along(out_rows, "section", 1)
    last_rows = from_root(finished, "section", segments - 1)
    final_rows = (
        normed(last_rows.astype(jnp.float32), final_gain)
        .astype(jnp.bfloat16)
        .reshape(steps * row_count, feature_count)
    )
    logits = lax.dot_general(
        final_rows, codec_table, (((1,), (1,)), ((), ())), preferred_element_type=jnp.float32
    ) * feature_count ** (-0.5)
    return logits.reshape(steps, row_count, codes_local)


def solution(mesh):
    placed = (
        P("section", "expert", None),
        P("section", "expert", None, "seq", None),
        P(None, "expert"),
        P("section", None, None),
        P("section", None, "expert", None),
        P("section", None, "expert", None),
        P("section", ("expert", "seq"), None, None),
        P("section", ("expert", "seq"), None, None),
        P("section", ("expert", "seq"), None, None),
        P(None, "expert"),
        P(("section", "seq"), None),
        P(),
    )
    return jax.shard_map(
        per_device,
        mesh=mesh,
        in_specs=placed,
        out_specs=P(None, "expert", ("section", "seq")),
        check_vma=False,
    )
```

profile of v0, /device:TPU:1, one launch (start us, length us, event | category | flops | bytes accessed | tf_op | source)
XLA Modules:
  0.0 1519.8 jit_solution(17466324095457256231)
XLA Ops:
  9.4 6.2 copy.77
  15.6 4.6 fusion.298
  28.1 85.7 %all-reduce.13.cloned.1.call-done = bf16[4,8,2048]{2,1,0:T(8,128)(2,1)} async-done(((bf16[4,8,2048]{2,1,0:T(8,128)(2,1)}), bf16[4,8,2048]{2,1,0:T(8,128)(2,1)}) %all-reduce.13.cloned.1.call-update) | async-done | bytes 131088 | tf_op jit(solution)/shard_map/psum | solution.py:92
  116.8 3.3 fusion.300
  120.1 59.0 %pmax.35 = f32[8,4,4]{2,1,0:T(4,128)} all-reduce(f32[8,4,4]{2,1,0:T(4,128)} %get-tuple-element.93), channel_id=1, replica_groups=mesh['section'=2,'expert'=4,'seq'=16] {'seq'}, use_global_device_ids=true, to_apply=%region_3.4 | all-reduce | flops 128 | bytes 1024 | tf_op jit(solution)/shard_map/pmax | solution.py:129
  184.0 55.9 %psum.121 = f32[8,4,4]{2,1,0:T(4,128)} all-reduce(f32[8,4,4]{2,1,0:T(4,128)} %fusion.159), channel_id=1, replica_groups=mesh['section'=2,'expert'=4,'seq'=16] {'seq'}, use_global_device_ids=true, to_apply=%region_6.7 | all-reduce | flops 128 | bytes 1024 | tf_op jit(solution)/shard_map/psum | solution.py:131
  239.8 31.5 %all-reduce.15.cloned.1.call-done = f32[8,4,4,128]{3,2,1,0:T(4,128)} async-done(((f32[8,4,4,128]{3,2,1,0:T(4,128)}), f32[8,4,4,128]{3,2,1,0:T(4,128)}) %all-reduce.15.cloned.1.call-update) | async-done | bytes 65552 | tf_op jit(solution)/shard_map/psum | solution.py:131
  277.8 8.3 all_to_all.50
  286.6 3.4 fusion.66
  290.1 3.9 fusion.58
  294.8 6.7 all_to_all.51
  303.0 81.1 %all-reduce.17.cloned.1.call-done = f32[8,2048]{1,0:T(8,128)} async-done(((f32[8,2048]{1,0:T(8,128)}), f32[8,2048]{1,0:T(8,128)}) %all-reduce.17.cloned.1.call-update) | async-done | bytes 65552 | tf_op jit(solution)/shard_map/psum | solution.py:166
  394.1 58.1 %pmax.36 = f32[8,4,4]{2,1,0:T(4,128)} all-reduce(f32[8,4,4]{2,1,0:T(4,128)} %get-tuple-element.95), channel_id=1, replica_groups=mesh['section'=2,'expert'=4,'seq'=16] {'seq'}, use_global_device_ids=true, to_apply=%region_16.17 | all-reduce | flops 128 | bytes 1024 | tf_op jit(solution)/shard_map/pmax | solution.py:129
  457.0 56.0 %psum.124 = f32[8,4,4]{2,1,0:T(4,128)} all-reduce(f32[8,4,4]{2,1,0:T(4,128)} %fusion.161), channel_id=1, replica_groups=mesh['section'=2,'expert'=4,'seq'=16] {'seq'}, use_global_device_ids=true, to_apply=%region_19.20 | all-reduce | flops 128 | bytes 1024 | tf_op jit(solution)/shard_map/psum | solution.py:131
  513.0 31.5 %all-reduce.19.cloned.1.call-done = f32[8,4,4,128]{3,2,1,0:T(4,128)} async-done(((f32[8,4,4,128]{3,2,1,0:T(4,128)}), f32[8,4,4,128]{3,2,1,0:T(4,128)}) %all-reduce.19.cloned.1.call-update) | async-done | bytes 65552 | tf_op jit(solution)/shard_map/psum | solution.py:131
  552.0 8.3 all_to_all.52
  560.9 3.4 fusion.69
  564.3 3.9 fusion.55
  569.6 3.9 all-to-all-start.3
  573.6 4.3 all-to-all-done.3
  581.5 80.5 %all-reduce.21.cloned.1.call-done = f32[8,2048]{1,0:T(8,128)} async-done(((f32[8,2048]{1,0:T(8,128)}), f32[8,2048]{1,0:T(8,128)}) %all-reduce.21.cloned.1.call-update) | async-done | bytes 65552 | tf_op jit(solution)/shard_map/psum | solution.py:166
  671.9 58.1 %pmax.37 = f32[8,4,4]{2,1,0:T(4,128)} all-reduce(f32[8,4,4]{2,1,0:T(4,128)} %get-tuple-element.97), channel_id=1, replica_groups=mesh['section'=2,'expert'=4,'seq'=16] {'seq'}, use_global_device_ids=true, to_apply=%region_29.30 | all-reduce | flops 128 | bytes 1024 | tf_op jit(solution)/shard_map/pmax | solution.py:129
  734.8 55.8 %psum.127 = f32[8,4,4]{2,1,0:T(4,128)} all-reduce(f32[8,4,4]{2,1,0:T(4,128)} %fusion.163), channel_id=1, replica_groups=mesh['section'=2,'expert'=4,'seq'=16] {'seq'}, use_global_device_ids=true, to_apply=%region_32.33 | all-reduce | flops 128 | bytes 1024 | tf_op jit(solution)/shard_map/psum | solution.py:131
  790.6 31.6 %all-reduce.23.cloned.1.call-done = f32[8,4,4,128]{3,2,1,0:T(4,128)} async-done(((f32[8,4,4,128]{3,2,1,0:T(4,128)}), f32[8,4,4,128]{3,2,1,0:T(4,128)}) %all-reduce.23.cloned.1.call-update) | async-done | bytes 65552 | tf_op jit(solution)/shard_map/psum | solution.py:131
  829.8 8.3 all_to_all.53
  838.6 3.4 fusion.72
  842.1 3.9 fusion.52
  847.4 3.9 all-to-all-start.5
  851.3 4.3 all-to-all-done.5
  859.2 80.5 %all-reduce.25.cloned.1.call-done = f32[8,2048]{1,0:T(8,128)} async-done(((f32[8,2048]{1,0:T(8,128)}), f32[8,2048]{1,0:T(8,128)}) %all-reduce.25.cloned.1.call-update) | async-done | bytes 65552 | tf_op jit(solution)/shard_map/psum | solution.py:166
  949.7 58.1 %pmax.38 = f32[8,4,4]{2,1,0:T(4,128)} all-reduce(f32[8,4,4]{2,1,0:T(4,128)} %get-tuple-element.99), channel_id=1, replica_groups=mesh['section'=2,'expert'=4,'seq'=16] {'seq'}, use_global_device_ids=true, to_apply=%region_42.43 | all-reduce | flops 128 | bytes 1024 | tf_op jit(solution)/shard_map/pmax | solution.py:129
  1012.5 56.0 %psum.130 = f32[8,4,4]{2,1,0:T(4,128)} all-reduce(f32[8,4,4]{2,1,0:T(4,128)} %fusion.165), channel_id=1, replica_groups=mesh['section'=2,'expert'=4,'seq'=16] {'seq'}, use_global_device_ids=true, to_apply=%region_45.46 | all-reduce | flops 128 | bytes 1024 | tf_op jit(solution)/shard_map/psum | solution.py:131
  1068.5 31.5 %all-reduce.27.cloned.1.call-done = f32[8,4,4,128]{3,2,1,0:T(4,128)} async-done(((f32[8,4,4,128]{3,2,1,0:T(4,128)}), f32[8,4,4,128]{3,2,1,0:T(4,128)}) %all-reduce.27.cloned.1.call-update) | async-done | bytes 65552 | tf_op jit(solution)/shard_map/psum | solution.py:131
  1107.5 8.3 all_to_all.54
  1116.4 3.4 fusion.75
  1119.8 3.9 fusion.49
  1125.2 3.9 all-to-all-start.7
  1129.1 4.3 all-to-all-done.7
  1137.0 80.5 %all-reduce.29.cloned.1.call-done = f32[8,2048]{1,0:T(8,128)} async-done(((f32[8,2048]{1,0:T(8,128)}), f32[8,2048]{1,0:T(8,128)}) %all-reduce.29.cloned.1.call-update) | async-done | bytes 65552 | tf_op jit(solution)/shard_map/psum | solution.py:166
  1226.3 58.1 %pmax.39 = f32[8,4,4]{2,1,0:T(4,128)S(1)} all-reduce(f32[8,4,4]{2,1,0:T(4,128)S(1)} %get-tuple-element.101), channel_id=1, replica_groups=mesh['section'=2,'expert'=4,'seq'=16] {'seq'}, use_global_device_ids=true, to_apply=%region_55.56 | all-reduce | flops 128 | bytes 1024 | tf_op jit(solution)/shard_map/pmax | solution.py:129
  1287.6 56.0 %psum.133 = f32[8,4,4]{2,1,0:T(4,128)S(1)} all-reduce(f32[8,4,4]{2,1,0:T(4,128)S(1)} %fusion.167), channel_id=1, replica_groups=mesh['section'=2,'expert'=4,'seq'=16] {'seq'}, use_global_device_ids=true, to_apply=%region_58.59 | all-reduce | flops 128 | bytes 1024 | tf_op jit(solution)/shard_map/psum | solution.py:131
  1343.6 33.0 %all-reduce.31.cloned.1.call-done = f32[8,4,4,128]{3,2,1,0:T(4,128)} async-done(((f32[8,4,4,128]{3,2,1,0:T(4,128)}), f32[8,4,4,128]{3,2,1,0:T(4,128)}) %all-reduce.31.cloned.1.call-update) | async-done | bytes 65552 | tf_op jit(solution)/shard_map/psum | solution.py:131
  1378.0 8.1 all_to_all.55
  1386.1 3.4 fusion.78
  1389.5 3.4 fusion.46
  1396.9 4.2 all-to-all-done.9
  1402.0 81.1 %all-reduce.33.cloned.1.call-done = f32[8,2048]{1,0:T(8,128)} async-done(((f32[8,2048]{1,0:T(8,128)}), f32[8,2048]{1,0:T(8,128)}) %all-reduce.33.cloned.1.call-update) | async-done | bytes 65552 | tf_op jit(solution)/shard_map/psum | solution.py:166
  1484.6 25.6 %all-reduce.35.cloned.1.call-done = bf16[4,8,2048]{2,1,0:T(8,128)(2,1)} async-done(((bf16[4,8,2048]{2,1,0:T(8,128)(2,1)}), bf16[4,8,2048]{2,1,0:T(8,128)(2,1)}) %all-reduce.35.cloned.1.call-update) | async-done | bytes 131088 | tf_op jit(solution)/shard_map/psum | solution.py:22
  (214 shorter events, 133.8 us)
Async XLA Ops:
  6.5 283.6 %copy-start = (bf16[1,1,768,2048]{3,2,1,0:T(8,128)(2,1)S(1)}, bf16[1,1,768,2048]{3,2,1,0:T(8,128)(2,1)}, u32[]{:S(2)}) copy-start(bf16[1,1,768,2048]{3,2,1,0:T(8,128)(2,1)} %param.20) | copy-start | bytes 9437188
  6.5 107.2 %all-reduce.13.cloned.1.call-start = ((), (), s32[]{:S(2)}) async-start(), calls=%async_computation.10 | async-start | bytes 262144 | tf_op jit(solution)/shard_map/psum | solution.py:92
  9.3 262.1 %all-reduce.15.cloned.1.call-start = ((), (), s32[]{:S(2)}) async-start(), calls=%async_computation.11 | async-start | bytes 131072 | tf_op jit(solution)/shard_map/psum | solution.py:131
  15.6 4.7 copy-start.21
  15.6 4.7 copy-start.23
  15.6 4.7 copy-start.19
  15.6 6.9 copy-start.16
  15.6 9.4 copy-start.17
  116.1 174.0 %copy-start.1 = (f32[1,8,2048]{2,1,0:T(8,128)}, f32[1,8,2048]{2,1,0:T(8,128)S(1)}, u32[]{:S(2)}) copy-start(f32[1,8,2048]{2,1,0:T(8,128)S(1)} %get-tuple-element.55) | copy-start | bytes 196612
  182.2 202.0 %all-reduce.17.cloned.1.call-start = ((), (), s32[]{:S(2)}) async-start(), calls=%async_computation.12 | async-start | bytes 131072 | tf_op jit(solution)/shard_map/psum | solution.py:166
  274.3 19.8 %copy-start.10 = (f32[8,2048]{1,0:T(8,128)}, f32[8,2048]{1,0:T(8,128)S(1)}, u32[]{:S(2)}) copy-start(f32[8,2048]{1,0:T(8,128)S(1)} %reshape.818) | copy-start | bytes 196612
  286.0 0.6 copy-start.11
  303.0 241.5 %all-reduce.19.cloned.1.call-start = ((), (), s32[]{:S(2)}) async-start(), calls=%async_computation.13 | async-start | bytes 131072 | tf_op jit(solution)/shard_map/psum | solution.py:131
  385.1 4.2 collective-permute-start
  390.2 0.6 copy-start.7
  548.5 0.6 copy-start.2
  560.3 0.6 copy-start.12
  569.6 8.2 all-to-all-start.3
  573.5 88.4 %all-reduce.21.cloned.1.call-start = ((), (), s32[]{:S(2)}) async-start(), calls=%async_computation.14 | async-start | bytes 131072 | tf_op jit(solution)/shard_map/psum | solution.py:166
  580.8 241.4 %all-reduce.23.cloned.1.call-start = ((), (), s32[]{:S(2)}) async-start(), calls=%async_computation.15 | async-start | bytes 131072 | tf_op jit(solution)/shard_map/psum | solution.py:131
  662.8 4.2 collective-permute-start.1
  668.0 0.6 copy-start.8
  826.3 0.6 copy-start.3
  838.0 0.6 copy-start.13
  847.4 8.2 all-to-all-start.5
  851.3 88.4 %all-reduce.25.cloned.1.call-start = ((), (), s32[]{:S(2)}) async-start(), calls=%async_computation.16 | async-start | bytes 131072 | tf_op jit(solution)/shard_map/psum | solution.py:166
  858.6 241.4 %all-reduce.27.cloned.1.call-start = ((), (), s32[]{:S(2)}) async-start(), calls=%async_computation.17 | async-start | bytes 131072 | tf_op jit(solution)/shard_map/psum | solution.py:131
  940.6 4.2 collective-permute-start.2
  945.7 0.6 copy-start.9
  1104.0 0.6 copy-start.4
  1115.8 0.6 copy-start.14
  1125.2 8.2 all-to-all-start.7
  1129.1 88.4 %all-reduce.29.cloned.1.call-start = ((), (), s32[]{:S(2)}) async-start(), calls=%async_computation.18 | async-start | bytes 131072 | tf_op jit(solution)/shard_map/psum | solution.py:166
  1136.3 240.3 %all-reduce.31.cloned.1.call-start = ((), (), s32[]{:S(2)}) async-start(), calls=%async_computation.19 | async-start | bytes 131072 | tf_op jit(solution)/shard_map/psum | solution.py:131
  1218.4 4.2 collective-permute-start.3
  1223.5 0.6 copy-start.5
  1223.5 63.9 %copy-start.18 = (f32[8,256]{1,0:T(8,128)S(1)}, f32[8,256]{1,0:T(8,128)}, u32[]{:S(2)}) copy-start(f32[8,256]{1,0:T(8,128)} %get-tuple-element.75) | copy-start | bytes 24580
  1224.2 153.4 %copy-start.6 = (f32[8,2048]{1,0:T(8,128)S(1)}, f32[8,2048]{1,0:T(8,128)}, u32[]{:S(2)}) copy-start(f32[8,2048]{1,0:T(8,128)} %copy-done.5) | copy-start | bytes 196612
  1224.2 153.6 %copy-start.22 = (bf16[8,8]{1,0:T(8,128)(2,1)S(1)}, bf16[8,8]{1,0:T(8,128)(2,1)}, u32[]{:S(2)}) copy-start(bf16[8,8]{1,0:T(8,128)(2,1)} %get-tuple-element.10) | copy-start | bytes 388
  1389.5 11.6 copy-start.20
  1389.5 121.7 %copy-start.15 = (bf16[32,2048]{1,0:T(8,128)(2,1)S(1)}, bf16[32,2048]{1,0:T(8,128)(2,1)}, u32[]{:S(2)}) copy-start(bf16[32,2048]{1,0:T(8,128)(2,1)} %param.22) | copy-start | bytes 393220
  1389.5 121.7 %copy-start.24 = (f32[2048]{0:T(1024)S(1)}, f32[2048]{0:T(1024)}, u32[]{:S(2)}) copy-start(f32[2048]{0:T(1024)} %param.23) | copy-start | bytes 24580
  1393.5 7.5 all-to-all-start.9
  1396.8 86.2 %all-reduce.33.cloned.1.call-start = ((), (), s32[]{:S(2)}) async-start(), calls=%async_computation.20 | async-start | bytes 131072 | tf_op jit(solution)/shard_map/psum | solution.py:166
  1401.9 108.3 %all-reduce.35.cloned.1.call-start = ((), (), s32[]{:S(2)}) async-start(), calls=%async_computation.21 | async-start | bytes 262144 | tf_op jit(solution)/shard_map/psum | solution.py:22
Sparse Core Ops, SparseCore 0:
  10.6 103.1 all-reduce.12
  182.3 89.0 all-reduce.14
  303.1 80.9 all-reduce.16
  455.4 89.0 all-reduce.18
  580.9 80.9 all-reduce.20
  733.2 89.0 all-reduce.22
  858.7 80.9 all-reduce.24
  1010.9 89.0 all-reduce.26
  1136.5 80.9 all-reduce.28
  1287.5 89.0 all-reduce.30
  1402.0 80.9 all-reduce.32
  1485.4 24.7 all-reduce.34
where the time goes:
time: 1520 us
  waiting for transfers between devices  703 us (46%)
  blocking collectives  622 us (41%)
  matrix products  82.9 us (5%)
  local copies, waits for them, and re-layouts  41.3 us (3%)
  other arithmetic  36.3 us (2%)
  starting transfers between devices  20.5 us (1%)
    psum x5, waiting for transfers between devices, per_device(): out_rows = (middle + lax.psum(partial_value, 'seq')).astype(jnp.bfloat16)  404 us
    pmax x5, blocking collectives, per_device(): highest = lax.pmax(local_max, 'seq')  291 us
    psum x5, blocking collectives, per_device(): lax.psum((jnp.sum(weights, axis=3), jnp.einsum('rkgp,rpkd->rkgd', weights...  280 us
    psum x5, waiting for transfers between devices, per_device(): lax.psum((jnp.sum(weights, axis=3), jnp.einsum('rkgp,rpkd->rkgd', weights...  159 us
    psum x1, waiting for transfers between devices, per_device(): lax.psum(codec_part.astype(jnp.bfloat16), ('section', 'seq'))  85.7 us
    all_to_all x5, blocking collectives, per_device(): lax.all_to_all(packed, 'expert', split_axis=0, concat_axis=0, tiled=True)  41.1 us
  transfers between devices with their start and end apart: 20, of which 20 were waited for; matrix products, arithmetic and copies ran while one was open for 2% of the time, Pallas kernels for 0%

commit v1 on v0

v1 whole, which is shorter than its diff:
```python
import functools

import jax
import jax.numpy as jnp
from jax import lax
from jax.experimental import pallas as pl
from jax.experimental.pallas import tpu as pltpu
from jax.sharding import PartitionSpec as P

F32 = jnp.float32
BF16 = jnp.bfloat16
STEPS = 4
ROWS = 8
D = 2048
HALF = D // 2
HEAD_DIM = 128
HEADS = D // HEAD_DIM
KV_HEADS = 4
GROUPS = HEADS // KV_HEADS
TOP = 8
CAP = 2
N_EXPERT = 4
N_SEQ = 16
DESTS = N_EXPERT * N_SEQ
SLOTS = STEPS * CAP
T = STEPS * ROWS
STAT = 128
PAY = HALF + STAT
PIECE = 256
EPS = 1e-6
LOWEST = -1e30


def vmem():
    return pl.BlockSpec(memory_space=pltpu.VMEM)


def smem():
    return pl.BlockSpec(memory_space=pltpu.SMEM)


def call(body, name, ins, outs, scratch=(), limit=24, flops=0, moved=0):
    return pl.pallas_call(
        body,
        name=name,
        in_specs=ins,
        out_shape=outs,
        out_specs=jax.tree.map(lambda _: vmem(), outs),
        scratch_shapes=scratch,
        compiler_params=pltpu.CompilerParams(vmem_limit_bytes=limit << 20),
        cost_estimate=pl.CostEstimate(flops=flops, bytes_accessed=moved, transcendentals=0),
    )


def shape(*dims, dtype=BF16):
    return jax.ShapeDtypeStruct(dims, dtype)


def iota(dims, axis):
    return lax.broadcasted_iota(jnp.int32, dims, axis)


def dot(a, b, dims=((1,), (0,))):
    return lax.dot_general(a, b, (dims, ((), ())), preferred_element_type=F32)


def row_order():
    to, source = iota((T, T), 0), iota((T, T), 1)
    return (source == (to % STEPS) * ROWS + to // STEPS).astype(F32).astype(BF16)


def rms(value, gain):
    return value * lax.rsqrt(jnp.mean(value * value, axis=1, keepdims=True) + EPS) * gain


def joined(section, mine, other):
    return jnp.where(
        section == 0,
        jnp.concatenate([mine, other], axis=1),
        jnp.concatenate([other, mine], axis=1),
    )


def route_body(ids_mine, ids_other, gates_mine, gates_other, books, table, hits, mixing, cod_mine, cod_other):
    section = lax.axis_index("section")
    seq = lax.axis_index("seq")
    width = DESTS * SLOTS
    column = iota((T, width), 1)
    row = iota((T, width), 0)
    same_step = (row // ROWS) == (column // CAP) % STEPS
    below, above = iota((T, T), 0), iota((T, T), 1)
    earlier = ((below // ROWS == above // ROWS) & (above < below)).astype(F32).astype(BF16)
    order = row_order()
    for layer in range(2):
        ids = jnp.where(section == layer, ids_mine[0], ids_other[0]).reshape(T, TOP)
        gates = jnp.where(section == layer, gates_mine[0], gates_other[0]).reshape(T, TOP)
        shares = gates / jnp.sum(gates, axis=1, keepdims=True)
        named = jnp.zeros((T, width), F32)
        weight = jnp.zeros((T, width), F32)
        for k in range(TOP):
            match = (ids[:, k : k + 1] == column // SLOTS) & same_step
            named = jnp.where(match, 1.0, named)
            weight = jnp.where(match, shares[:, k : k + 1], weight)
        rank = dot(earlier, named.astype(BF16))
        keep = rank == (column % CAP).astype(F32)
        hit = jnp.where(keep, named, 0.0)
        share = jnp.where(keep, weight, 0.0)
        high = share.astype(BF16)
        low = (share - high.astype(F32)).astype(BF16)
        hits[layer] = dot(order, hit.astype(BF16)).astype(BF16)
        mixing[layer, :T] = dot(order, high).astype(BF16)
        mixing[layer, T:] = dot(order, low).astype(BF16)
    codes = table.shape[0]
    line = iota((T, codes), 0)
    wanted = jnp.zeros((T, codes), jnp.int32)
    for row_at in range(ROWS):
        for step in range(STEPS):
            wanted = jnp.where(line == row_at * STEPS + step, books[step, row_at], wanted)
    start = (section * N_SEQ + seq) * codes
    picked = (wanted - start == iota((T, codes), 1)).astype(F32).astype(BF16)
    part = dot(picked, table[...])
    first, second = part[:, :HALF], part[:, HALF:]
    cod_mine[...] = jnp.where(section == 0, first, second).astype(BF16)
    cod_other[...] = jnp.where(section == 0, second, first).astype(BF16)


def attend_body(entering, lengths, part_a, part_b, gains, cache, mine, other, kv, queries, values, stats, sems):
    section = lax.axis_index("section")
    seq = lax.axis_index("seq")
    ctx = kv.shape[2]
    copies = [pltpu.make_async_copy(cache.at[0, r], kv.at[r], sems.at[r]) for r in range(ROWS)]
    for copy in copies:
        copy.start()
    if entering:
        a = part_a[...].astype(F32).reshape(T // 2, D)
        b = part_b[...].astype(F32).reshape(T // 2, D)
        rows = jnp.where(section == 0, jnp.concatenate([a, b], axis=0), jnp.concatenate([b, a], axis=0))
        hidden = dot(row_order(), rows.astype(BF16))
    else:
        hidden = joined(section, part_a[...], part_b[...])
    normed = rms(hidden, gains[0, 0:1, :])
    values[...] = hidden
    for r in range(ROWS):
        for h in range(HEADS):
            at = (h % GROUPS) * STEPS
            queries[r, h // GROUPS, at : at + STEPS, :] = normed[
                r * STEPS : (r + 1) * STEPS, h * HEAD_DIM : (h + 1) * HEAD_DIM
            ]
    lines = GROUPS * STEPS
    step_of = iota((KV_HEADS * lines, ctx), 0) % STEPS
    position = seq * ctx + iota((KV_HEADS * lines, ctx), 1)
    lane = iota((STEPS, STAT), 1)
    for r in range(ROWS):
        copies[r].wait()
        scores = jnp.concatenate(
            [
                dot(
                    queries[r, k].astype(BF16),
                    kv[r, 0, :, k * HEAD_DIM : (k + 1) * HEAD_DIM],
                    ((1,), (1,)),
                )
                for k in range(KV_HEADS)
            ],
            axis=0,
        ) * HEAD_DIM ** (-0.5)
        limit = jnp.zeros_like(step_of)
        for step in range(STEPS):
            limit = jnp.where(step_of == step, lengths[step, r], limit)
        live = position < limit
        scores = jnp.where(live, scores, LOWEST)
        highest = jnp.max(scores, axis=1, keepdims=True)
        weights = jnp.where(live, jnp.exp(scores - highest), 0.0)
        total = jnp.sum(weights, axis=1, keepdims=True)
        some = total > 0.0
        safe = jnp.where(some, total, 1.0)
        log_sum = jnp.where(some, highest + jnp.log(safe), LOWEST)
        scaled = 1.0 / safe
        weights = weights.astype(BF16)
        line_stats = jnp.zeros((STEPS, STAT), F32)
        for k in range(KV_HEADS):
            span = slice(k * lines, (k + 1) * lines)
            out = dot(weights[span], kv[r, 1, :, k * HEAD_DIM : (k + 1) * HEAD_DIM]) * scaled[span]
            logs = jnp.broadcast_to(log_sum[span], (lines, STAT))
            for g in range(GROUPS):
                h = k * GROUPS + g
                at = slice(g * STEPS, (g + 1) * STEPS)
                rows_at = slice(r * STEPS, (r + 1) * STEPS)
                lanes_at = slice(h * HEAD_DIM, (h + 1) * HEAD_DIM)
                values[rows_at, lanes_at] = values[rows_at, lanes_at] + out[at]
                line_stats = jnp.where(lane == h, logs[at], line_stats)
        stats[r * STEPS : (r + 1) * STEPS, :] = line_stats
    logs = stats[...]
    high = logs.astype(BF16).astype(F32)
    mid = (logs - high).astype(BF16).astype(F32)
    low = (logs - high - mid).astype(BF16).astype(F32)
    lane = iota((T, STAT), 1)
    half = HEADS // 2

    def block(second):
        def moved(value, by):
            by = (by - (half if second else 0)) % STAT
            return pltpu.roll(value, by, 1) if by else value

        packed = jnp.where(lane < 2 * half, moved(mid, half), moved(low, 2 * half))
        return jnp.where(lane < half, moved(high, 0), packed)

    is_first = section == 0
    mine[:, :HALF] = jnp.where(is_first, values[:, :HALF], values[:, HALF:]).astype(BF16)
    other[:, :HALF] = jnp.where(is_first, values[:, HALF:], values[:, :HALF]).astype(BF16)
    first, second = block(False), block(True)
    mine[:, HALF:] = jnp.where(is_first, first, second).astype(BF16)
    other[:, HALF:] = jnp.where(is_first, second, first).astype(BF16)


def spread_body(layer, mine, got, hits, *rest):
    out = rest[-1]
    section = lax.axis_index("section")
    expert = lax.axis_index("expert")
    active = section == layer
    use = jnp.where(active, mine[...].astype(F32), got[...].astype(F32)).astype(BF16)
    pick = hits[layer]
    for at in range(0, PAY, 384):
        out[:, at : at + 384] = dot(pick, use[:, at : at + 384], ((0,), (0,))).astype(BF16)
    if layer == 0:
        codes = rest[0][...].astype(F32) + rest[1][...].astype(F32)
        for s in range(0, N_SEQ, 2):
            rows_at = slice((s // 4) * ROWS, (s // 4 + 1) * ROWS)
            pair = jnp.concatenate(
                [codes[rows_at, (q % 4) * PIECE : (q % 4 + 1) * PIECE] for q in (s, s + 1)], axis=0
            )
            for x in range(N_EXPERT):
                at = (x * N_SEQ + s) * SLOTS
                out[at : at + 2 * SLOTS, PAY:] = jnp.where(expert == x, pair, 0.0).astype(BF16)


def combine_body(layer, got, *outs):
    middle = outs[0]
    half = HEADS // 2
    block = N_SEQ * SLOTS
    for x in range(N_EXPERT):
        rows_at = slice(x * block, (x + 1) * block)
        packed = got[rows_at, HALF:PAY].astype(F32)
        logs = packed[:, :half] + packed[:, half : 2 * half] + packed[:, 2 * half : 3 * half]
        logs = logs.reshape(N_SEQ, SLOTS, half)
        weights = jnp.exp(logs - jnp.max(logs, axis=0, keepdims=True))
        weights = weights / jnp.sum(weights, axis=0, keepdims=True)
        for h in range(half):
            lanes_at = slice(h * HEAD_DIM, (h + 1) * HEAD_DIM)
            part = got[rows_at, lanes_at].astype(F32).reshape(N_SEQ, SLOTS, HEAD_DIM)
            middle[x * SLOTS : (x + 1) * SLOTS, lanes_at] = jnp.sum(part * weights[:, :, h : h + 1], axis=0)
    if layer == 0:
        codes = got[:, PAY:].astype(F32).reshape(DESTS, SLOTS, PIECE)
        outs[1][...] = jnp.sum(codes, axis=0)


def expert_body(mid_mine, mid_got, gains, gate, up, down, mine, other, gate_v, up_v, down_v, sems):
    section = lax.axis_index("section")
    ff = gate_v.shape[0]
    chunks = sems.shape[1]
    size = ff // chunks
    copies = {}
    for j in range(chunks):
        at = pl.ds(j * size, size)
        for i, (source, target) in enumerate(((gate, gate_v), (up, up_v))):
            copies[i, j] = pltpu.make_async_copy(source.at[0, 0, at], target.at[at], sems.at[i, j])
    for j in range(chunks):
        at = pl.ds(j * size, size)
        copies[2, j] = pltpu.make_async_copy(down.at[0, 0, at], down_v.at[at], sems.at[2, j])
    for copy in copies.values():
        copy.start()
    middle = joined(section, mid_mine[...], mid_got[...])
    moe_in = rms(middle, gains[0, 1:2, :]).astype(BF16)
    activ = []
    for j in range(chunks):
        at = slice(j * size, (j + 1) * size)
        copies[0, j].wait()
        gate_out = dot(moe_in, gate_v[at], ((1,), (1,)))
        copies[1, j].wait()
        up_out = dot(moe_in, up_v[at], ((1,), (1,)))
        activ.append((gate_out / (1.0 + jnp.exp(-gate_out)) * up_out).astype(BF16))
    total = jnp.zeros((T, D), F32)
    for j in range(chunks):
        at = slice(j * size, (j + 1) * size)
        copies[2, j].wait()
        total = total + dot(activ[j], down_v[at])
    result = total.astype(BF16).astype(F32) + middle
    first, second = result[:, :HALF], result[:, HALF:]
    mine[...] = jnp.where(section == 0, first, second).astype(BF16)
    other[...] = jnp.where(section == 0, second, first).astype(BF16)


def share_body(layer, mine, got, *rest):
    out = rest[-1]
    section = lax.axis_index("section")
    expert = lax.axis_index("expert")
    use = jnp.where(section == layer, mine[...].astype(F32), got[...].astype(F32))
    for x in range(N_EXPERT):
        rows = use[x * SLOTS : (x + 1) * SLOTS]
        pair = jnp.concatenate([rows, rows], axis=0).astype(BF16)
        if layer == 0:
            piece = jnp.where(expert == x, rest[0][...], 0.0)
            codes = jnp.concatenate([piece, piece], axis=0).astype(BF16)
        for s in range(0, N_SEQ, 2):
            at = (x * N_SEQ + s) * SLOTS
            out[at : at + 2 * SLOTS, :HALF] = pair
            if layer == 0:
                out[at : at + 2 * SLOTS, HALF:] = codes


def mix_body(layer, got, mixing, out):
    both = dot(mixing[layer], got[:, :HALF])
    hidden = (both[:T] + both[T:]).astype(BF16).astype(F32)
    if layer == 0:
        codes = got[:, HALF:].astype(F32).reshape(N_EXPERT, N_SEQ, SLOTS, PIECE)
        codes = jnp.sum(codes, axis=0)
        for s in range(N_SEQ):
            rows_at = slice((s // 4) * ROWS, (s // 4 + 1) * ROWS)
            lanes_at = slice((s % 4) * PIECE, (s % 4 + 1) * PIECE)
            out[rows_at, lanes_at] = hidden[rows_at, lanes_at] + codes[s]
    else:
        out[...] = hidden


def head_body(mine, got, gain, table, out):
    hidden = joined(lax.axis_index("section"), mine[...], got[...])
    final = rms(hidden, gain[...]).astype(BF16)
    final = dot(row_order(), final, ((0,), (0,))).astype(BF16)
    logits = dot(final, table[...], ((1,), (1,))) * D ** (-0.5)
    out[...] = logits.reshape(out.shape)


def swapped(value):
    return lax.ppermute(value, "section", [(0, 1), (1, 0)])


def exchanged(value):
    return lax.all_to_all(value, ("expert", "seq"), 0, 0, tiled=True)


def per_device(
    entry_rows,
    cache_entries,
    cache_lengths,
    norm_gains,
    expert_ids,
    gate_weights,
    gate_weight,
    up_weight,
    down_weight,
    codebook_ids,
    codec_table,
    final_gain,
):
    ctx = cache_entries.shape[3]
    kv_width = cache_entries.shape[4]
    ff = gate_weight.shape[2]
    codes = codec_table.shape[0]
    anywhere = pl.BlockSpec(memory_space=pl.ANY)
    entry_got = swapped(entry_rows)
    ids_got = swapped(expert_ids)
    gates_got = swapped(gate_weights)
    hits, mixing, cod_mine, cod_other = call(
        route_body,
        "route",
        [vmem()] * 4 + [smem(), vmem()],
        (
            shape(2, T, DESTS * SLOTS),
            shape(2, 2 * T, DESTS * SLOTS),
            shape(T, HALF),
            shape(T, HALF),
        ),
    )(expert_ids, ids_got, gate_weights, gates_got, codebook_ids, codec_table)
    cod_got = swapped(cod_other)
    part_a, part_b = entry_rows, entry_got
    for layer in range(2):
        first = layer == 0
        mine, other = call(
            functools.partial(attend_body, first),
            "attend",
            [smem(), vmem(), vmem(), vmem(), anywhere],
            (shape(T, PAY), shape(T, PAY)),
            [
                pltpu.VMEM((ROWS, 2, ctx, kv_width), BF16),
                pltpu.VMEM((ROWS, KV_HEADS, GROUPS * STEPS, HEAD_DIM), F32),
                pltpu.VMEM((T, D), F32),
                pltpu.VMEM((T, STAT), F32),
                pltpu.SemaphoreType.DMA((ROWS,)),
            ],
        )(cache_lengths, part_a, part_b, norm_gains, cache_entries)
        codec_in = (cod_mine, cod_got) if first else ()
        width = PAY + PIECE if first else PAY
        sent = call(
            functools.partial(spread_body, layer),
            "spread",
            [vmem()] * (3 + len(codec_in)),
            shape(DESTS * SLOTS, width),
        )(mine, swapped(other), hits, *codec_in)
        outs = (shape(T, HALF, dtype=F32), shape(SLOTS, PIECE, dtype=F32))
        combined = call(
            functools.partial(combine_body, layer),
            "combine",
            [vmem()],
            outs if first else outs[:1],
        )(exchanged(sent))
        middle = combined[0]
        mine, other = call(
            expert_body,
            "experts",
            [vmem()] * 3 + [anywhere] * 3,
            (shape(T, HALF), shape(T, HALF)),
            [pltpu.VMEM((ff, D), BF16)] * 3 + [pltpu.SemaphoreType.DMA((3, 3))],
            limit=32,
        )(middle, swapped(middle), norm_gains, gate_weight, up_weight, down_weight)
        pieces = combined[1:]
        sent = call(
            functools.partial(share_body, layer),
            "share",
            [vmem()] * (2 + len(pieces)),
            shape(DESTS * SLOTS, HALF + PIECE if first else HALF),
        )(mine, swapped(other), *pieces)
        part_a = call(
            functools.partial(mix_body, layer),
            "mix",
            [vmem()] * 2,
            shape(T, HALF, dtype=F32),
        )(exchanged(sent), mixing)
        part_b = swapped(part_a)
    return call(
        head_body,
        "head",
        [vmem()] * 4,
        shape(STEPS, ROWS, codes, dtype=F32),
    )(part_a, part_b, final_gain.reshape(1, D), codec_table)


def solution(mesh):
    placed = (
        P("section", "expert", None),
        P("section", "expert", None, "seq", None),
        P(None, "expert"),
        P("section", None, None),
        P("section", None, "expert", None),
        P("section", None, "expert", None),
        P("section", ("expert", "seq"), None, None),
        P("section", ("expert", "seq"), None, None),
        P("section", ("expert", "seq"), None, None),
        P(None, "expert"),
        P(("section", "seq"), None),
        P(),
    )
    return jax.shard_map(
        per_device,
        mesh=mesh,
        in_specs=placed,
        out_specs=P(None, "expert", ("section", "seq")),
        check_vma=False,
    )
```

time: 1520 us -> 157 us (0.10)
  waiting for transfers between devices: 703 us -> 9.52 us
  blocking collectives: 622 us -> 100 us
  matrix products: 82.9 us -> 0 us
  local copies, waits for them, and re-layouts: 41.3 us -> 4.47 us
  other arithmetic: 36.3 us -> 0 us
  Pallas kernels: 0 us -> 27 us
    psum x12 -> x0, waiting for transfers between devices: 674 us -> none  [the longest x5 404 us: per_device(): out_rows = (middle + lax.psum(partial_value, 'seq')).astype(jnp.bfloat16)]
    pmax x5 -> x0, blocking collectives: 291 us -> none  [per_device(): highest = lax.pmax(local_max, 'seq')]
    psum x5 -> x0, blocking collectives: 280 us -> none  [per_device(): lax.psum((jnp.sum(weights, axis=3), jnp.einsum('rkgp,rpkd->rkgd', weights...]
    dot_general x32 -> x0, matrix products: 82.9 us -> none  [the longest x5 19.1 us: experts_apply(): jnp.einsum('sxnf,xfd->sxnd', activ, down_part, preferred_element_type=jnp...]
    all_to_all x6 -> x4, blocking collectives: 47.8 us -> 100 us  [exchanged(): return lax.all_to_all(value, ('expert', 'seq'), 0, 0, tiled=True)]
    pallas_call x0 -> x14, Pallas kernels: none -> 27 us  [the longest x2 11.1 us: per_device(): call(expert_body, 'experts', [vmem()] * 3 + [anywhere] * 3, (shape(T, HAL...]
    reduce_sum x23 -> x0, other arithmetic: 20.3 us -> none  [the longest x11 11.2 us: normed(): jnp.mean(values_in * values_in, axis=-1, keepdims=True) + epsilon]
    all_to_all x4 -> x0, waiting for transfers between devices: 17.1 us -> none  [per_device(): lax.all_to_all(experts_apply(lax.all_to_all(packed, 'expert', split_axis=...]
  transfers between devices with their start and end apart: 20 -> 12, of which waited for: 20 -> 11; matrix products, arithmetic and copies ran while one was open for 2% -> 0% of each run, Pallas kernels for 0% -> 1%
where the time goes in v1:
time: 157 us
  blocking collectives  100 us (64%)
  Pallas kernels  27 us (17%)
  starting transfers between devices  15.3 us (10%)
  waiting for transfers between devices  9.52 us (6%)
  local copies, waits for them, and re-layouts  4.47 us (3%)
    all_to_all x4, blocking collectives, exchanged(): return lax.all_to_all(value, ('expert', 'seq'), 0, 0, tiled=True)  100 us
    ppermute x12, starting transfers between devices, swapped(): return lax.ppermute(value, 'section', [(0, 1), (1, 0)])  15.3 us
    pallas_call x2, Pallas kernels, per_device(): call(expert_body, 'experts', [vmem()] * 3 + [anywhere] * 3, (shape(T, HAL...  11.1 us
    ppermute x12, waiting for transfers between devices, swapped(): return lax.ppermute(value, 'section', [(0, 1), (1, 0)])  9.52 us
    pallas_call x2, Pallas kernels, per_device(): call(functools.partial(attend_body, first), 'attend', [smem(), vmem(), vm...  8.76 us
    unnamed x30, local copies, waits for them, and re-layouts  4.47 us
  transfers between devices with their start and end apart: 12, of which 11 were waited for; matrix products, arithmetic and copies ran while one was open for 0% of the time, Pallas kernels for 1%

profile of v1, /device:TPU:1, one launch (start us, length us, event | category | flops | bytes accessed | tf_op | source)
XLA Modules:
  0.0 156.7 jit_solution(6632173448499641714)
XLA Ops:
  0.0 1.4 collective-permute-start
  1.4 1.1 collective-permute-done.part_b
  2.5 2.2 %copy-done = bf16[1,8,2,256,512]{4,3,2,1,0:T(8,128)(2,1)S(1)} copy-done((bf16[1,8,2,256,512]{4,3,2,1,0:T(8,128)(2,1)S(1)}, bf16[1,8,2,256,512]{4,3,2,1,0:T(8,128)(2,1)}, u32[]{:S(2)}) %copy-start) | copy-done | bytes 4194328
  4.7 0.7 copy-done.6
  5.4 0.8 copy-done.8
  6.3 0.7 copy-done.11
  7.0 4.5 %attend.2 = (bf16[32,1152]{1,0:T(8,128)(2,1)S(1)}, bf16[32,1152]{1,0:T(8,128)(2,1)S(1)}) custom-call(s32[4,8]{1,0:T(4,128)S(1)} %copy-done.11, bf16[2,8,2048]{2,1,0:T(8,128)(2,1)S(1)} %copy-done.8, bf16[2,8,2048]{2,1,0:T(8,128)(2,1)S(1)} %collective-permute-done.part_b, f32[1,2,2048]{2,1,0:T(2,128)S(1)} %copy-done.6, bf16[1,8,2,256,512]{4,3,2,1,0:T(8,128)(2,1)S(1)} %copy-done), custom_call_target="tpu_custom_call" | custom-call | tf_op jit(solution)/shard_map/attend/pallas_call | solution.py:377
  11.4 0.4 collective-permute-start.1
  11.9 0.2 collective-permute-start.2
  12.0 0.4 collective-permute-start.3
  12.4 0.7 collective-permute-done.2.ids_other
  13.1 0.2 collective-permute-done.3.gates_other
  13.2 1.4 route.1
  14.6 0.4 collective-permute-start.4
  15.1 0.9 collective-permute-done.4.rest_1_
  16.0 0.5 spread.2
  16.5 0.0 copy-start.2
  16.5 32.4 %all_to_all.44 = bf16[64,8,1408]{2,1,0:T(8,128)(2,1)S(1)} all-to-all(bf16[64,8,1408]{2,1,0:T(8,128)(2,1)S(1)} %bitcast.9), channel_id=1, replica_groups=mesh['section'=2,'expert'=4,'seq'=16] {'expert','seq'}, dimensions={0} | all-to-all | bytes 2883584 | tf_op jit(solution)/shard_map/all_to_all | solution.py:337
  48.9 1.4 combine.2
  50.3 2.7 %collective-permute-start.5 = (f32[32,1024]{1,0:T(8,128)S(1)}, f32[32,1024]{1,0:T(8,128)S(1)}, u32[]{:S(2)}, u32[]{:S(2)}) collective-permute-start(f32[32,1024]{1,0:T(8,128)S(1)} %get-tuple-element.24.mid_mine), channel_id=1, source_target_pairs={{0,64},{64,0},{1,65},{65,1},{2,66},{66,2},{3,67},{67,3},{4,68},{68... | collective-permute-start | bytes 393224 | tf_op jit(solution)/shard_map/ppermute | solution.py:333
  53.0 1.0 collective-permute-done.5.mid_got
  54.0 5.6 %experts.2 = (bf16[32,1024]{1,0:T(8,128)(2,1)S(1)}, bf16[32,1024]{1,0:T(8,128)(2,1)S(1)}) custom-call(f32[32,1024]{1,0:T(8,128)S(1)} %get-tuple-element.24.mid_mine, f32[32,1024]{1,0:T(8,128)S(1)} %collective-permute-done.5.mid_got, f32[1,2,2048]{2,1,0:T(2,128)S(1)} %copy-done.7, bf16[1,1,768,2048]{3,2,1,0:T(8,128)(2,1)S(1)} %copy-done.2, ...), custom_call_target="tpu_custom_call" | custom-call | tf_op jit(solution)/shard_map/experts/pallas_call | solution.py:406
  59.6 0.4 collective-permute-start.6
  60.1 0.9 collective-permute-done.6.got
  61.0 0.1 share.2
  61.1 0.0 copy-start.1
  61.1 24.3 %all_to_all.45 = bf16[64,8,1280]{2,1,0:T(8,128)(2,1)S(1)} all-to-all(bf16[64,8,1280]{2,1,0:T(8,128)(2,1)S(1)} %bitcast.11), channel_id=1, replica_groups=mesh['section'=2,'expert'=4,'seq'=16] {'expert','seq'}, dimensions={0} | all-to-all | bytes 2621440 | tf_op jit(solution)/shard_map/all_to_all | solution.py:337
  85.4 0.3 mix.2.part_a
  85.7 2.8 %collective-permute-start.7 = (f32[32,1024]{1,0:T(8,128)S(1)}, f32[32,1024]{1,0:T(8,128)S(1)}, u32[]{:S(2)}, u32[]{:S(2)}) collective-permute-start(f32[32,1024]{1,0:T(8,128)S(1)} %mix.2.part_a), channel_id=1, source_target_pairs={{0,64},{64,0},{1,65},{65,1},{2,66},{66,2},{3,67},{67,3},{4,68},{68... | collective-permute-start | bytes 393224 | tf_op jit(solution)/shard_map/ppermute | solution.py:333
  88.5 1.0 collective-permute-done.7.part_b
  89.4 4.3 %attend.3 = (bf16[32,1152]{1,0:T(8,128)(2,1)S(1)}, bf16[32,1152]{1,0:T(8,128)(2,1)S(1)}) custom-call(s32[4,8]{1,0:T(4,128)S(1)} %copy-done.12, f32[32,1024]{1,0:T(8,128)S(1)} %mix.2.part_a, f32[32,1024]{1,0:T(8,128)S(1)} %collective-permute-done.7.part_b, f32[1,2,2048]{2,1,0:T(2,128)S(1)} %copy-done.7, bf16[1,8,2,256,512]{4,3,2,1,0:T(8,128)(2,1)S(1)} %copy-done.1), custom_call_target="tpu_custom_call" | custom-call | tf_op jit(solution)/shard_map/attend/pallas_call | solution.py:377
  93.8 0.6 collective-permute-start.8
  94.4 0.9 collective-permute-done.8.got
  95.3 0.5 spread.3
  95.8 22.4 %all_to_all.46 = bf16[64,8,1152]{2,1,0:T(8,128)(2,1)S(1)} all-to-all(bf16[64,8,1152]{2,1,0:T(8,128)(2,1)S(1)} %bitcast.13), channel_id=1, replica_groups=mesh['section'=2,'expert'=4,'seq'=16] {'expert','seq'}, dimensions={0} | all-to-all | bytes 2359296 | tf_op jit(solution)/shard_map/all_to_all | solution.py:337
  118.2 1.4 combine.3.mid_mine
  119.6 2.9 %collective-permute-start.9 = (f32[32,1024]{1,0:T(8,128)S(1)}, f32[32,1024]{1,0:T(8,128)S(1)}, u32[]{:S(2)}, u32[]{:S(2)}) collective-permute-start(f32[32,1024]{1,0:T(8,128)S(1)} %combine.3.mid_mine), channel_id=1, source_target_pairs={{0,64},{64,0},{1,65},{65,1},{2,66},{66,2},{3,67},{67,3},{4,68},{68... | collective-permute-start | bytes 393224 | tf_op jit(solution)/shard_map/ppermute | solution.py:333
  122.6 1.0 collective-permute-done.9.mid_got
  123.6 5.5 %experts.3 = (bf16[32,1024]{1,0:T(8,128)(2,1)S(1)}, bf16[32,1024]{1,0:T(8,128)(2,1)S(1)}) custom-call(f32[32,1024]{1,0:T(8,128)S(1)} %combine.3.mid_mine, f32[32,1024]{1,0:T(8,128)S(1)} %collective-permute-done.9.mid_got, f32[1,2,2048]{2,1,0:T(2,128)S(1)} %copy-done.7, bf16[1,1,768,2048]{3,2,1,0:T(8,128)(2,1)S(1)} %copy-done.2, ...), custom_call_target="tpu_custom_call" | custom-call | tf_op jit(solution)/shard_map/experts/pallas_call | solution.py:406
  129.1 0.4 collective-permute-start.10
  129.6 0.9 collective-permute-done.10.got
  130.5 0.1 share.3
  130.6 0.0 copy-start.13
  130.6 21.2 %all_to_all.47 = bf16[64,8,1024]{2,1,0:T(8,128)(2,1)S(1)} all-to-all(bf16[64,8,1024]{2,1,0:T(8,128)(2,1)S(1)} %bitcast.16), channel_id=1, replica_groups=mesh['section'=2,'expert'=4,'seq'=16] {'expert','seq'}, dimensions={0} | all-to-all | bytes 2097152 | tf_op jit(solution)/shard_map/all_to_all | solution.py:337
  151.8 0.3 mix.3.mine
  152.1 2.5 %collective-permute-start.11 = (f32[32,1024]{1,0:T(8,128)S(1)}, f32[32,1024]{1,0:T(8,128)S(1)}, u32[]{:S(2)}, u32[]{:S(2)}) collective-permute-start(f32[32,1024]{1,0:T(8,128)S(1)} %mix.3.mine), channel_id=1, source_target_pairs={{0,64},{64,0},{1,65},{65,1},{2,66},{66,2},{3,67},{67,3},{4,68},{68... | collective-permute-start | bytes 393224 | tf_op jit(solution)/shard_map/ppermute | solution.py:333
  154.7 1.0 collective-permute-done.11.got
  155.6 1.0 head.1
  (24 shorter events, 0.0 us)
Async XLA Ops:
  0.0 2.5 %collective-permute-start = (bf16[2,8,2048]{2,1,0:T(8,128)(2,1)}, bf16[2,8,2048]{2,1,0:T(8,128)(2,1)S(1)}, u32[]{:S(2)}, u32[]{:S(2)}) collective-permute-start(bf16[2,8,2048]{2,1,0:T(8,128)(2,1)} %part_a.1), channel_id=1, source_target_pairs={{0,64},{64,0},{1,65},{65,1},{2,66},{66,2},{3,67},{67,3},{4,68},{68... | collective-permute-start | bytes 196616 | tf_op jit(solution)/shard_map/ppermute | solution.py:333
  2.5 2.2 %copy-start = (bf16[1,8,2,256,512]{4,3,2,1,0:T(8,128)(2,1)S(1)}, bf16[1,8,2,256,512]{4,3,2,1,0:T(8,128)(2,1)}, u32[]{:S(2)}) copy-start(bf16[1,8,2,256,512]{4,3,2,1,0:T(8,128)(2,1)} %cache.3) | copy-start | bytes 12582916
  4.7 0.7 copy-start.6
  5.4 0.8 copy-start.8
  6.3 0.7 copy-start.11
  7.0 4.9 %copy-start.9 = (s32[1,4,8,8]{3,2,1,0:T(8,128)S(1)}, s32[1,4,8,8]{3,2,1,0:T(8,128)}, u32[]{:S(2)}) copy-start(s32[1,4,8,8]{3,2,1,0:T(8,128)} %ids_mine.1) | copy-start | bytes 3076
  7.0 5.1 %copy-start.10 = (f32[1,4,8,8]{3,2,1,0:T(8,128)S(1)}, f32[1,4,8,8]{3,2,1,0:T(8,128)}, u32[]{:S(2)}) copy-start(f32[1,4,8,8]{3,2,1,0:T(8,128)} %gates_mine.1) | copy-start | bytes 3076
  7.0 6.3 %copy-start.5 = (bf16[32,2048]{1,0:T(8,128)(2,1)S(1)}, bf16[32,2048]{1,0:T(8,128)(2,1)}, u32[]{:S(2)}) copy-start(bf16[32,2048]{1,0:T(8,128)(2,1)} %table.3) | copy-start | bytes 393220
  7.0 6.3 %copy-start.14 = (s32[4,8]{1,0:T(4,128)S(1)}, s32[4,8]{1,0:T(4,128)}, u32[]{:S(2)}) copy-start(s32[4,8]{1,0:T(4,128)} %books.1) | copy-start | bytes 388
  7.0 47.1 %copy-start.4 = (bf16[1,1,768,2048]{3,2,1,0:T(8,128)(2,1)S(1)}, bf16[1,1,768,2048]{3,2,1,0:T(8,128)(2,1)}, u32[]{:S(2)}) copy-start(bf16[1,1,768,2048]{3,2,1,0:T(8,128)(2,1)} %down.3) | copy-start | bytes 9437188
  11.4 4.5 %collective-permute-start.1 = (bf16[32,1152]{1,0:T(8,128)(2,1)S(1)}, bf16[32,1152]{1,0:T(8,128)(2,1)S(1)}, u32[]{:S(2)}, u32[]{:S(2)}) collective-permute-start(bf16[32,1152]{1,0:T(8,128)(2,1)S(1)} %get-tuple-element.20), channel_id=1, source_target_pairs={{0,64},{64,0},{1,65},{65,1},{2,66},{66,2},{3,67},{67,3},{4,68},{68... | collective-permute-start | bytes 221192 | tf_op jit(solution)/shard_map/ppermute | solution.py:333
  11.9 1.2 collective-permute-start.2
  12.0 1.2 collective-permute-start.3
  13.2 40.8 %copy-start.3 = (bf16[1,1,768,2048]{3,2,1,0:T(8,128)(2,1)S(1)}, bf16[1,1,768,2048]{3,2,1,0:T(8,128)(2,1)}, u32[]{:S(2)}) copy-start(bf16[1,1,768,2048]{3,2,1,0:T(8,128)(2,1)} %up.3) | copy-start | bytes 9437188
  14.6 1.3 collective-permute-start.4
  16.5 37.6 %copy-start.2 = (bf16[1,1,768,2048]{3,2,1,0:T(8,128)(2,1)S(1)}, bf16[1,1,768,2048]{3,2,1,0:T(8,128)(2,1)}, u32[]{:S(2)}) copy-start(bf16[1,1,768,2048]{3,2,1,0:T(8,128)(2,1)} %gate.3) | copy-start | bytes 9437188
  48.9 5.2 %copy-start.7 = (f32[1,2,2048]{2,1,0:T(2,128)S(1)}, f32[1,2,2048]{2,1,0:T(2,128)}, u32[]{:S(2)}) copy-start(f32[1,2,2048]{2,1,0:T(2,128)} %gains.7) | copy-start | bytes 49156
  50.3 3.7 %collective-permute-start.5 = (f32[32,1024]{1,0:T(8,128)S(1)}, f32[32,1024]{1,0:T(8,128)S(1)}, u32[]{:S(2)}, u32[]{:S(2)}) collective-permute-start(f32[32,1024]{1,0:T(8,128)S(1)} %get-tuple-element.24.mid_mine), channel_id=1, source_target_pairs={{0,64},{64,0},{1,65},{65,1},{2,66},{66,2},{3,67},{67,3},{4,68},{68... | collective-permute-start | bytes 393224 | tf_op jit(solution)/shard_map/ppermute | solution.py:333
  59.6 1.4 collective-permute-start.6
  61.1 28.4 %copy-start.1 = (bf16[1,8,2,256,512]{4,3,2,1,0:T(8,128)(2,1)S(1)}, bf16[1,8,2,256,512]{4,3,2,1,0:T(8,128)(2,1)}, u32[]{:S(2)}) copy-start(bf16[1,8,2,256,512]{4,3,2,1,0:T(8,128)(2,1)} %cache.3) | copy-start | bytes 12582916
  85.4 4.1 %copy-start.12 = (s32[4,8]{1,0:T(4,128)S(1)}, s32[4,8]{1,0:T(4,128)}, u32[]{:S(2)}) copy-start(s32[4,8]{1,0:T(4,128)} %lengths.3) | copy-start | bytes 388
  85.7 3.8 %collective-permute-start.7 = (f32[32,1024]{1,0:T(8,128)S(1)}, f32[32,1024]{1,0:T(8,128)S(1)}, u32[]{:S(2)}, u32[]{:S(2)}) collective-permute-start(f32[32,1024]{1,0:T(8,128)S(1)} %mix.2.part_a), channel_id=1, source_target_pairs={{0,64},{64,0},{1,65},{65,1},{2,66},{66,2},{3,67},{67,3},{4,68},{68... | collective-permute-start | bytes 393224 | tf_op jit(solution)/shard_map/ppermute | solution.py:333
  93.8 1.5 collective-permute-start.8
  119.6 3.9 %collective-permute-start.9 = (f32[32,1024]{1,0:T(8,128)S(1)}, f32[32,1024]{1,0:T(8,128)S(1)}, u32[]{:S(2)}, u32[]{:S(2)}) collective-permute-start(f32[32,1024]{1,0:T(8,128)S(1)} %combine.3.mid_mine), channel_id=1, source_target_pairs={{0,64},{64,0},{1,65},{65,1},{2,66},{66,2},{3,67},{67,3},{4,68},{68... | collective-permute-start | bytes 393224 | tf_op jit(solution)/shard_map/ppermute | solution.py:333
  129.1 1.3 collective-permute-start.10
  130.6 25.1 %copy-start.13 = (f32[2048]{0:T(1024)S(1)}, f32[2048]{0:T(1024)}, u32[]{:S(2)}) copy-start(f32[2048]{0:T(1024)} %param.23) | copy-start | bytes 24580
  152.1 3.5 %collective-permute-start.11 = (f32[32,1024]{1,0:T(8,128)S(1)}, f32[32,1024]{1,0:T(8,128)S(1)}, u32[]{:S(2)}, u32[]{:S(2)}) collective-permute-start(f32[32,1024]{1,0:T(8,128)S(1)} %mix.3.mine), channel_id=1, source_target_pairs={{0,64},{64,0},{1,65},{65,1},{2,66},{66,2},{3,67},{67,3},{4,68},{68... | collective-permute-start | bytes 393224 | tf_op jit(solution)/shard_map/ppermute | solution.py:333

commit v2 on v1

v2 whole, which is shorter than its diff:
```python
import functools

import jax
import jax.numpy as jnp
from jax import lax
from jax.experimental import pallas as pl
from jax.experimental.pallas import tpu as pltpu
from jax.sharding import PartitionSpec as P

F32 = jnp.float32
BF16 = jnp.bfloat16
STEPS = 4
ROWS = 8
D = 2048
HALF = D // 2
HEAD_DIM = 128
HEADS = D // HEAD_DIM
KV_HEADS = 4
GROUPS = HEADS // KV_HEADS
TOP = 8
CAP = 2
N_EXPERT = 4
N_SEQ = 16
DESTS = N_EXPERT * N_SEQ
SLOTS = STEPS * CAP
T = STEPS * ROWS
STAT = 128
PAY = HALF + STAT
PIECE = HALF // N_SEQ
EPS = 1e-6
LOWEST = -1e30


def vmem():
    return pl.BlockSpec(memory_space=pltpu.VMEM)


def hbm():
    return pl.BlockSpec(memory_space=pltpu.HBM)


def smem():
    return pl.BlockSpec(memory_space=pltpu.SMEM)


def call(body, name, ins, outs, scratch=(), limit=24):
    return pl.pallas_call(
        body,
        name=name,
        in_specs=ins,
        out_shape=outs,
        out_specs=jax.tree.map(lambda _: vmem(), outs),
        scratch_shapes=scratch,
        compiler_params=pltpu.CompilerParams(vmem_limit_bytes=limit << 20),
    )


def shape(*dims, dtype=BF16):
    return jax.ShapeDtypeStruct(dims, dtype)


def iota(dims, axis):
    return lax.broadcasted_iota(jnp.int32, dims, axis)


def dot(a, b, dims=((1,), (0,))):
    return lax.dot_general(a, b, (dims, ((), ())), preferred_element_type=F32)


def row_order():
    to, source = iota((T, T), 0), iota((T, T), 1)
    return (source == (to % STEPS) * ROWS + to // STEPS).astype(F32).astype(BF16)


def rms(value, gain):
    return value * lax.rsqrt(jnp.mean(value * value, axis=1, keepdims=True) + EPS) * gain


def joined(section, mine, other):
    return jnp.where(
        section == 0,
        jnp.concatenate([mine, other], axis=1),
        jnp.concatenate([other, mine], axis=1),
    )


def placed_rows(section, layer, ids_mine, ids_other, gates_mine, gates_other, hits, mixing):
    width = DESTS * SLOTS
    column = iota((T, width), 1)
    row = iota((T, width), 0)
    same_step = (row // ROWS) == (column // CAP) % STEPS
    below, above = iota((T, T), 0), iota((T, T), 1)
    earlier = ((below // ROWS == above // ROWS) & (above < below)).astype(F32).astype(BF16)
    order = row_order()
    ids = jnp.where(section == layer, ids_mine[0], ids_other[0]).reshape(T, TOP)
    gates = jnp.where(section == layer, gates_mine[0], gates_other[0]).reshape(T, TOP)
    shares = gates / jnp.sum(gates, axis=1, keepdims=True)
    named = jnp.zeros((T, width), F32)
    weight = jnp.zeros((T, width), F32)
    for k in range(TOP):
        match = (ids[:, k : k + 1] == column // SLOTS) & same_step
        named = jnp.where(match, 1.0, named)
        weight = jnp.where(match, shares[:, k : k + 1], weight)
    rank = dot(earlier, named.astype(BF16))
    keep = rank == (column % CAP).astype(F32)
    hit = jnp.where(keep, named, 0.0)
    share = jnp.where(keep, weight, 0.0)
    high = share.astype(BF16)
    low = (share - high.astype(F32)).astype(BF16)
    hits[layer] = dot(order, hit.astype(BF16)).astype(BF16)
    mixing[layer, :T] = dot(order, high).astype(BF16)
    mixing[layer, T:] = dot(order, low).astype(BF16)


def codec_part(section, seq, books, table):
    codes = table.shape[0]
    line = iota((T, codes), 0)
    wanted = jnp.zeros((T, codes), jnp.int32)
    for row_at in range(ROWS):
        for step in range(STEPS):
            wanted = jnp.where(line == row_at * STEPS + step, books[step, row_at], wanted)
    start = (section * N_SEQ + seq) * codes
    picked = (wanted - start == iota((T, codes), 1)).astype(F32).astype(BF16)
    return dot(picked, table[...])


def lay_queries(hidden, gain, queries, values):
    normed = rms(hidden, gain)
    values[...] = hidden
    queries[...] = jnp.zeros_like(queries)
    for r in range(ROWS):
        for h in range(HEADS):
            k = h // GROUPS
            at = h * STEPS
            queries[r, at : at + STEPS, k * HEAD_DIM : (k + 1) * HEAD_DIM] = normed[
                r * STEPS : (r + 1) * STEPS, h * HEAD_DIM : (h + 1) * HEAD_DIM
            ]


def attend_rows(seq, lengths, cache_row, queries, values, stats, scores, weights):
    lines = GROUPS * STEPS
    size = HEADS * STEPS
    ctx = scores.shape[1]
    lane = iota((STEPS, STAT), 1)
    step_of = iota((size, ctx), 0) % STEPS
    position = seq * ctx + iota((size, ctx), 1)
    for r in range(ROWS):
        keys, _ = cache_row(r)
        scores[r * size : (r + 1) * size] = dot(queries[r].astype(BF16), keys, ((1,), (1,)))
    scales = []
    for r in range(ROWS):
        limit = jnp.where(step_of == 0, lengths[0, r], 0)
        for step in range(1, STEPS):
            limit = jnp.where(step_of == step, lengths[step, r], limit)
        live = position < limit
        score = jnp.where(live, scores[r * size : (r + 1) * size] * HEAD_DIM ** (-0.5), LOWEST)
        highest = jnp.max(score, axis=1, keepdims=True)
        weight = jnp.where(live, jnp.exp(score - highest), 0.0)
        total = jnp.sum(weight, axis=1, keepdims=True)
        some = total > 0.0
        safe = jnp.where(some, total, 1.0)
        log_sum = jnp.where(some, highest + jnp.log(safe), LOWEST)
        scales.append(1.0 / safe)
        weights[r * size : (r + 1) * size] = weight.astype(BF16)
        logs = jnp.broadcast_to(log_sum, (size, STAT))
        line_stats = jnp.zeros((STEPS, STAT), F32)
        for h in range(HEADS):
            line_stats = jnp.where(lane == h, logs[h * STEPS : (h + 1) * STEPS], line_stats)
        stats[r * STEPS : (r + 1) * STEPS, :] = line_stats
    for r in range(ROWS):
        _, held = cache_row(r)
        outs = dot(weights[r * size : (r + 1) * size], held)
        rows_at = slice(r * STEPS, (r + 1) * STEPS)
        for k in range(KV_HEADS):
            span = slice(k * lines, (k + 1) * lines)
            out = outs[span, k * HEAD_DIM : (k + 1) * HEAD_DIM] * scales[r][span]
            for g in range(GROUPS):
                h = k * GROUPS + g
                lanes_at = slice(h * HEAD_DIM, (h + 1) * HEAD_DIM)
                values[rows_at, lanes_at] = values[rows_at, lanes_at] + out[g * STEPS : (g + 1) * STEPS]


def pack_halves(section, values, stats, mine, other):
    logs = stats[...]
    high = logs.astype(BF16).astype(F32)
    mid = (logs - high).astype(BF16).astype(F32)
    low = (logs - high - mid).astype(BF16).astype(F32)
    lane = iota((T, STAT), 1)
    half = HEADS // 2

    def block(second):
        def moved(value, by):
            by = (by - (half if second else 0)) % STAT
            return pltpu.roll(value, by, 1) if by else value

        packed = jnp.where(lane < 2 * half, moved(mid, half), moved(low, 2 * half))
        return jnp.where(lane < half, moved(high, 0), jnp.where(lane < 3 * half, packed, 0.0))

    is_first = section == 0
    mine[:, :HALF] = jnp.where(is_first, values[:, :HALF], values[:, HALF:]).astype(BF16)
    other[:, :HALF] = jnp.where(is_first, values[:, HALF:], values[:, :HALF]).astype(BF16)
    first, second = block(False), block(True)
    mine[:, HALF:PAY] = jnp.where(is_first, first, second).astype(BF16)
    other[:, HALF:PAY] = jnp.where(is_first, second, first).astype(BF16)


def enter_body(
    ids_in, ids_got, gates_in, gates_got, books_in, lengths_in, table_in, entry_in, entry_got, gains_in, cache,
    mine, other, hits, mixing,
    ids, gates, books, lengths, table, entry, gains, kv, queries, values, stats, scores, weights, small_sems, sems,
):
    section = lax.axis_index("section")
    seq = lax.axis_index("seq")
    small = [
        pltpu.make_async_copy(source, target, small_sems.at[i])
        for i, (source, target) in enumerate(
            (
                (entry_in, entry),
                (gains_in, gains),
                (ids_in, ids),
                (gates_in, gates),
                (books_in, books),
                (lengths_in, lengths),
                (table_in, table),
            )
        )
    ]
    copies = [pltpu.make_async_copy(cache.at[0, r], kv.at[r], sems.at[r]) for r in range(ROWS)]
    for copy in small + copies:
        copy.start()
    for copy in small:
        copy.wait()
    for layer in range(2):
        placed_rows(section, layer, ids, ids_got, gates, gates_got, hits, mixing)
    codes = codec_part(section, seq, books, table)
    first, second = codes[:, :HALF], codes[:, HALF:]
    mine[:, PAY:] = jnp.where(section == 0, first, second).astype(BF16)
    other[:, PAY:] = jnp.where(section == 0, second, first).astype(BF16)
    a = entry[...].astype(F32).reshape(T // 2, D)
    b = entry_got[...].astype(F32).reshape(T // 2, D)
    rows = jnp.where(section == 0, jnp.concatenate([a, b], axis=0), jnp.concatenate([b, a], axis=0))
    lay_queries(dot(row_order(), rows.astype(BF16)), gains[0, 0:1, :], queries, values)

    for copy in copies:
        copy.wait()
    attend_rows(seq, lengths, lambda r: (kv[r, 0], kv[r, 1]), queries, values, stats, scores, weights)
    pack_halves(section, values, stats, mine, other)


def attend_body(lengths, part_a, part_b, gains, cache, mine, other, queries, values, stats, scores, weights):
    section = lax.axis_index("section")
    lay_queries(joined(section, part_a[...], part_b[...]), gains[0, 0:1, :], queries, values)
    seq = lax.axis_index("seq")
    attend_rows(
        seq, lengths, lambda r: (cache[0, r, 0], cache[0, r, 1]), queries, values, stats, scores, weights
    )
    pack_halves(section, values, stats, mine, other)


def spread_body(layer, mine, got, hits, held):
    section = lax.axis_index("section")
    pick = hits[layer]
    use = jnp.where(section == layer, mine[...].astype(F32), got[...].astype(F32)).astype(BF16)
    for at in range(0, HALF, 512):
        held[:, at : at + 512] = dot(pick, use[:, at : at + 512], ((0,), (0,))).astype(BF16)
    last = dot(pick, use[:, HALF:PAY], ((0,), (0,)))
    if layer == 0:
        codes = mine[:, PAY:].astype(F32) + got[:, PAY:].astype(F32)
        tiles = []
        for x in range(N_EXPERT):
            for s in range(0, HALF, STAT):
                tile = codes[x * SLOTS : (x + 1) * SLOTS, s : s + STAT]
                tiles += [pltpu.roll(tile, PIECE, 1), tile]
        last = jnp.where(iota(last.shape, 1) < STAT - PIECE, last, jnp.concatenate(tiles, axis=0))
    held[:, HALF:PAY] = last.astype(BF16)


def combine_body(layer, got, *outs):
    middle = outs[0]
    half = HEADS // 2
    block = N_SEQ * SLOTS
    widen = (iota((STAT, HALF), 0) == iota((STAT, HALF), 1) // HEAD_DIM).astype(F32).astype(BF16)
    for x in range(N_EXPERT):
        rows_at = slice(x * block, (x + 1) * block)
        packed = got[rows_at, HALF:PAY].astype(F32)
        logs = packed + pltpu.roll(packed, STAT - half, 1) + pltpu.roll(packed, STAT - 2 * half, 1)
        logs = logs.reshape(N_SEQ, SLOTS, STAT)
        weights = jnp.exp(logs - jnp.max(logs, axis=0, keepdims=True))
        weights = weights / jnp.sum(weights, axis=0, keepdims=True)
        weights = weights.reshape(block, STAT)
        high = weights.astype(BF16)
        low = (weights - high.astype(F32)).astype(BF16)
        wide = dot(high, widen) + dot(low, widen)
        for at in range(0, HALF, 256):
            lanes_at = slice(at, at + 256)
            part = (got[rows_at, lanes_at].astype(F32) * wide[:, lanes_at]).reshape(N_SEQ, SLOTS, 256)
            middle[x * SLOTS : (x + 1) * SLOTS, lanes_at] = jnp.sum(part, axis=0)
        if layer == 0:
            outs[1][x * SLOTS : (x + 1) * SLOTS, :] = jnp.sum(packed.reshape(N_SEQ, SLOTS, STAT), axis=0)


def expert_body(mid_mine, mid_got, gains, gate, up, down, mine, other):
    section = lax.axis_index("section")
    ff = gate.shape[2]
    size = 256
    middle = joined(section, mid_mine[...], mid_got[...])
    moe_in = rms(middle, gains[0, 1:2, :]).astype(BF16)
    total = jnp.zeros((T, D), F32)
    for j in range(0, ff, size):
        at = slice(j, j + size)
        gate_out = dot(moe_in, gate[0, 0, at, :], ((1,), (1,)))
        up_out = dot(moe_in, up[0, 0, at, :], ((1,), (1,)))
        activ = (gate_out / (1.0 + jnp.exp(-gate_out)) * up_out).astype(BF16)
        total = total + dot(activ, down[0, 0, at, :])
    result = total.astype(BF16).astype(F32) + middle
    first, second = result[:, :HALF], result[:, HALF:]
    mine[...] = jnp.where(section == 0, first, second).astype(BF16)
    other[...] = jnp.where(section == 0, second, first).astype(BF16)


def share_body(layer, mine, got, *rest):
    held = rest[-1]
    section = lax.axis_index("section")
    use = jnp.where(section == layer, mine[...].astype(F32), got[...].astype(F32))
    if layer == 0:
        use = jnp.concatenate([use, rest[0][...]], axis=1)
    for x in range(N_EXPERT):
        rows = use[x * SLOTS : (x + 1) * SLOTS]
        pair = jnp.concatenate([rows, rows], axis=0).astype(BF16)
        for s in range(0, N_SEQ, 2):
            at = (x * N_SEQ + s) * SLOTS
            held[at : at + 2 * SLOTS, :] = pair


def mix_body(layer, got, mixing, out):
    both = dot(mixing[layer], got[:, :HALF])
    hidden = (both[:T] + both[T:]).astype(BF16).astype(F32)
    if layer == 0:
        codes = got[:, HALF:].astype(F32)
        lower = iota((SLOTS, STAT), 1) < PIECE
        for x in range(N_EXPERT):
            rows_at = slice(x * SLOTS, (x + 1) * SLOTS)
            for s in range(0, N_SEQ, 2):
                at = (x * N_SEQ + s) * SLOTS
                even, odd = codes[at : at + SLOTS], codes[at + SLOTS : at + 2 * SLOTS]
                lanes_at = slice(s * PIECE, (s + 2) * PIECE)
                tile = jnp.where(lower, pltpu.roll(even, PIECE, 1), odd)
                out[rows_at, lanes_at] = hidden[rows_at, lanes_at] + tile
    else:
        out[...] = hidden


def head_body(mine, got, gain, table, out):
    hidden = joined(lax.axis_index("section"), mine[...], got[...])
    final = rms(hidden, gain[...]).astype(BF16)
    final = dot(row_order(), final, ((0,), (0,))).astype(BF16)
    logits = dot(final, table[...], ((1,), (1,))) * D ** (-0.5)
    out[...] = logits.reshape(out.shape)


def swapped(value):
    return lax.ppermute(value, "section", [(0, 1), (1, 0)])


def in_hbm(value):
    return pltpu.with_memory_space_constraint(value, pltpu.HBM)


def exchanged(value):
    return lax.all_to_all(value, ("expert", "seq"), 0, 0, tiled=True)


def per_device(
    entry_rows,
    cache_entries,
    cache_lengths,
    norm_gains,
    expert_ids,
    gate_weights,
    gate_weight,
    up_weight,
    down_weight,
    codebook_ids,
    codec_table,
    final_gain,
):
    ctx = cache_entries.shape[3]
    kv_width = cache_entries.shape[4]
    codes = codec_table.shape[0]
    attention_scratch = [
        pltpu.VMEM((ROWS, HEADS * STEPS, kv_width), F32),
        pltpu.VMEM((T, D), F32),
        pltpu.VMEM((T, STAT), F32),
        pltpu.VMEM((ROWS * HEADS * STEPS, ctx), F32),
        pltpu.VMEM((ROWS * HEADS * STEPS, ctx), BF16),
    ]
    entry_got, ids_got, gates_got = swapped(entry_rows), swapped(expert_ids), swapped(gate_weights)
    mine, other, hits, mixing = call(
        enter_body,
        "enter",
        [hbm(), vmem()] * 2 + [hbm()] * 4 + [vmem()] + [hbm()] * 2,
        (
            shape(T, PAY + HALF),
            shape(T, PAY + HALF),
            shape(2, T, DESTS * SLOTS),
            shape(2, 2 * T, DESTS * SLOTS),
        ),
        [
            pltpu.VMEM(expert_ids.shape, jnp.int32),
            pltpu.VMEM(gate_weights.shape, F32),
            pltpu.SMEM(codebook_ids.shape, jnp.int32),
            pltpu.SMEM(cache_lengths.shape, jnp.int32),
            pltpu.VMEM(codec_table.shape, BF16),
            pltpu.VMEM(entry_rows.shape, BF16),
            pltpu.VMEM(norm_gains.shape, F32),
            pltpu.VMEM((ROWS, 2, ctx, kv_width), BF16),
            *attention_scratch,
            pltpu.SemaphoreType.DMA((7,)),
            pltpu.SemaphoreType.DMA((ROWS,)),
        ],
    )(
        in_hbm(expert_ids),
        ids_got,
        in_hbm(gate_weights),
        gates_got,
        in_hbm(codebook_ids),
        in_hbm(cache_lengths),
        in_hbm(codec_table),
        in_hbm(entry_rows),
        entry_got,
        in_hbm(norm_gains),
        in_hbm(cache_entries),
    )
    for layer in range(2):
        first = layer == 0
        if not first:
            mine, other = call(
                attend_body,
                "attend",
                [smem()] + [vmem()] * 4,
                (shape(T, PAY), shape(T, PAY)),
                attention_scratch,
            )(cache_lengths, part_a, part_b, norm_gains, cache_entries)
        sent = call(
            functools.partial(spread_body, layer),
            "spread",
            [vmem()] * 3,
            shape(DESTS * SLOTS, PAY),
        )(mine, swapped(other), hits)
        outs = (shape(T, HALF, dtype=F32), shape(T, STAT, dtype=F32))
        combined = call(
            functools.partial(combine_body, layer),
            "combine",
            [vmem()],
            outs if first else outs[:1],
        )(exchanged(sent))
        middle = combined[0]
        mine, other = call(
            expert_body,
            "experts",
            [vmem()] * 6,
            (shape(T, HALF), shape(T, HALF)),
        )(middle, swapped(middle), norm_gains, gate_weight, up_weight, down_weight)
        pieces = combined[1:]
        width = PAY if first else HALF
        sent = call(
            functools.partial(share_body, layer),
            "share",
            [vmem()] * (2 + len(pieces)),
            shape(DESTS * SLOTS, width),
        )(mine, swapped(other), *pieces)
        part_a = call(
            functools.partial(mix_body, layer),
            "mix",
            [vmem()] * 2,
            shape(T, HALF, dtype=F32),
        )(exchanged(sent), mixing)
        part_b = swapped(part_a)
    return call(
        head_body,
        "head",
        [vmem()] * 4,
        shape(STEPS, ROWS, codes, dtype=F32),
    )(part_a, part_b, final_gain.reshape(1, D), codec_table)


def solution(mesh):
    placed = (
        P("section", "expert", None),
        P("section", "expert", None, "seq", None),
        P(None, "expert"),
        P("section", None, None),
        P("section", None, "expert", None),
        P("section", None, "expert", None),
        P("section", ("expert", "seq"), None, None),
        P("section", ("expert", "seq"), None, None),
        P("section", ("expert", "seq"), None, None),
        P(None, "expert"),
        P(("section", "seq"), None),
        P(),
    )
    return jax.shard_map(
        per_device,
        mesh=mesh,
        in_specs=placed,
        out_specs=P(None, "expert", ("section", "seq")),
        check_vma=False,
    )
```

time: 157 us -> 136 us (0.87)
  Pallas kernels: 27 us -> 16.3 us
  local copies, waits for them, and re-layouts: 4.47 us -> 0.03 us
  blocking collectives: 100 us -> 95.6 us
    pallas_call x7 -> x6, Pallas kernels: 22.2 us -> 12.9 us  [the longest x2 5.47 us: per_device(): call(expert_body, 'experts', [vmem()] * 6, (shape(T, HALF), shape(T, HALF)))]
    all_to_all x4, blocking collectives: 100 us -> 95.6 us  [exchanged(): return lax.all_to_all(value, ('expert', 'seq'), 0, 0, tiled=True)]
    unnamed x30 -> x16, local copies, waits for them, and re-layouts: 4.47 us -> 0.03 us
    ppermute x12 -> x11, waiting for transfers between devices: 9.52 us -> 8.73 us  [swapped(): return lax.ppermute(value, 'section', [(0, 1), (1, 0)])]
    ppermute x12 -> x11, starting transfers between devices: 15.3 us -> 15.2 us  [swapped(): return lax.ppermute(value, 'section', [(0, 1), (1, 0)])]
  transfers between devices with their start and end apart: 12 -> 11, of which waited for: 11 -> 10; matrix products, arithmetic and copies ran while one was open for 0% -> 0% of each run, Pallas kernels for 1% -> 0%
where the time goes in v2:
time: 136 us
  blocking collectives  95.6 us (70%)
  Pallas kernels  16.3 us (12%)
  starting transfers between devices  15.2 us (11%)
  waiting for transfers between devices  8.73 us (6%)
    all_to_all x4, blocking collectives, exchanged(): return lax.all_to_all(value, ('expert', 'seq'), 0, 0, tiled=True)  95.6 us
    ppermute x11, starting transfers between devices, swapped(): return lax.ppermute(value, 'section', [(0, 1), (1, 0)])  15.2 us
    ppermute x11, waiting for transfers between devices, swapped(): return lax.ppermute(value, 'section', [(0, 1), (1, 0)])  8.73 us
    pallas_call x2, Pallas kernels, per_device(): call(expert_body, 'experts', [vmem()] * 6, (shape(T, HALF), shape(T, HALF)))  5.47 us
    pallas_call x1, Pallas kernels, per_device(): call(enter_body, 'enter', [hbm(), vmem()] * 2 + [hbm()] * 4 + [vmem()] +...  4.53 us
  transfers between devices with their start and end apart: 11, of which 10 were waited for; matrix products, arithmetic and copies ran while one was open for 0% of the time, Pallas kernels for 0%

profile of v2, /device:TPU:1, one launch (start us, length us, event | category | flops | bytes accessed | tf_op | source)
XLA Modules:
  0.0 136.1 jit_solution(6193054273586670670)
XLA Ops:
  0.0 1.4 %collective-permute-start.2 = (bf16[2,8,2048]{2,1,0:T(8,128)(2,1)}, bf16[2,8,2048]{2,1,0:T(8,128)(2,1)S(1)}, u32[]{:S(2)}, u32[]{:S(2)}) collective-permute-start(bf16[2,8,2048]{2,1,0:T(8,128)(2,1)} %entry_in.1), channel_id=1, source_target_pairs={{0,64},{64,0},{1,65},{65,1},{2,66},{66,2},{3,67},{67,3},{4,68},{68... | collective-permute-start | bytes 196616 | tf_op jit(solution)/shard_map/ppermute | solution.py:362
  1.4 0.0 collective-permute-start
  1.4 0.5 collective-permute-start.1
  1.9 0.9 collective-permute-done.ids_got
  2.8 0.2 collective-permute-done.1.gates_got
  3.0 0.0 collective-permute-done.2.entry_got
  3.0 4.5 %enter.1 = (bf16[32,2176]{1,0:T(8,128)(2,1)S(1)}, bf16[32,2176]{1,0:T(8,128)(2,1)S(1)}, bf16[2,32,512]{2,1,0:T(8,128)(2,1)S(1)}, bf16[2,64,512]{2,1,0:T(8,128)(2,1)S(1)}) custom-call(s32[1,4,8,8]{3,2,1,0:T(8,128)} %ids_in.1, s32[1,4,8,8]{3,2,1,0:T(8,128)S(1)} %collective-permute-done.ids_got, f32[1,4,8,8]{3,2,1,0:T(8,128)} %gates_in.1, ...), custom_call_target="tpu_custom_call" | custom-call | tf_op jit(solution)/shard_map/enter/pallas_call | solution.py:398
  7.5 0.4 collective-permute-start.3
  8.0 1.0 collective-permute-done.3.got
  9.0 0.5 spread.2
  9.5 0.0 copy-start.1
  9.5 29.5 %all_to_all.44 = bf16[64,8,1152]{2,1,0:T(8,128)(2,1)S(1)} all-to-all(bf16[64,8,1152]{2,1,0:T(8,128)(2,1)S(1)} %bitcast.12), channel_id=1, replica_groups=mesh['section'=2,'expert'=4,'seq'=16] {'expert','seq'}, dimensions={0} | all-to-all | bytes 2359296 | tf_op jit(solution)/shard_map/all_to_all | solution.py:370
  38.9 0.8 combine.2
  39.8 2.9 %collective-permute-start.4 = (f32[32,1024]{1,0:T(8,128)S(1)}, f32[32,1024]{1,0:T(8,128)S(1)}, u32[]{:S(2)}, u32[]{:S(2)}) collective-permute-start(f32[32,1024]{1,0:T(8,128)S(1)} %get-tuple-element.20.mid_mine), channel_id=1, source_target_pairs={{0,64},{64,0},{1,65},{65,1},{2,66},{66,2},{3,67},{67,3},{4,68},{68... | collective-permute-start | bytes 393224 | tf_op jit(solution)/shard_map/ppermute | solution.py:362
  42.7 1.0 collective-permute-done.4.mid_got
  43.7 0.0 copy-done.2
  43.7 0.0 copy-done.3
  43.7 0.0 copy-done.1
  43.7 0.0 copy-done.5
  43.7 2.7 %experts.2 = (bf16[32,1024]{1,0:T(8,128)(2,1)S(1)}, bf16[32,1024]{1,0:T(8,128)(2,1)S(1)}) custom-call(f32[32,1024]{1,0:T(8,128)S(1)} %get-tuple-element.20.mid_mine, f32[32,1024]{1,0:T(8,128)S(1)} %collective-permute-done.4.mid_got, f32[1,2,2048]{2,1,0:T(2,128)S(1)} %copy-done.5, bf16[1,1,768,2048]{3,2,1,0:T(8,128)(2,1)S(1)} %copy-done.1, ...), custom_call_target="tpu_custom_call" | custom-call | tf_op jit(solution)/shard_map/experts/pallas_call | solution.py:458
  46.4 0.5 collective-permute-start.5
  46.9 0.9 collective-permute-done.5.got
  47.8 0.1 share.2
  47.9 22.6 %all_to_all.45 = bf16[64,8,1152]{2,1,0:T(8,128)(2,1)S(1)} all-to-all(bf16[64,8,1152]{2,1,0:T(8,128)(2,1)S(1)} %bitcast.10), channel_id=1, replica_groups=mesh['section'=2,'expert'=4,'seq'=16] {'expert','seq'}, dimensions={0} | all-to-all | bytes 2359296 | tf_op jit(solution)/shard_map/all_to_all | solution.py:370
  70.5 0.3 mix.2.part_a
  70.8 2.9 %collective-permute-start.6 = (f32[32,1024]{1,0:T(8,128)S(1)}, f32[32,1024]{1,0:T(8,128)S(1)}, u32[]{:S(2)}, u32[]{:S(2)}) collective-permute-start(f32[32,1024]{1,0:T(8,128)S(1)} %mix.2.part_a), channel_id=1, source_target_pairs={{0,64},{64,0},{1,65},{65,1},{2,66},{66,2},{3,67},{67,3},{4,68},{68... | collective-permute-start | bytes 393224 | tf_op jit(solution)/shard_map/ppermute | solution.py:362
  73.7 1.0 collective-permute-done.6.part_b
  74.7 0.0 copy-done
  74.7 0.0 copy-done.6
  74.7 1.9 %attend.1 = (bf16[32,1152]{1,0:T(8,128)(2,1)S(1)}, bf16[32,1152]{1,0:T(8,128)(2,1)S(1)}) custom-call(s32[4,8]{1,0:T(4,128)S(1)} %copy-done.6, f32[32,1024]{1,0:T(8,128)S(1)} %mix.2.part_a, f32[32,1024]{1,0:T(8,128)S(1)} %collective-permute-done.6.part_b, f32[1,2,2048]{2,1,0:T(2,128)S(1)} %copy-done.5, bf16[1,8,2,256,512]{4,3,2,1,0:T(8,128)(2,1)S(1)} %copy-done), custom_call_target="tpu_custom_call" | custom-call | tf_op jit(solution)/shard_map/attend/pallas_call | solution.py:437
  76.6 0.4 collective-permute-start.7
  77.1 0.9 collective-permute-done.7.got
  78.0 0.5 spread.3
  78.5 22.4 %all_to_all.46 = bf16[64,8,1152]{2,1,0:T(8,128)(2,1)S(1)} all-to-all(bf16[64,8,1152]{2,1,0:T(8,128)(2,1)S(1)} %bitcast.11), channel_id=1, replica_groups=mesh['section'=2,'expert'=4,'seq'=16] {'expert','seq'}, dimensions={0} | all-to-all | bytes 2359296 | tf_op jit(solution)/shard_map/all_to_all | solution.py:370
  100.8 0.8 combine.3.mid_mine
  101.6 3.1 %collective-permute-start.8 = (f32[32,1024]{1,0:T(8,128)S(1)}, f32[32,1024]{1,0:T(8,128)S(1)}, u32[]{:S(2)}, u32[]{:S(2)}) collective-permute-start(f32[32,1024]{1,0:T(8,128)S(1)} %combine.3.mid_mine), channel_id=1, source_target_pairs={{0,64},{64,0},{1,65},{65,1},{2,66},{66,2},{3,67},{67,3},{4,68},{68... | collective-permute-start | bytes 393224 | tf_op jit(solution)/shard_map/ppermute | solution.py:362
  104.8 1.0 collective-permute-done.8.mid_got
  105.8 2.7 %experts.3 = (bf16[32,1024]{1,0:T(8,128)(2,1)S(1)}, bf16[32,1024]{1,0:T(8,128)(2,1)S(1)}) custom-call(f32[32,1024]{1,0:T(8,128)S(1)} %combine.3.mid_mine, f32[32,1024]{1,0:T(8,128)S(1)} %collective-permute-done.8.mid_got, f32[1,2,2048]{2,1,0:T(2,128)S(1)} %copy-done.5, bf16[1,1,768,2048]{3,2,1,0:T(8,128)(2,1)S(1)} %copy-done.1, ...), custom_call_target="tpu_custom_call" | custom-call | tf_op jit(solution)/shard_map/experts/pallas_call | solution.py:458
  108.5 0.4 collective-permute-start.9
  108.9 0.9 collective-permute-done.9.got
  109.8 0.1 share.3
  110.0 21.2 %all_to_all.47 = bf16[64,8,1024]{2,1,0:T(8,128)(2,1)S(1)} all-to-all(bf16[64,8,1024]{2,1,0:T(8,128)(2,1)S(1)} %bitcast.16), channel_id=1, replica_groups=mesh['section'=2,'expert'=4,'seq'=16] {'expert','seq'}, dimensions={0} | all-to-all | bytes 2097152 | tf_op jit(solution)/shard_map/all_to_all | solution.py:370
  131.2 0.3 mix.3.mine
  131.5 2.5 %collective-permute-start.10 = (f32[32,1024]{1,0:T(8,128)S(1)}, f32[32,1024]{1,0:T(8,128)S(1)}, u32[]{:S(2)}, u32[]{:S(2)}) collective-permute-start(f32[32,1024]{1,0:T(8,128)S(1)} %mix.3.mine), channel_id=1, source_target_pairs={{0,64},{64,0},{1,65},{65,1},{2,66},{66,2},{3,67},{67,3},{4,68},{68... | collective-permute-start | bytes 393224 | tf_op jit(solution)/shard_map/ppermute | solution.py:362
  134.0 1.0 collective-permute-done.10.got
  135.0 0.0 copy-done.4
  135.0 0.0 copy-done.7
  135.0 1.0 head.1
  (7 shorter events, 0.0 us)
Async XLA Ops:
  0.0 3.0 %collective-permute-start.2 = (bf16[2,8,2048]{2,1,0:T(8,128)(2,1)}, bf16[2,8,2048]{2,1,0:T(8,128)(2,1)S(1)}, u32[]{:S(2)}, u32[]{:S(2)}) collective-permute-start(bf16[2,8,2048]{2,1,0:T(8,128)(2,1)} %entry_in.1), channel_id=1, source_target_pairs={{0,64},{64,0},{1,65},{65,1},{2,66},{66,2},{3,67},{67,3},{4,68},{68... | collective-permute-start | bytes 196616 | tf_op jit(solution)/shard_map/ppermute | solution.py:362
  1.4 1.4 %collective-permute-start = (s32[1,4,8,8]{3,2,1,0:T(8,128)}, s32[1,4,8,8]{3,2,1,0:T(8,128)S(1)}, u32[]{:S(2)}, u32[]{:S(2)}) collective-permute-start(s32[1,4,8,8]{3,2,1,0:T(8,128)} %ids_in.1), channel_id=1, source_target_pairs={{0,64},{64,0},{1,65},{65,1},{2,66},{66,2},{3,67},{67,3},{4,68},{68... | collective-permute-start | bytes 3080 | tf_op jit(solution)/shard_map/ppermute | solution.py:362
  1.4 1.6 %collective-permute-start.1 = (f32[1,4,8,8]{3,2,1,0:T(8,128)}, f32[1,4,8,8]{3,2,1,0:T(8,128)S(1)}, u32[]{:S(2)}, u32[]{:S(2)}) collective-permute-start(f32[1,4,8,8]{3,2,1,0:T(8,128)} %gates_in.1), channel_id=1, source_target_pairs={{0,64},{64,0},{1,65},{65,1},{2,66},{66,2},{3,67},{67,3},{4,68},{68... | collective-permute-start | bytes 3080 | tf_op jit(solution)/shard_map/ppermute | solution.py:362
  3.0 40.7 %copy-start.2 = (bf16[1,1,768,2048]{3,2,1,0:T(8,128)(2,1)S(1)}, bf16[1,1,768,2048]{3,2,1,0:T(8,128)(2,1)}, u32[]{:S(2)}) copy-start(bf16[1,1,768,2048]{3,2,1,0:T(8,128)(2,1)} %up.3) | copy-start | bytes 9437188
  3.0 40.7 %copy-start.3 = (bf16[1,1,768,2048]{3,2,1,0:T(8,128)(2,1)S(1)}, bf16[1,1,768,2048]{3,2,1,0:T(8,128)(2,1)}, u32[]{:S(2)}) copy-start(bf16[1,1,768,2048]{3,2,1,0:T(8,128)(2,1)} %down.3) | copy-start | bytes 9437188
  7.5 1.4 %collective-permute-start.3 = (bf16[32,2176]{1,0:T(8,128)(2,1)S(1)}, bf16[32,2176]{1,0:T(8,128)(2,1)S(1)}, u32[]{:S(2)}, u32[]{:S(2)}) collective-permute-start(bf16[32,2176]{1,0:T(8,128)(2,1)S(1)} %get-tuple-element.18), channel_id=1, source_target_pairs={{0,64},{64,0},{1,65},{65,1},{2,66},{66,2},{3,67},{67,3},{4,68},{68... | collective-permute-start | bytes 417800 | tf_op jit(solution)/shard_map/ppermute | solution.py:362
  9.5 34.2 %copy-start.1 = (bf16[1,1,768,2048]{3,2,1,0:T(8,128)(2,1)S(1)}, bf16[1,1,768,2048]{3,2,1,0:T(8,128)(2,1)}, u32[]{:S(2)}) copy-start(bf16[1,1,768,2048]{3,2,1,0:T(8,128)(2,1)} %gate.3) | copy-start | bytes 9437188
  38.9 4.8 %copy-start.5 = (f32[1,2,2048]{2,1,0:T(2,128)S(1)}, f32[1,2,2048]{2,1,0:T(2,128)}, u32[]{:S(2)}) copy-start(f32[1,2,2048]{2,1,0:T(2,128)} %gains.5) | copy-start | bytes 49156
  39.8 3.9 %collective-permute-start.4 = (f32[32,1024]{1,0:T(8,128)S(1)}, f32[32,1024]{1,0:T(8,128)S(1)}, u32[]{:S(2)}, u32[]{:S(2)}) collective-permute-start(f32[32,1024]{1,0:T(8,128)S(1)} %get-tuple-element.20.mid_mine), channel_id=1, source_target_pairs={{0,64},{64,0},{1,65},{65,1},{2,66},{66,2},{3,67},{67,3},{4,68},{68... | collective-permute-start | bytes 393224 | tf_op jit(solution)/shard_map/ppermute | solution.py:362
  46.4 1.4 collective-permute-start.5
  47.8 26.9 %copy-start = (bf16[1,8,2,256,512]{4,3,2,1,0:T(8,128)(2,1)S(1)}, bf16[1,8,2,256,512]{4,3,2,1,0:T(8,128)(2,1)}, u32[]{:S(2)}) copy-start(bf16[1,8,2,256,512]{4,3,2,1,0:T(8,128)(2,1)} %cache.3) | copy-start | bytes 12582916
  70.5 4.2 %copy-start.6 = (s32[4,8]{1,0:T(4,128)S(1)}, s32[4,8]{1,0:T(4,128)}, u32[]{:S(2)}) copy-start(s32[4,8]{1,0:T(4,128)} %lengths.1) | copy-start | bytes 388
  70.8 3.9 %collective-permute-start.6 = (f32[32,1024]{1,0:T(8,128)S(1)}, f32[32,1024]{1,0:T(8,128)S(1)}, u32[]{:S(2)}, u32[]{:S(2)}) collective-permute-start(f32[32,1024]{1,0:T(8,128)S(1)} %mix.2.part_a), channel_id=1, source_target_pairs={{0,64},{64,0},{1,65},{65,1},{2,66},{66,2},{3,67},{67,3},{4,68},{68... | collective-permute-start | bytes 393224 | tf_op jit(solution)/shard_map/ppermute | solution.py:362
  76.6 1.4 collective-permute-start.7
  101.6 4.1 %collective-permute-start.8 = (f32[32,1024]{1,0:T(8,128)S(1)}, f32[32,1024]{1,0:T(8,128)S(1)}, u32[]{:S(2)}, u32[]{:S(2)}) collective-permute-start(f32[32,1024]{1,0:T(8,128)S(1)} %combine.3.mid_mine), channel_id=1, source_target_pairs={{0,64},{64,0},{1,65},{65,1},{2,66},{66,2},{3,67},{67,3},{4,68},{68... | collective-permute-start | bytes 393224 | tf_op jit(solution)/shard_map/ppermute | solution.py:362
  108.5 1.3 collective-permute-start.9
  131.2 3.8 %copy-start.4 = (bf16[32,2048]{1,0:T(8,128)(2,1)S(1)}, bf16[32,2048]{1,0:T(8,128)(2,1)}, u32[]{:S(2)}) copy-start(bf16[32,2048]{1,0:T(8,128)(2,1)} %table.1) | copy-start | bytes 393220
  131.2 3.9 %copy-start.7 = (f32[2048]{0:T(1024)S(1)}, f32[2048]{0:T(1024)}, u32[]{:S(2)}) copy-start(f32[2048]{0:T(1024)} %param.23) | copy-start | bytes 24580
  131.5 3.5 %collective-permute-start.10 = (f32[32,1024]{1,0:T(8,128)S(1)}, f32[32,1024]{1,0:T(8,128)S(1)}, u32[]{:S(2)}, u32[]{:S(2)}) collective-permute-start(f32[32,1024]{1,0:T(8,128)S(1)} %mix.3.mine), channel_id=1, source_target_pairs={{0,64},{64,0},{1,65},{65,1},{2,66},{66,2},{3,67},{67,3},{4,68},{68... | collective-permute-start | bytes 393224 | tf_op jit(solution)/shard_map/ppermute | solution.py:362

commit v3 on v2

v3 whole, which is shorter than its diff:
```python
import functools

import jax
import jax.numpy as jnp
from jax import lax
from jax.experimental import pallas as pl
from jax.experimental.pallas import tpu as pltpu
from jax.sharding import PartitionSpec as P

F32 = jnp.float32
BF16 = jnp.bfloat16
STEPS = 4
ROWS = 8
D = 2048
HEAD_DIM = 128
HEADS = D // HEAD_DIM
KV_HEADS = 4
GROUPS = HEADS // KV_HEADS
TOP = 8
CAP = 2
N_EXPERT = 4
N_SEQ = 16
DESTS = N_EXPERT * N_SEQ
SLOTS = STEPS * CAP
T = STEPS * ROWS
STAT = 128
PAY = D + STAT
PIECE = D // 4
CHUNKS = 3
EPS = 1e-6
LOWEST = -1e30


def vmem():
    return pl.BlockSpec(memory_space=pltpu.VMEM)


def hbm():
    return pl.BlockSpec(memory_space=pltpu.HBM)


def smem():
    return pl.BlockSpec(memory_space=pltpu.SMEM)


def call(body, name, ins, outs, scratch=(), limit=24):
    return pl.pallas_call(
        body,
        name=name,
        in_specs=ins,
        out_shape=outs,
        out_specs=jax.tree.map(lambda _: vmem(), outs),
        scratch_shapes=scratch,
        compiler_params=pltpu.CompilerParams(vmem_limit_bytes=limit << 20),
    )


def shape(*dims, dtype=BF16):
    return jax.ShapeDtypeStruct(dims, dtype)


def iota(dims, axis):
    return lax.broadcasted_iota(jnp.int32, dims, axis)


def dot(a, b, dims=((1,), (0,))):
    return lax.dot_general(a, b, (dims, ((), ())), preferred_element_type=F32)


def row_order():
    to, source = iota((T, T), 0), iota((T, T), 1)
    return (source == (to % STEPS) * ROWS + to // STEPS).astype(F32).astype(BF16)


def rms(value, gain):
    return value * lax.rsqrt(jnp.mean(value * value, axis=1, keepdims=True) + EPS) * gain


def placed_rows(ids, gates, mixing):
    width = DESTS * SLOTS
    column = iota((T, width), 1)
    row = iota((T, width), 0)
    same_step = (row // ROWS) == (column // CAP) % STEPS
    below, above = iota((T, T), 0), iota((T, T), 1)
    earlier = ((below // ROWS == above // ROWS) & (above < below)).astype(F32).astype(BF16)
    order = row_order()
    ids = ids[0].reshape(T, TOP)
    gates = gates[0].reshape(T, TOP)
    shares = gates / jnp.sum(gates, axis=1, keepdims=True)
    named = jnp.zeros((T, width), F32)
    weight = jnp.zeros((T, width), F32)
    for k in range(TOP):
        match = (ids[:, k : k + 1] == column // SLOTS) & same_step
        named = jnp.where(match, 1.0, named)
        weight = jnp.where(match, shares[:, k : k + 1], weight)
    rank = dot(earlier, named.astype(BF16))
    keep = rank == (column % CAP).astype(F32)
    hit = jnp.where(keep, named, 0.0)
    share = jnp.where(keep, weight, 0.0)
    high = share.astype(BF16)
    low = (share - high.astype(F32)).astype(BF16)
    mixing[:T] = dot(order, high).astype(BF16)
    mixing[T:] = dot(order, low).astype(BF16)
    return dot(order, hit.astype(BF16)).astype(BF16)


def codec_body(books, table_mine, table_other, pieces):
    section = lax.axis_index("section")
    seq = lax.axis_index("seq")
    codes = table_mine.shape[0]
    line = iota((T, codes), 0)
    wanted = jnp.zeros((T, codes), jnp.int32)
    for row_at in range(ROWS):
        for step in range(STEPS):
            wanted = jnp.where(line == row_at * STEPS + step, books[step, row_at], wanted)
    found = jnp.zeros((T, D), F32)
    for owner, table in ((section, table_mine), (1 - section, table_other)):
        start = (owner * N_SEQ + seq) * codes
        picked = (wanted - start == iota((T, codes), 1)).astype(F32).astype(BF16)
        found = found + dot(picked, table[...])
    for s in range(0, N_SEQ, 2):
        rows_at = slice((s // 4) * ROWS, (s // 4 + 1) * ROWS)
        pair = [found[rows_at, (q % 4) * PIECE : (q % 4 + 1) * PIECE] for q in (s, s + 1)]
        pieces[s * ROWS : (s + 2) * ROWS] = jnp.concatenate(pair, axis=0).astype(BF16)


def lay_queries(hidden, gain, queries, values):
    normed = rms(hidden, gain)
    values[...] = hidden
    queries[...] = jnp.zeros_like(queries)
    for r in range(ROWS):
        for h in range(HEADS):
            k = h // GROUPS
            at = h * STEPS
            queries[r, at : at + STEPS, k * HEAD_DIM : (k + 1) * HEAD_DIM] = normed[
                r * STEPS : (r + 1) * STEPS, h * HEAD_DIM : (h + 1) * HEAD_DIM
            ]


def cache_copies(cache, kv, sems):
    half = ROWS // 2
    return [
        pltpu.make_async_copy(cache.at[0, r : r + half, i], kv.at[r : r + half, i], sems.at[r // half, i])
        for i in range(2)
        for r in range(0, ROWS, half)
    ]


def attend_rows(seq, lengths, kv, copies, queries, values, stats, scores, weights):
    lines = GROUPS * STEPS
    size = HEADS * STEPS
    ctx = scores.shape[1]
    lane = iota((STEPS, STAT), 1)
    step_of = iota((size, ctx), 0) % STEPS
    position = seq * ctx + iota((size, ctx), 1)
    for copy in copies[:2]:
        copy.wait()
    for r in range(ROWS):
        scores[r * size : (r + 1) * size] = dot(queries[r].astype(BF16), kv[r, 0], ((1,), (1,)))
    scales = []
    for r in range(ROWS):
        limit = jnp.where(step_of == 0, lengths[0, r], 0)
        for step in range(1, STEPS):
            limit = jnp.where(step_of == step, lengths[step, r], limit)
        live = position < limit
        score = jnp.where(live, scores[r * size : (r + 1) * size] * HEAD_DIM ** (-0.5), LOWEST)
        highest = jnp.max(score, axis=1, keepdims=True)
        weight = jnp.where(live, jnp.exp(score - highest), 0.0)
        total = jnp.sum(weight, axis=1, keepdims=True)
        some = total > 0.0
        safe = jnp.where(some, total, 1.0)
        log_sum = jnp.where(some, highest + jnp.log(safe), LOWEST)
        scales.append(1.0 / safe)
        weights[r * size : (r + 1) * size] = weight.astype(BF16)
        logs = jnp.broadcast_to(log_sum, (size, STAT))
        line_stats = jnp.zeros((STEPS, STAT), F32)
        for h in range(HEADS):
            line_stats = jnp.where(lane == h, logs[h * STEPS : (h + 1) * STEPS], line_stats)
        stats[r * STEPS : (r + 1) * STEPS, :] = line_stats
    for copy in copies[2:]:
        copy.wait()
    for r in range(ROWS):
        outs = dot(weights[r * size : (r + 1) * size], kv[r, 1])
        rows_at = slice(r * STEPS, (r + 1) * STEPS)
        for k in range(KV_HEADS):
            span = slice(k * lines, (k + 1) * lines)
            out = outs[span, k * HEAD_DIM : (k + 1) * HEAD_DIM] * scales[r][span]
            for g in range(GROUPS):
                h = k * GROUPS + g
                lanes_at = slice(h * HEAD_DIM, (h + 1) * HEAD_DIM)
                values[rows_at, lanes_at] = values[rows_at, lanes_at] + out[g * STEPS : (g + 1) * STEPS]


def spread_rows(values, stats, pick, sent):
    logs = stats[...]
    high = logs.astype(BF16).astype(F32)
    mid = (logs - high).astype(BF16).astype(F32)
    low = (logs - high - mid).astype(BF16).astype(F32)
    lane = iota((T, STAT), 1)
    packed = jnp.where(lane < 2 * HEADS, pltpu.roll(mid, HEADS, 1), pltpu.roll(low, 2 * HEADS, 1))
    packed = jnp.where(lane < HEADS, high, jnp.where(lane < 3 * HEADS, packed, 0.0))
    for at in range(0, D, 512):
        sent[:, at : at + 512] = dot(pick, values[:, at : at + 512].astype(BF16), ((0,), (0,))).astype(BF16)
    sent[:, D:] = dot(pick, packed.astype(BF16), ((0,), (0,))).astype(BF16)


def attend_body(
    layer, ids_in, gates_in, lengths_in, gains_in, cache, part_a, part_b,
    sent, mixing,
    ids, gates, lengths, gains, entry, kv, queries, values, stats, scores, weights, small_sems, sems,
):
    section = lax.axis_index("section")
    seq = lax.axis_index("seq")
    pairs = [(gains_in, gains), (ids_in, ids), (gates_in, gates), (lengths_in, lengths)]
    if layer == 0:
        pairs = [(part_a, entry)] + pairs
    small = [pltpu.make_async_copy(source, target, small_sems.at[i]) for i, (source, target) in enumerate(pairs)]
    copies = cache_copies(cache, kv, sems)
    for copy in small + copies:
        copy.start()
    for copy in small:
        copy.wait()
    if layer == 0:
        a = entry[...].astype(F32).reshape(T // 2, D)
        b = part_b[...].astype(F32).reshape(T // 2, D)
        rows = jnp.where(section == 0, jnp.concatenate([a, b], axis=0), jnp.concatenate([b, a], axis=0))
        hidden = dot(row_order(), rows.astype(BF16))
    else:
        codes = part_b[...].astype(F32)
        codes = jnp.concatenate(
            [
                jnp.concatenate([codes[s * ROWS : (s + 1) * ROWS] for s in range(b, b + 4)], axis=1)
                for b in range(0, N_SEQ, 4)
            ],
            axis=0,
        )
        hidden = part_a[...].astype(F32) + codes
    lay_queries(hidden, gains[0, 0:1, :], queries, values)
    pick = placed_rows(ids, gates, mixing)
    attend_rows(seq, lengths, kv, copies, queries, values, stats, scores, weights)
    spread_rows(values, stats, pick, sent)


def expert_body(got, gains_in, gate_in, up_in, down_in, sent, middle, gains, gate, up, down, sems):
    block = N_SEQ * SLOTS
    size = gate.shape[0] // CHUNKS
    pairs = [(gains_in, gains)]
    for j in range(CHUNKS):
        at = slice(j * size, (j + 1) * size)
        pairs += [(gate_in.at[0, 0, at], gate.at[at]), (up_in.at[0, 0, at], up.at[at])]
    for j in range(CHUNKS):
        at = slice(j * size, (j + 1) * size)
        pairs.append((down_in.at[0, 0, at], down.at[at]))
    copies = [pltpu.make_async_copy(source, target, sems.at[i]) for i, (source, target) in enumerate(pairs)]
    for copy in copies:
        copy.start()
    widen = (iota((STAT, D), 0) == iota((STAT, D), 1) // HEAD_DIM).astype(F32).astype(BF16)
    for x in range(N_EXPERT):
        rows_at = slice(x * block, (x + 1) * block)
        packed = got[rows_at, D:PAY].astype(F32)
        logs = packed + pltpu.roll(packed, STAT - HEADS, 1) + pltpu.roll(packed, STAT - 2 * HEADS, 1)
        logs = logs.reshape(N_SEQ, SLOTS, STAT)
        weights = jnp.exp(logs - jnp.max(logs, axis=0, keepdims=True))
        weights = weights / jnp.sum(weights, axis=0, keepdims=True)
        weights = weights.reshape(block, STAT)
        high = weights.astype(BF16)
        low = (weights - high.astype(F32)).astype(BF16)
        for at in range(0, D, 256):
            lanes_at = slice(at, at + 256)
            wide = dot(high, widen[:, lanes_at]) + dot(low, widen[:, lanes_at])
            part = (got[rows_at, lanes_at].astype(F32) * wide).reshape(N_SEQ, SLOTS, 256)
            middle[x * SLOTS : (x + 1) * SLOTS, lanes_at] = jnp.sum(part, axis=0)
    rows = middle[...]
    copies[0].wait()
    moe_in = rms(rows, gains[0, 1:2, :]).astype(BF16)
    activ = []
    for j in range(CHUNKS):
        at = slice(j * size, (j + 1) * size)
        copies[1 + 2 * j].wait()
        copies[2 + 2 * j].wait()
        gate_out = dot(moe_in, gate[at], ((1,), (1,)))
        up_out = dot(moe_in, up[at], ((1,), (1,)))
        activ.append((gate_out / (1.0 + jnp.exp(-gate_out)) * up_out).astype(BF16))
    total = jnp.zeros((T, D), F32)
    for j in range(CHUNKS):
        copies[1 + 2 * CHUNKS + j].wait()
        total = total + dot(activ[j], down[j * size : (j + 1) * size])
    result = total.astype(BF16).astype(F32) + rows
    for x in range(N_EXPERT):
        part = result[x * SLOTS : (x + 1) * SLOTS]
        pair = jnp.concatenate([part, part], axis=0).astype(BF16)
        for s in range(0, N_SEQ, 2):
            at = (x * N_SEQ + s) * SLOTS
            sent[at : at + 2 * SLOTS, :] = pair


def mix_body(got, mixing, out):
    both = dot(mixing[...], got[...])
    out[...] = (both[:T] + both[T:]).astype(BF16)


def head_body(mine, got, gain, table, out):
    last = lax.axis_index("section") == 1
    hidden = jnp.where(last, mine[...].astype(F32), got[...].astype(F32))
    final = rms(hidden, gain[...]).astype(BF16)
    final = dot(row_order(), final, ((0,), (0,))).astype(BF16)
    logits = dot(final, table[...], ((1,), (1,))) * D ** (-0.5)
    out[...] = logits.reshape(out.shape)


def in_hbm(value):
    return pltpu.with_memory_space_constraint(value, pltpu.HBM)


def swapped(value):
    return lax.ppermute(value, "section", [(0, 1), (1, 0)])


def exchanged(value):
    return lax.all_to_all(value, ("expert", "seq"), 0, 0, tiled=True)


def gathered(parts):
    held = lax.all_to_all(parts, "seq", 0, 0, tiled=True)
    held = jnp.sum(held.astype(F32).reshape(N_SEQ, ROWS, PIECE), axis=0).astype(BF16)
    return lax.all_to_all(jnp.tile(held, (N_SEQ, 1)), "seq", 0, 0, tiled=True)


def one_layer(layer, part_a, part_b, ids, gates, lengths, gains, cache, gate, up, down):
    _, _, _, ctx, kv_width = cache.shape
    lines = ROWS * HEADS * STEPS
    sent, mixing = call(
        functools.partial(attend_body, layer),
        "attend",
        [hbm()] * 5 + [vmem() if layer else hbm(), vmem()],
        (shape(DESTS * SLOTS, PAY), shape(2 * T, DESTS * SLOTS)),
        [
            pltpu.VMEM(ids.shape, jnp.int32),
            pltpu.VMEM(gates.shape, F32),
            pltpu.SMEM(lengths.shape, jnp.int32),
            pltpu.VMEM(gains.shape, F32),
            pltpu.VMEM((STEPS // 2, ROWS, D), BF16),
            pltpu.VMEM((ROWS, 2, ctx, kv_width), BF16),
            pltpu.VMEM((ROWS, HEADS * STEPS, kv_width), F32),
            pltpu.VMEM((T, D), F32),
            pltpu.VMEM((T, STAT), F32),
            pltpu.VMEM((lines, ctx), F32),
            pltpu.VMEM((lines, ctx), BF16),
            pltpu.SemaphoreType.DMA((5,)),
            pltpu.SemaphoreType.DMA((2, 2)),
        ],
    )(*(in_hbm(v) for v in (ids, gates, lengths, gains, cache)), part_a if layer else in_hbm(part_a), part_b)
    sent = call(
        expert_body,
        "experts",
        [vmem()] + [hbm()] * 4,
        shape(DESTS * SLOTS, D),
        [
            pltpu.VMEM((T, D), F32),
            pltpu.VMEM(gains.shape, F32),
            *(pltpu.VMEM(weight.shape[2:], BF16) for weight in (gate, up, down)),
            pltpu.SemaphoreType.DMA((1 + 3 * CHUNKS,)),
        ],
    )(exchanged(sent), *(in_hbm(v) for v in (gains, gate, up, down)))
    return call(mix_body, "mix", [vmem()] * 2, shape(T, D))(exchanged(sent), mixing)


def per_device(
    entry_rows,
    cache_entries,
    cache_lengths,
    norm_gains,
    expert_ids,
    gate_weights,
    gate_weight,
    up_weight,
    down_weight,
    codebook_ids,
    codec_table,
    final_gain,
):
    codes = codec_table.shape[0]
    section = lax.axis_index("section")
    held = (
        expert_ids,
        gate_weights,
        cache_lengths,
        norm_gains,
        cache_entries,
        gate_weight,
        up_weight,
        down_weight,
    )

    def first(entry, entry_got, books, table, table_got, *held):
        return one_layer(0, entry, entry_got, *held), jnp.zeros((N_SEQ * ROWS, PIECE), BF16)

    def codec(entry, entry_got, books, table, table_got, *held):
        pieces = call(codec_body, "codec", [smem()] + [vmem()] * 2, shape(N_SEQ * ROWS, PIECE))(
            books, table, table_got
        )
        return jnp.zeros((T, D), BF16), gathered(pieces)

    rows, pieces = lax.cond(
        section == 0,
        first,
        codec,
        entry_rows,
        swapped(entry_rows),
        codebook_ids,
        codec_table,
        swapped(codec_table),
        *held,
    )
    rows = lax.cond(
        section == 1,
        lambda *values: one_layer(1, *values),
        lambda *values: jnp.zeros((T, D), BF16),
        swapped(rows),
        pieces,
        *held,
    )
    rows_got = swapped(rows)
    return call(
        head_body,
        "head",
        [vmem()] * 4,
        shape(STEPS, ROWS, codes, dtype=F32),
    )(rows, rows_got, final_gain.reshape(1, D), codec_table)


def solution(mesh):
    placed = (
        P("section", "expert", None),
        P("section", "expert", None, "seq", None),
        P(None, "expert"),
        P("section", None, None),
        P("section", None, "expert", None),
        P("section", None, "expert", None),
        P("section", ("expert", "seq"), None, None),
        P("section", ("expert", "seq"), None, None),
        P("section", ("expert", "seq"), None, None),
        P(None, "expert"),
        P(("section", "seq"), None),
        P(),
    )
    return jax.shard_map(
        per_device,
        mesh=mesh,
        in_specs=placed,
        out_specs=P(None, "expert", ("section", "seq")),
        check_vma=False,
    )
```

time: 136 us -> 131 us (0.963)
  starting transfers between devices: 15.2 us -> 36.6 us
  blocking collectives: 95.6 us -> 78.6 us
  waiting for transfers between devices: 8.73 us -> 3.79 us
  Pallas kernels: 16.3 us -> 11.7 us
    all_to_all x4 -> x2, blocking collectives: 95.6 us -> 47.7 us  [exchanged(): return lax.all_to_all(value, ('expert', 'seq'), 0, 0, tiled=True)]
    all_to_all x0 -> x2, blocking collectives: none -> 30.9 us  [the longest x1 16.4 us: gathered(): return lax.all_to_all(jnp.tile(held, (N_SEQ, 1)), 'seq', 0, 0, tiled=True)]
    ppermute x11 -> x4, starting transfers between devices: 15.2 us -> 36.6 us  [swapped(): return lax.ppermute(value, 'section', [(0, 1), (1, 0)])]
    ppermute x11 -> x4, waiting for transfers between devices: 8.73 us -> 3.79 us  [swapped(): return lax.ppermute(value, 'section', [(0, 1), (1, 0)])]
    pallas_call x12 -> x4, Pallas kernels: 15.3 us -> 10.6 us  [the longest x1 4.88 us: one_layer(): call(expert_body, 'experts', [vmem()] + [hbm()] * 4, shape(DESTS * SLOTS,...]
  transfers between devices with their start and end apart: 11 -> 4, of which waited for: 10 -> 3; matrix products, arithmetic and copies ran while one was open for 0% -> 0% of each run, Pallas kernels for 0% -> 0%
where the time goes in v3:
time: 131 us
  blocking collectives  78.6 us (60%)
  starting transfers between devices  36.6 us (28%)
  Pallas kernels  11.7 us (9%)
  waiting for transfers between devices  3.79 us (3%)
    all_to_all x2, blocking collectives, exchanged(): return lax.all_to_all(value, ('expert', 'seq'), 0, 0, tiled=True)  47.7 us
    ppermute x4, starting transfers between devices, swapped(): return lax.ppermute(value, 'section', [(0, 1), (1, 0)])  36.6 us
    all_to_all x1, blocking collectives, gathered(): return lax.all_to_all(jnp.tile(held, (N_SEQ, 1)), 'seq', 0, 0, tiled=True)  16.4 us
    all_to_all x1, blocking collectives, gathered(): held = lax.all_to_all(parts, 'seq', 0, 0, tiled=True)  14.5 us
    pallas_call x1, Pallas kernels, one_layer(): call(expert_body, 'experts', [vmem()] + [hbm()] * 4, shape(DESTS * SLOTS,...  4.88 us
    pallas_call x1, Pallas kernels, one_layer(): call(functools.partial(attend_body, layer), 'attend', [hbm()] * 5 + [vmem...  4.14 us
    ppermute x4, waiting for transfers between devices, swapped(): return lax.ppermute(value, 'section', [(0, 1), (1, 0)])  3.79 us
  transfers between devices with their start and end apart: 4, of which 3 were waited for; matrix products, arithmetic and copies ran while one was open for 0% of the time, Pallas kernels for 0%

profile of v3, /device:TPU:1, one launch (start us, length us, event | category | flops | bytes accessed | tf_op | source)
XLA Modules:
  0.0 130.9 jit_solution(12479866269375854560)
XLA Ops:
  0.0 1.4 %collective-permute-start = (bf16[32,2048]{1,0:T(8,128)(2,1)}, bf16[32,2048]{1,0:T(8,128)(2,1)S(1)}, u32[]{:S(2)}, u32[]{:S(2)}) collective-permute-start(bf16[32,2048]{1,0:T(8,128)(2,1)} %table.1), channel_id=1, source_target_pairs={{0,64},{64,0},{1,65},{65,1},{2,66},{66,2},{3,67},{67,3},{4,68},{68... | collective-permute-start | bytes 393224 | tf_op jit(solution)/shard_map/ppermute | solution.py:316
  1.4 0.0 collective-permute-start.1
  1.4 1.5 %collective-permute-done.1 = bf16[2,8,2048]{2,1,0:T(8,128)(2,1)S(1)} collective-permute-done((bf16[2,8,2048]{2,1,0:T(8,128)(2,1)}, bf16[2,8,2048]{2,1,0:T(8,128)(2,1)S(1)}, u32[]{:S(2)}, u32[]{:S(2)}) %collective-permute-start.1) | collective-permute-done | bytes 65568 | tf_op jit(solution)/shard_map/ppermute | solution.py:316
  2.9 0.0 collective-permute-done
  2.9 32.1 %conditional.2 = (bf16[32,2048]{1,0:T(8,128)(2,1)S(1)}, bf16[128,512]{1,0:T(8,128)(2,1)S(1)}) conditional(s32[]{:T(128)} %convert_element_type.14, (s32[4,8]{1,0:T(4,128)}, bf16[32,2048]{1,0:T(8,128)(2,1)}, bf16[32,2048]{1,0:T(8,128)(2,1)S(1)}) %tuple.20, (s32[1,4,8,8]{3,2,1,0:T(8,128)}, f32[1,4,8,8]{3,2,1,0:T(8,128)}, s32[4,8]{1,0:T(4,128)}, ...), branch_computations={%region_0.0_spmd, %region_2.0_spmd} | conditional | flops 61440 | bytes 8781842 | solution.py:404
  2.9 1.1 codec.1
  4.0 14.5 %all_to_all.46 = bf16[16,8,512]{2,1,0:T(8,128)(2,1)S(1)} all-to-all(bf16[16,8,512]{2,1,0:T(8,128)(2,1)S(1)} %bitcast.19), channel_id=1, replica_groups=mesh['section'=2,'expert'=4,'seq'=16] {'seq'}, dimensions={0} | all-to-all | bytes 262144 | tf_op jit(solution)/shard_map/cond/branch_0_fun/all_to_all | solution.py:324
  18.6 16.4 %all_to_all.47 = bf16[16,8,512]{2,1,0:T(8,128)(2,1)S(1)} all-to-all(bf16[16,8,512]{2,1,0:T(8,128)(2,1)S(1)} %tile.0), channel_id=1, replica_groups=mesh['section'=2,'expert'=4,'seq'=16] {'seq'}, dimensions={0} | all-to-all | bytes 262144 | tf_op jit(solution)/shard_map/cond/branch_0_fun/all_to_all | solution.py:326
  35.0 35.0 %collective-permute-start.2 = (bf16[32,2048]{1,0:T(8,128)(2,1)S(1)}, bf16[32,2048]{1,0:T(8,128)(2,1)S(1)}, u32[]{:S(2)}, u32[]{:S(2)}) collective-permute-start(bf16[32,2048]{1,0:T(8,128)(2,1)S(1)} %get-tuple-element.83), channel_id=1, source_target_pairs={{0,64},{64,0},{1,65},{65,1},{2,66},{66,2},{3,67},{67,3},{4,68},{68... | collective-permute-start | bytes 393224 | tf_op jit(solution)/shard_map/ppermute | solution.py:316
  70.0 1.0 collective-permute-done.2
  71.0 0.0 copy-start
  71.0 0.0 copy-start.1
  71.0 57.4 %conditional.3 = (bf16[32,2048]{1,0:T(8,128)(2,1)S(1)}) conditional(s32[]{:T(128)} %convert_element_type.13, () %tuple.19, (s32[1,4,8,8]{3,2,1,0:T(8,128)}, f32[1,4,8,8]{3,2,1,0:T(8,128)}, s32[4,8]{1,0:T(4,128)}, f32[1,2,2048]{2,1,0:T(2,128)}, bf16[1,8,2,256,512]{4,3,2,1,0:T(8,128)(2,1)}, /*index=5*/bf16[32,2048]{1,0:T(8,128)(2,1)S(1)}, ...), branch_computations={%region_3.0_spmd, %region_4.0_spmd} | conditional | bytes 8650760 | solution.py:415
  71.0 4.1 %attend.3 = (bf16[512,2176]{1,0:T(8,128)(2,1)S(1)}, bf16[64,512]{1,0:T(8,128)(2,1)S(1)}) custom-call(s32[1,4,8,8]{3,2,1,0:T(8,128)} %get-tuple-element.69.ids_in, f32[1,4,8,8]{3,2,1,0:T(8,128)} %get-tuple-element.70.gates_in, s32[4,8]{1,0:T(4,128)} %get-tuple-element.71.lengths_in, f32[1,2,2048]{2,1,0:T(2,128)} %get-tuple-element.72.gains_in, ...), custom_call_target="tpu_custom_call" | custom-call | tf_op jit(solution)/shard_map/cond/branch_1_fun/attend/pallas_call | solution.py:332
  75.2 24.5 %all_to_all.50 = bf16[64,8,2176]{2,1,0:T(8,128)(2,1)S(1)} all-to-all(bf16[64,8,2176]{2,1,0:T(8,128)(2,1)S(1)} %bitcast.18), channel_id=1, replica_groups=mesh['section'=2,'expert'=4,'seq'=16] {'expert','seq'}, dimensions={0} | all-to-all | bytes 4456448 | tf_op jit(solution)/shard_map/cond/branch_1_fun/all_to_all | solution.py:320
  99.7 4.9 %experts.3 = bf16[512,2048]{1,0:T(8,128)(2,1)S(1)} custom-call(bf16[512,2176]{1,0:T(8,128)(2,1)S(1)} %bitcast.12, f32[1,2,2048]{2,1,0:T(2,128)} %get-tuple-element.72.gains_in, bf16[1,1,768,2048]{3,2,1,0:T(8,128)(2,1)} %get-tuple-element.77.gate_in, bf16[1,1,768,2048]{3,2,1,0:T(8,128)(2,1)} %get-tuple-element.78.up_in, ...), custom_call_target="tpu_custom_call" | custom-call | tf_op jit(solution)/shard_map/cond/branch_1_fun/experts/pallas_call | solution.py:353
  104.5 23.3 %all_to_all.51 = bf16[64,8,2048]{2,1,0:T(8,128)(2,1)S(1)} all-to-all(bf16[64,8,2048]{2,1,0:T(8,128)(2,1)S(1)} %bitcast.16), channel_id=1, replica_groups=mesh['section'=2,'expert'=4,'seq'=16] {'expert','seq'}, dimensions={0} | all-to-all | bytes 4194304 | tf_op jit(solution)/shard_map/cond/branch_1_fun/all_to_all | solution.py:320
  127.8 0.5 mix.3
  128.4 0.1 collective-permute-start.3
  128.5 1.3 %collective-permute-done.3.got = bf16[32,2048]{1,0:T(8,128)(2,1)S(1)} collective-permute-done((bf16[32,2048]{1,0:T(8,128)(2,1)S(1)}, bf16[32,2048]{1,0:T(8,128)(2,1)S(1)}, u32[]{:S(2)}, u32[]{:S(2)}) %collective-permute-start.3) | collective-permute-done | bytes 131104 | tf_op jit(solution)/shard_map/ppermute | solution.py:316
  129.9 0.0 copy-done
  129.9 0.0 copy-done.1
  129.9 1.1 head.1
  (3 shorter events, 0.0 us)
Async XLA Ops:
  0.0 2.9 %collective-permute-start = (bf16[32,2048]{1,0:T(8,128)(2,1)}, bf16[32,2048]{1,0:T(8,128)(2,1)S(1)}, u32[]{:S(2)}, u32[]{:S(2)}) collective-permute-start(bf16[32,2048]{1,0:T(8,128)(2,1)} %table.1), channel_id=1, source_target_pairs={{0,64},{64,0},{1,65},{65,1},{2,66},{66,2},{3,67},{67,3},{4,68},{68... | collective-permute-start | bytes 393224 | tf_op jit(solution)/shard_map/ppermute | solution.py:316
  1.4 1.5 %collective-permute-start.1 = (bf16[2,8,2048]{2,1,0:T(8,128)(2,1)}, bf16[2,8,2048]{2,1,0:T(8,128)(2,1)S(1)}, u32[]{:S(2)}, u32[]{:S(2)}) collective-permute-start(bf16[2,8,2048]{2,1,0:T(8,128)(2,1)} %param.16), channel_id=1, source_target_pairs={{0,64},{64,0},{1,65},{65,1},{2,66},{66,2},{3,67},{67,3},{4,68},{68... | collective-permute-start | bytes 196616 | tf_op jit(solution)/shard_map/ppermute | solution.py:316
  35.0 36.0 %collective-permute-start.2 = (bf16[32,2048]{1,0:T(8,128)(2,1)S(1)}, bf16[32,2048]{1,0:T(8,128)(2,1)S(1)}, u32[]{:S(2)}, u32[]{:S(2)}) collective-permute-start(bf16[32,2048]{1,0:T(8,128)(2,1)S(1)} %get-tuple-element.83), channel_id=1, source_target_pairs={{0,64},{64,0},{1,65},{65,1},{2,66},{66,2},{3,67},{67,3},{4,68},{68... | collective-permute-start | bytes 393224 | tf_op jit(solution)/shard_map/ppermute | solution.py:316
  71.0 58.8 %copy-start = (f32[2048]{0:T(1024)S(1)}, f32[2048]{0:T(1024)}, u32[]{:S(2)}) copy-start(f32[2048]{0:T(1024)} %param.27) | copy-start | bytes 24580
  71.0 58.8 %copy-start.1 = (bf16[32,2048]{1,0:T(8,128)(2,1)S(1)}, bf16[32,2048]{1,0:T(8,128)(2,1)}, u32[]{:S(2)}) copy-start(bf16[32,2048]{1,0:T(8,128)(2,1)} %table.1) | copy-start | bytes 393220
  128.4 1.4 %collective-permute-start.3 = (bf16[32,2048]{1,0:T(8,128)(2,1)S(1)}, bf16[32,2048]{1,0:T(8,128)(2,1)S(1)}, u32[]{:S(2)}, u32[]{:S(2)}) collective-permute-start(bf16[32,2048]{1,0:T(8,128)(2,1)S(1)} %get-tuple-element.91.mine), channel_id=1, source_target_pairs={{0,64},{64,0},{1,65},{65,1},{2,66},{66,2},{3,67},{67,3},{4,68},{68... | collective-permute-start | bytes 393224 | tf_op jit(solution)/shard_map/ppermute | solution.py:316

commit v4 on v3

--- a/solution.py
+++ b/solution.py
@@ -25,7 +25,6 @@
 T = STEPS * ROWS
 STAT = 128
 PAY = D + STAT
-PIECE = D // 4
 CHUNKS = 3
 EPS = 1e-6
 LOWEST = -1e30
@@ -43,13 +42,13 @@
     return pl.BlockSpec(memory_space=pltpu.SMEM)
 
 
-def call(body, name, ins, outs, scratch=(), limit=24):
+def call(body, name, ins, outs, scratch=(), limit=24, places=None):
     return pl.pallas_call(
         body,
         name=name,
         in_specs=ins,
         out_shape=outs,
-        out_specs=jax.tree.map(lambda _: vmem(), outs),
+        out_specs=places or jax.tree.map(lambda _: vmem(), outs),
         scratch_shapes=scratch,
         compiler_params=pltpu.CompilerParams(vmem_limit_bytes=limit << 20),
     )
@@ -101,27 +100,22 @@
     low = (share - high.astype(F32)).astype(BF16)
     mixing[:T] = dot(order, high).astype(BF16)
     mixing[T:] = dot(order, low).astype(BF16)
-    return dot(order, hit.astype(BF16)).astype(BF16)
-
-
-def codec_body(books, table_mine, table_other, pieces):
-    section = lax.axis_index("section")
-    seq = lax.axis_index("seq")
-    codes = table_mine.shape[0]
+    return dot(hit.astype(BF16), order, ((0,), (1,))).astype(BF16)
+
+
+def codec_part(section, seq, books, tables):
+    codes = tables[0].shape[0]
     line = iota((T, codes), 0)
     wanted = jnp.zeros((T, codes), jnp.int32)
     for row_at in range(ROWS):
         for step in range(STEPS):
             wanted = jnp.where(line == row_at * STEPS + step, books[step, row_at], wanted)
     found = jnp.zeros((T, D), F32)
-    for owner, table in ((section, table_mine), (1 - section, table_other)):
+    for owner, table in zip((section, 1 - section), tables):
         start = (owner * N_SEQ + seq) * codes
         picked = (wanted - start == iota((T, codes), 1)).astype(F32).astype(BF16)
         found = found + dot(picked, table[...])
-    for s in range(0, N_SEQ, 2):
-        rows_at = slice((s // 4) * ROWS, (s // 4 + 1) * ROWS)
-        pair = [found[rows_at, (q % 4) * PIECE : (q % 4 + 1) * PIECE] for q in (s, s + 1)]
-        pieces[s * ROWS : (s + 2) * ROWS] = jnp.concatenate(pair, axis=0).astype(BF16)
+    return found
 
 
 def lay_queries(hidden, gain, queries, values):
@@ -144,6 +138,16 @@
         for i in range(2)
         for r in range(0, ROWS, half)
     ]
+
+
+def softened(scores, live):
+    score = jnp.where(live, scores * HEAD_DIM ** (-0.5), LOWEST)
+    highest = jnp.max(score, axis=1, keepdims=True)
+    weight = jnp.where(live, jnp.exp(score - highest), 0.0)
+    total = jnp.sum(weight, axis=1, keepdims=True)
+    some = total > 0.0
+    safe = jnp.where(some, total, 1.0)
+    return weight.astype(BF16), jnp.where(some, highest + jnp.log(safe), LOWEST), 1.0 / safe
 
 
 def attend_rows(seq, lengths, kv, copies, queries, values, stats, scores, weights):
@@ -162,16 +166,9 @@
         limit = jnp.where(step_of == 0, lengths[0, r], 0)
         for step in range(1, STEPS):
             limit = jnp.where(step_of == step, lengths[step, r], limit)
-        live = position < limit
-        score = jnp.where(live, scores[r * size : (r + 1) * size] * HEAD_DIM ** (-0.5), LOWEST)
-        highest = jnp.max(score, axis=1, keepdims=True)
-        weight = jnp.where(live, jnp.exp(score - highest), 0.0)
-        total = jnp.sum(weight, axis=1, keepdims=True)
-        some = total > 0.0
-        safe = jnp.where(some, total, 1.0)
-        log_sum = jnp.where(some, highest + jnp.log(safe), LOWEST)
-        scales.append(1.0 / safe)
-        weights[r * size : (r + 1) * size] = weight.astype(BF16)
+        weight, log_sum, scale = softened(scores[r * size : (r + 1) * size], position < limit)
+        weights[r * size : (r + 1) * size] = weight
+        scales.append(scale)
         logs = jnp.broadcast_to(log_sum, (size, STAT))
         line_stats = jnp.zeros((STEPS, STAT), F32)
         for h in range(HEADS):
@@ -192,56 +189,137 @@
 
 
 def spread_rows(values, stats, pick, sent):
+    width = values.shape[1]
+    heads = width // HEAD_DIM
     logs = stats[...]
     high = logs.astype(BF16).astype(F32)
     mid = (logs - high).astype(BF16).astype(F32)
     low = (logs - high - mid).astype(BF16).astype(F32)
     lane = iota((T, STAT), 1)
-    packed = jnp.where(lane < 2 * HEADS, pltpu.roll(mid, HEADS, 1), pltpu.roll(low, 2 * HEADS, 1))
-    packed = jnp.where(lane < HEADS, high, jnp.where(lane < 3 * HEADS, packed, 0.0))
-    for at in range(0, D, 512):
-        sent[:, at : at + 512] = dot(pick, values[:, at : at + 512].astype(BF16), ((0,), (0,))).astype(BF16)
-    sent[:, D:] = dot(pick, packed.astype(BF16), ((0,), (0,))).astype(BF16)
-
-
-def attend_body(
-    layer, ids_in, gates_in, lengths_in, gains_in, cache, part_a, part_b,
-    sent, mixing,
-    ids, gates, lengths, gains, entry, kv, queries, values, stats, scores, weights, small_sems, sems,
+    packed = jnp.where(lane < 2 * heads, pltpu.roll(mid, heads, 1), pltpu.roll(low, 2 * heads, 1))
+    packed = jnp.where(lane < heads, high, jnp.where(lane < 3 * heads, packed, 0.0))
+    for at in range(0, width, 512):
+        sent[:, at : at + 512] = dot(pick, values[:, at : at + 512].astype(BF16)).astype(BF16)
+    sent[:, width : width + STAT] = dot(pick, packed.astype(BF16)).astype(BF16)
+
+
+def enter_body(
+    ids_in, gates_in, lengths_in, gains_in, cache, entry_in, books_in, table_in, entry_got, table_got,
+    sent, mixing, unused,
+    ids, gates, lengths, gains, entry, books, table, kv, queries, values, stats, scores, weights, small_sems, sems,
 ):
     section = lax.axis_index("section")
     seq = lax.axis_index("seq")
-    pairs = [(gains_in, gains), (ids_in, ids), (gates_in, gates), (lengths_in, lengths)]
-    if layer == 0:
-        pairs = [(part_a, entry)] + pairs
+    pairs = (
+        (entry_in, entry),
+        (gains_in, gains),
+        (ids_in, ids),
+        (gates_in, gates),
+        (lengths_in, lengths),
+        (books_in, books),
+        (table_in, table),
+    )
     small = [pltpu.make_async_copy(source, target, small_sems.at[i]) for i, (source, target) in enumerate(pairs)]
     copies = cache_copies(cache, kv, sems)
     for copy in small + copies:
         copy.start()
     for copy in small:
         copy.wait()
-    if layer == 0:
-        a = entry[...].astype(F32).reshape(T // 2, D)
-        b = part_b[...].astype(F32).reshape(T // 2, D)
-        rows = jnp.where(section == 0, jnp.concatenate([a, b], axis=0), jnp.concatenate([b, a], axis=0))
-        hidden = dot(row_order(), rows.astype(BF16))
-    else:
-        codes = part_b[...].astype(F32)
-        codes = jnp.concatenate(
-            [
-                jnp.concatenate([codes[s * ROWS : (s + 1) * ROWS] for s in range(b, b + 4)], axis=1)
-                for b in range(0, N_SEQ, 4)
-            ],
-            axis=0,
-        )
-        hidden = part_a[...].astype(F32) + codes
-    lay_queries(hidden, gains[0, 0:1, :], queries, values)
+    a = entry[...].astype(F32).reshape(T // 2, D)
+    b = entry_got[...].astype(F32).reshape(T // 2, D)
+    rows = jnp.where(section == 0, jnp.concatenate([a, b], axis=0), jnp.concatenate([b, a], axis=0))
+    lay_queries(dot(row_order(), rows.astype(BF16)), gains[0, 0:1, :], queries, values)
     pick = placed_rows(ids, gates, mixing)
+    codes = codec_part(section, seq, books, (table, table_got))
+    tiles = [
+        codes[x * SLOTS : (x + 1) * SLOTS, s * STAT : (s + 1) * STAT] for x in range(N_EXPERT) for s in range(N_SEQ)
+    ]
+    sent[:, PAY:] = jnp.concatenate(tiles, axis=0).astype(BF16)
     attend_rows(seq, lengths, kv, copies, queries, values, stats, scores, weights)
     spread_rows(values, stats, pick, sent)
 
 
-def expert_body(got, gains_in, gate_in, up_in, down_in, sent, middle, gains, gate, up, down, sems):
+def trade_body(cache, out, held, parts, in_sems, out_sems):
+    copies = [pltpu.make_async_copy(cache.at[0, r], held.at[r], in_sems.at[r]) for r in range(ROWS)]
+    for copy in copies:
+        copy.start()
+    sends = []
+    for r in range(ROWS):
+        copies[r].wait()
+        for k in range(KV_HEADS):
+            parts[k, r] = held[r, :, :, k * HEAD_DIM : (k + 1) * HEAD_DIM]
+    for k in range(KV_HEADS):
+        sends.append(pltpu.make_async_copy(parts.at[k], out.at[k], out_sems.at[k]))
+        sends[-1].start()
+    for send in sends:
+        send.wait()
+
+
+def attend_body(
+    ids_in, gates_in, lengths_in, gains_in, cache, rows,
+    sent, mixing,
+    ids, gates, lengths, gains, kv, normed, hidden, queries, values, stats, scores, weights, small_sems, sems,
+):
+    seq = lax.axis_index("seq")
+    pairs = ((gains_in, gains), (ids_in, ids), (gates_in, gates), (lengths_in, lengths))
+    small = [pltpu.make_async_copy(source, target, small_sems.at[i]) for i, (source, target) in enumerate(pairs)]
+    local = cache.shape[3]
+    copies = [
+        pltpu.make_async_copy(cache.at[y, :, i], kv.at[:, i, y * local : (y + 1) * local], sems.at[i, y])
+        for i in range(2)
+        for y in range(KV_HEADS)
+    ]
+    for copy in small + copies:
+        copy.start()
+    whole = rows[...].astype(F32)
+    hidden[...] = whole
+    for copy in small:
+        copy.wait()
+    normed[...] = rms(whole, gains[0, 0:1, :])
+    width = values.shape[1]
+    own = pl.ds(pl.multiple_of((seq % KV_HEADS) * width, width), width)
+    asked = normed[:, own]
+    values[...] = hidden[:, own]
+    size = GROUPS * STEPS
+    for r in range(ROWS):
+        for g in range(GROUPS):
+            queries[r, g * STEPS : (g + 1) * STEPS, :] = asked[
+                r * STEPS : (r + 1) * STEPS, g * HEAD_DIM : (g + 1) * HEAD_DIM
+            ]
+    pick = placed_rows(ids, gates, mixing)
+    for copy in copies[:KV_HEADS]:
+        copy.wait()
+    for r in range(ROWS):
+        scores[r * size : (r + 1) * size] = dot(queries[r].astype(BF16), kv[r, 0], ((1,), (1,)))
+    ctx = scores.shape[1]
+    step_of = iota((size, ctx), 0) % STEPS
+    position = (seq // KV_HEADS) * ctx + iota((size, ctx), 1)
+    lane = iota((STEPS, STAT), 1)
+    scales = []
+    for r in range(ROWS):
+        limit = jnp.where(step_of == 0, lengths[0, r], 0)
+        for step in range(1, STEPS):
+            limit = jnp.where(step_of == step, lengths[step, r], limit)
+        weight, log_sum, scale = softened(scores[r * size : (r + 1) * size], position < limit)
+        weights[r * size : (r + 1) * size] = weight
+        scales.append(scale)
+        logs = jnp.broadcast_to(log_sum, (size, STAT))
+        line_stats = jnp.zeros((STEPS, STAT), F32)
+        for g in range(GROUPS):
+            line_stats = jnp.where(lane == g, logs[g * STEPS : (g + 1) * STEPS], line_stats)
+        stats[r * STEPS : (r + 1) * STEPS, :] = line_stats
+    for copy in copies[KV_HEADS:]:
+        copy.wait()
+    for r in range(ROWS):
+        out = dot(weights[r * size : (r + 1) * size], kv[r, 1]) * scales[r]
+        rows_at = slice(r * STEPS, (r + 1) * STEPS)
+        for g in range(GROUPS):
+            lanes_at = slice(g * HEAD_DIM, (g + 1) * HEAD_DIM)
+            values[rows_at, lanes_at] = values[rows_at, lanes_at] + out[g * STEPS : (g + 1) * STEPS]
+    spread_rows(values, stats, pick, sent)
+
+
+def expert_body(width, got, gains_in, gate_in, up_in, down_in, sent, middle, gains, gate, up, down, sems):
     block = N_SEQ * SLOTS
     size = gate.shape[0] // CHUNKS
     pairs = [(gains_in, gains)]
@@ -254,22 +332,30 @@
     copies = [pltpu.make_async_copy(source, target, sems.at[i]) for i, (source, target) in enumerate(pairs)]
     for copy in copies:
         copy.start()
-    widen = (iota((STAT, D), 0) == iota((STAT, D), 1) // HEAD_DIM).astype(F32).astype(BF16)
+    heads = width // HEAD_DIM
+    widen = (iota((2 * STAT, width), 0) % STAT == iota((2 * STAT, width), 1) // HEAD_DIM).astype(F32).astype(BF16)
+    parts = D // width
+    lines = parts * SLOTS
     for x in range(N_EXPERT):
         rows_at = slice(x * block, (x + 1) * block)
-        packed = got[rows_at, D:PAY].astype(F32)
-        logs = packed + pltpu.roll(packed, STAT - HEADS, 1) + pltpu.roll(packed, STAT - 2 * HEADS, 1)
-        logs = logs.reshape(N_SEQ, SLOTS, STAT)
+        packed = got[rows_at, width : width + STAT].astype(F32)
+        logs = packed + pltpu.roll(packed, STAT - heads, 1) + pltpu.roll(packed, STAT - 2 * heads, 1)
+        logs = logs.reshape(block // lines, lines, STAT)
         weights = jnp.exp(logs - jnp.max(logs, axis=0, keepdims=True))
         weights = weights / jnp.sum(weights, axis=0, keepdims=True)
         weights = weights.reshape(block, STAT)
         high = weights.astype(BF16)
         low = (weights - high.astype(F32)).astype(BF16)
-        for at in range(0, D, 256):
+        weights = jnp.concatenate([high, low], axis=1)
+        for at in range(0, width, 256):
             lanes_at = slice(at, at + 256)
-            wide = dot(high, widen[:, lanes_at]) + dot(low, widen[:, lanes_at])
-            part = (got[rows_at, lanes_at].astype(F32) * wide).reshape(N_SEQ, SLOTS, 256)
-            middle[x * SLOTS : (x + 1) * SLOTS, lanes_at] = jnp.sum(part, axis=0)
+            wide = dot(weights, widen[:, lanes_at])
+            part = (got[rows_at, lanes_at].astype(F32) * wide).reshape(block // lines, lines, 256)
+            part = jnp.sum(part, axis=0)
+            for y in range(parts):
+                middle[x * SLOTS : (x + 1) * SLOTS, y * width + at : y * width + at + 256] = part[
+                    y * SLOTS : (y + 1) * SLOTS
+                ]
     rows = middle[...]
     copies[0].wait()
     moe_in = rms(rows, gains[0, 1:2, :]).astype(BF16)
@@ -286,8 +372,13 @@
         copies[1 + 2 * CHUNKS + j].wait()
         total = total + dot(activ[j], down[j * size : (j + 1) * size])
     result = total.astype(BF16).astype(F32) + rows
+    coded = got.shape[1] > width + STAT
+    if coded:
+        codes = jnp.sum(got[:, width + STAT :].astype(F32).reshape(N_EXPERT, N_SEQ, SLOTS, STAT), axis=1)
     for x in range(N_EXPERT):
         part = result[x * SLOTS : (x + 1) * SLOTS]
+        if coded:
+            part = jnp.concatenate([part, codes[x]], axis=1)
         pair = jnp.concatenate([part, part], axis=0).astype(BF16)
         for s in range(0, N_SEQ, 2):
             at = (x * N_SEQ + s) * SLOTS
@@ -295,8 +386,18 @@
 
 
 def mix_body(got, mixing, out):
-    both = dot(mixing[...], got[...])
-    out[...] = (both[:T] + both[T:]).astype(BF16)
+    both = dot(mixing[...], got[:, :D])
+    hidden = (both[:T] + both[T:]).astype(BF16)
+    if got.shape[1] > D:
+        codes = got[:, D:].astype(F32)
+        lines = [
+            jnp.concatenate(
+                [codes[(x * N_SEQ + s) * SLOTS : (x * N_SEQ + s + 1) * SLOTS] for s in range(N_SEQ)], axis=1
+            )
+            for x in range(N_EXPERT)
+        ]
+        hidden = hidden.astype(F32) + jnp.concatenate(lines, axis=0)
+    out[...] = hidden.astype(out.dtype)
 
 
 def head_body(mine, got, gain, table, out):
@@ -320,41 +421,33 @@
     return lax.all_to_all(value, ("expert", "seq"), 0, 0, tiled=True)
 
 
-def gathered(parts):
-    held = lax.all_to_all(parts, "seq", 0, 0, tiled=True)
-    held = jnp.sum(held.astype(F32).reshape(N_SEQ, ROWS, PIECE), axis=0).astype(BF16)
-    return lax.all_to_all(jnp.tile(held, (N_SEQ, 1)), "seq", 0, 0, tiled=True)
-
-
-def one_layer(layer, part_a, part_b, ids, gates, lengths, gains, cache, gate, up, down):
-    _, _, _, ctx, kv_width = cache.shape
-    lines = ROWS * HEADS * STEPS
-    sent, mixing = call(
-        functools.partial(attend_body, layer),
-        "attend",
-        [hbm()] * 5 + [vmem() if layer else hbm(), vmem()],
-        (shape(DESTS * SLOTS, PAY), shape(2 * T, DESTS * SLOTS)),
-        [
-            pltpu.VMEM(ids.shape, jnp.int32),
-            pltpu.VMEM(gates.shape, F32),
-            pltpu.SMEM(lengths.shape, jnp.int32),
-            pltpu.VMEM(gains.shape, F32),
-            pltpu.VMEM((STEPS // 2, ROWS, D), BF16),
-            pltpu.VMEM((ROWS, 2, ctx, kv_width), BF16),
-            pltpu.VMEM((ROWS, HEADS * STEPS, kv_width), F32),
-            pltpu.VMEM((T, D), F32),
-            pltpu.VMEM((T, STAT), F32),
-            pltpu.VMEM((lines, ctx), F32),
-            pltpu.VMEM((lines, ctx), BF16),
-            pltpu.SemaphoreType.DMA((5,)),
-            pltpu.SemaphoreType.DMA((2, 2)),
+def traded(cache):
+    _, rows, kinds, ctx, _ = cache.shape
+    parts = pl.pallas_call(
+        trade_body,
+        name="trade",
+        in_specs=[hbm()],
+        out_specs=hbm(),
+        out_shape=shape(KV_HEADS, rows, kinds, ctx, HEAD_DIM),
+        scratch_shapes=[
+            pltpu.VMEM(cache.shape[1:], BF16),
+            pltpu.VMEM((KV_HEADS, rows, kinds, ctx, HEAD_DIM), BF16),
+            pltpu.SemaphoreType.DMA((rows,)),
+            pltpu.SemaphoreType.DMA((KV_HEADS,)),
         ],
-    )(*(in_hbm(v) for v in (ids, gates, lengths, gains, cache)), part_a if layer else in_hbm(part_a), part_b)
+        compiler_params=pltpu.CompilerParams(vmem_limit_bytes=56 << 20),
+    )(in_hbm(cache))
+    groups = [list(range(at, at + KV_HEADS)) for at in range(0, N_SEQ, KV_HEADS)]
+    return lax.all_to_all(parts, "seq", 0, 0, axis_index_groups=groups, tiled=True)
+
+
+def experts(width, sent, mixing, gains, gate, up, down):
+    coded = STAT if sent.shape[1] > width + STAT else 0
     sent = call(
-        expert_body,
+        functools.partial(expert_body, width),
         "experts",
         [vmem()] + [hbm()] * 4,
-        shape(DESTS * SLOTS, D),
+        shape(DESTS * SLOTS, D + coded),
         [
             pltpu.VMEM((T, D), F32),
             pltpu.VMEM(gains.shape, F32),
@@ -381,43 +474,93 @@
 ):
     codes = codec_table.shape[0]
     section = lax.axis_index("section")
-    held = (
-        expert_ids,
-        gate_weights,
-        cache_lengths,
-        norm_gains,
-        cache_entries,
-        gate_weight,
-        up_weight,
-        down_weight,
-    )
-
-    def first(entry, entry_got, books, table, table_got, *held):
-        return one_layer(0, entry, entry_got, *held), jnp.zeros((N_SEQ * ROWS, PIECE), BF16)
-
-    def codec(entry, entry_got, books, table, table_got, *held):
-        pieces = call(codec_body, "codec", [smem()] + [vmem()] * 2, shape(N_SEQ * ROWS, PIECE))(
-            books, table, table_got
-        )
-        return jnp.zeros((T, D), BF16), gathered(pieces)
-
-    rows, pieces = lax.cond(
+    ctx = cache_entries.shape[3]
+    kv_width = cache_entries.shape[4]
+    width = DESTS * SLOTS
+
+    def small(ids, gates, lengths, gains, *rest):
+        return [
+            pltpu.VMEM(ids.shape, jnp.int32),
+            pltpu.VMEM(gates.shape, F32),
+            pltpu.SMEM(lengths.shape, jnp.int32),
+            pltpu.VMEM(gains.shape, F32),
+        ]
+
+    def first(entry, entry_got, books, table, table_got, cache, weights, *held):
+        lines = ROWS * HEADS * STEPS
+        sent, mixing, unused = call(
+            enter_body,
+            "enter",
+            [hbm()] * 8 + [vmem()] * 2,
+            (shape(width, PAY + STAT), shape(2 * T, width), shape(KV_HEADS, ROWS, 2, ctx, HEAD_DIM)),
+            [
+                *small(*held),
+                pltpu.VMEM(entry.shape, BF16),
+                pltpu.SMEM(books.shape, jnp.int32),
+                pltpu.VMEM(table.shape, BF16),
+                pltpu.VMEM((ROWS, 2, ctx, kv_width), BF16),
+                pltpu.VMEM((ROWS, HEADS * STEPS, kv_width), F32),
+                pltpu.VMEM((T, D), F32),
+                pltpu.VMEM((T, STAT), F32),
+                pltpu.VMEM((lines, ctx), F32),
+                pltpu.VMEM((lines, ctx), BF16),
+                pltpu.SemaphoreType.DMA((7,)),
+                pltpu.SemaphoreType.DMA((2, 2)),
+            ],
+            places=(vmem(), vmem(), hbm()),
+        )(*(in_hbm(v) for v in (*held, cache, entry, books, table)), entry_got, table_got)
+        return experts(D, sent, mixing, held[3], *weights), unused
+
+    def waiting(entry, entry_got, books, table, table_got, cache, weights, *held):
+        return jnp.zeros((T, D), BF16), traded(cache)
+
+    def second(rows, cache, weights, *held):
+        lines = ROWS * GROUPS * STEPS
+        span = KV_HEADS * ctx
+        share = GROUPS * HEAD_DIM
+        sent, mixing = call(
+            attend_body,
+            "attend",
+            [hbm()] * 5 + [vmem()],
+            (shape(width, share + STAT), shape(2 * T, width)),
+            [
+                *small(*held),
+                pltpu.VMEM((ROWS, 2, span, HEAD_DIM), BF16),
+                pltpu.VMEM((T, D), F32),
+                pltpu.VMEM((T, D), F32),
+                pltpu.VMEM((ROWS, GROUPS * STEPS, HEAD_DIM), F32),
+                pltpu.VMEM((T, share), F32),
+                pltpu.VMEM((T, STAT), F32),
+                pltpu.VMEM((lines, span), F32),
+                pltpu.VMEM((lines, span), BF16),
+                pltpu.SemaphoreType.DMA((4,)),
+                pltpu.SemaphoreType.DMA((2, KV_HEADS)),
+            ],
+        )(*(in_hbm(v) for v in (*held, cache)), rows)
+        return experts(share, sent, mixing, held[3], *weights)
+
+    held = (expert_ids, gate_weights, cache_lengths, norm_gains)
+    weights = (gate_weight, up_weight, down_weight)
+    rows, cache = lax.cond(
         section == 0,
         first,
-        codec,
+        waiting,
         entry_rows,
         swapped(entry_rows),
         codebook_ids,
         codec_table,
         swapped(codec_table),
+        cache_entries,
+        weights,
         *held,
     )
     rows = lax.cond(
         section == 1,
-        lambda *values: one_layer(1, *values),
+        second,
         lambda *values: jnp.zeros((T, D), BF16),
         swapped(rows),
-        pieces,
+        cache,
+        weights,
         *held,
     )
     rows_got = swapped(rows)

time: 131 us -> 126 us (0.962)
  starting transfers between devices: 36.6 us -> 23.7 us
  blocking collectives: 78.6 us -> 83.8 us
  Pallas kernels: 11.7 us -> 14.6 us
    all_to_all x2 -> x1, blocking collectives: 30.9 us -> 45 us  [traded(): lax.all_to_all(parts, 'seq', 0, 0, axis_index_groups=groups, tiled=True)]
    ppermute x4, starting transfers between devices: 36.6 us -> 23.7 us  [swapped(): return lax.ppermute(value, 'section', [(0, 1), (1, 0)])]
    all_to_all x2, blocking collectives: 47.7 us -> 38.8 us  [exchanged(): return lax.all_to_all(value, ('expert', 'seq'), 0, 0, tiled=True)]
    pallas_call x4, Pallas kernels: 10.6 us -> 13.5 us  [the longest x1 4.74 us: experts(): call(functools.partial(expert_body, width), 'experts', [vmem()] + [hbm()]...]
where the time goes in v4:
time: 126 us
  blocking collectives  83.8 us (67%)
  starting transfers between devices  23.7 us (19%)
  Pallas kernels  14.6 us (12%)
  waiting for transfers between devices  3.79 us (3%)
    all_to_all x1, blocking collectives, traded(): lax.all_to_all(parts, 'seq', 0, 0, axis_index_groups=groups, tiled=True)  45 us
    all_to_all x2, blocking collectives, exchanged(): return lax.all_to_all(value, ('expert', 'seq'), 0, 0, tiled=True)  38.8 us
    ppermute x4, starting transfers between devices, swapped(): return lax.ppermute(value, 'section', [(0, 1), (1, 0)])  23.7 us
    pallas_call x1, Pallas kernels, experts(): call(functools.partial(expert_body, width), 'experts', [vmem()] + [hbm()]...  4.74 us
    pallas_call x1, Pallas kernels, traded(): pl.pallas_call(trade_body, name='trade', in_specs=[hbm()], out_specs=hbm(...  4.3 us
    pallas_call x1, Pallas kernels, second(): call(attend_body, 'attend', [hbm()] * 5 + [vmem()], (shape(width, share +...  4.04 us
    ppermute x4, waiting for transfers between devices, swapped(): return lax.ppermute(value, 'section', [(0, 1), (1, 0)])  3.79 us
  transfers between devices with their start and end apart: 4, of which 3 were waited for; matrix products, arithmetic and copies ran while one was open for 0% of the time, Pallas kernels for 0%

profile of v4, /device:TPU:1, one launch (start us, length us, event | category | flops | bytes accessed | tf_op | source)
XLA Modules:
  0.0 126.1 jit_solution(3595434695085964983)
XLA Ops:
  0.0 1.4 %collective-permute-start.1 = (bf16[32,2048]{1,0:T(8,128)(2,1)}, bf16[32,2048]{1,0:T(8,128)(2,1)S(1)}, u32[]{:S(2)}, u32[]{:S(2)}) collective-permute-start(bf16[32,2048]{1,0:T(8,128)(2,1)} %table.1), channel_id=1, source_target_pairs={{0,64},{64,0},{1,65},{65,1},{2,66},{66,2},{3,67},{67,3},{4,68},{68... | collective-permute-start | bytes 393224 | tf_op jit(solution)/shard_map/ppermute | solution.py:417
  1.4 0.0 collective-permute-start
  1.4 1.5 %collective-permute-done = bf16[2,8,2048]{2,1,0:T(8,128)(2,1)S(1)} collective-permute-done((bf16[2,8,2048]{2,1,0:T(8,128)(2,1)}, bf16[2,8,2048]{2,1,0:T(8,128)(2,1)S(1)}, u32[]{:S(2)}, u32[]{:S(2)}) %collective-permute-start) | collective-permute-done | bytes 65568 | tf_op jit(solution)/shard_map/ppermute | solution.py:417
  2.9 0.0 collective-permute-done.1
  2.9 49.3 %conditional.2 = (bf16[32,2048]{1,0:T(8,128)(2,1)S(1)}, bf16[4,8,2,256,128]{4,3,2,1,0:T(8,128)(2,1)}) conditional(s32[]{:T(128)} %convert_element_type.7, bf16[1,8,2,256,512]{4,3,2,1,0:T(8,128)(2,1)} %param.17, (s32[1,4,8,8]{3,2,1,0:T(8,128)}, f32[1,4,8,8]{3,2,1,0:T(8,128)}, s32[4,8]{1,0:T(4,128)}, f32[1,2,2048]{2,1,0:T(2,128)}, ...), branch_computations={%region_0.0_spmd, %region_1.0_spmd} | conditional | bytes 9175056 | solution.py:544
  2.9 4.3 %trade.1 = bf16[4,8,2,256,128]{4,3,2,1,0:T(8,128)(2,1)} custom-call(bf16[1,8,2,256,512]{4,3,2,1,0:T(8,128)(2,1)} %cache), custom_call_target="tpu_custom_call" | custom-call | tf_op jit(solution)/shard_map/cond/branch_0_fun/trade/pallas_call | solution.py:426
  7.2 45.0 %all_to_all.36 = bf16[4,8,2,256,128]{4,3,2,1,0:T(8,128)(2,1)} all-to-all(bf16[4,8,2,256,128]{4,3,2,1,0:T(8,128)(2,1)} %trade.1), channel_id=1, replica_groups={{0,1,2,3},{4,5,6,7},{8,9,10,11},{12,13,14,15},{16,17,18,19},{20,21,22,2..., dimensions={0} | all-to-all | bytes 8388608 | tf_op jit(solution)/shard_map/cond/branch_0_fun/all_to_all | solution.py:441
  52.2 22.1 %collective-permute-start.2 = (bf16[32,2048]{1,0:T(8,128)(2,1)S(1)}, bf16[32,2048]{1,0:T(8,128)(2,1)S(1)}, u32[]{:S(2)}, u32[]{:S(2)}) collective-permute-start(bf16[32,2048]{1,0:T(8,128)(2,1)S(1)} %get-tuple-element.83), channel_id=1, source_target_pairs={{0,64},{64,0},{1,65},{65,1},{2,66},{66,2},{3,67},{67,3},{4,68},{68... | collective-permute-start | bytes 393224 | tf_op jit(solution)/shard_map/ppermute | solution.py:417
  74.3 1.0 collective-permute-done.2
  75.3 0.0 copy-start
  75.3 0.0 copy-start.1
  75.3 48.2 %conditional.3 = (bf16[32,2048]{1,0:T(8,128)(2,1)S(1)}) conditional(s32[]{:T(128)} %convert_element_type.6, () %tuple.19, (s32[1,4,8,8]{3,2,1,0:T(8,128)}, f32[1,4,8,8]{3,2,1,0:T(8,128)}, s32[4,8]{1,0:T(4,128)}, f32[1,2,2048]{2,1,0:T(2,128)}, bf16[4,8,2,256,128]{4,3,2,1,0:T(8,128)(2,1)}, /*index=5*/bf16[32,2048]{1,0:T(8,128)(2,1)S(1)}, ...), branch_computations={%region_2.0_spmd, %region_3.0_spmd} | conditional | bytes 5505032 | solution.py:557
  75.3 4.0 %attend.1 = (bf16[512,640]{1,0:T(8,128)(2,1)S(1)}, bf16[64,512]{1,0:T(8,128)(2,1)S(1)}) custom-call(s32[1,4,8,8]{3,2,1,0:T(8,128)} %get-tuple-element.69.ids_in, f32[1,4,8,8]{3,2,1,0:T(8,128)} %get-tuple-element.70.gates_in, s32[4,8]{1,0:T(4,128)} %get-tuple-element.71.lengths_in, f32[1,2,2048]{2,1,0:T(2,128)} %get-tuple-element.72.gains_in, ...), custom_call_target="tpu_custom_call" | custom-call | tf_op jit(solution)/shard_map/cond/branch_1_fun/attend/pallas_call | solution.py:521
  79.4 15.9 %all_to_all.39 = bf16[64,8,640]{2,1,0:T(8,128)(2,1)S(1)} all-to-all(bf16[64,8,640]{2,1,0:T(8,128)(2,1)S(1)} %bitcast.16), channel_id=1, replica_groups=mesh['section'=2,'expert'=4,'seq'=16] {'expert','seq'}, dimensions={0} | all-to-all | bytes 1310720 | tf_op jit(solution)/shard_map/cond/branch_1_fun/all_to_all | solution.py:421
  95.3 4.7 %experts.3 = bf16[512,2048]{1,0:T(8,128)(2,1)S(1)} custom-call(bf16[512,640]{1,0:T(8,128)(2,1)S(1)} %bitcast.14, f32[1,2,2048]{2,1,0:T(2,128)} %get-tuple-element.72.gains_in, bf16[1,1,768,2048]{3,2,1,0:T(8,128)(2,1)} %get-tuple-element.76.gate_in, bf16[1,1,768,2048]{3,2,1,0:T(8,128)(2,1)} %get-tuple-element.77.up_in, ...), custom_call_target="tpu_custom_call" | custom-call | tf_op jit(solution)/shard_map/cond/branch_1_fun/experts/pallas_call | solution.py:446
  100.0 22.9 %all_to_all.40 = bf16[64,8,2048]{2,1,0:T(8,128)(2,1)S(1)} all-to-all(bf16[64,8,2048]{2,1,0:T(8,128)(2,1)S(1)} %bitcast.13), channel_id=1, replica_groups=mesh['section'=2,'expert'=4,'seq'=16] {'expert','seq'}, dimensions={0} | all-to-all | bytes 4194304 | tf_op jit(solution)/shard_map/cond/branch_1_fun/all_to_all | solution.py:421
  122.9 0.5 mix.3
  123.6 0.1 collective-permute-start.3
  123.7 1.3 %collective-permute-done.3.got = bf16[32,2048]{1,0:T(8,128)(2,1)S(1)} collective-permute-done((bf16[32,2048]{1,0:T(8,128)(2,1)S(1)}, bf16[32,2048]{1,0:T(8,128)(2,1)S(1)}, u32[]{:S(2)}, u32[]{:S(2)}) %collective-permute-start.3) | collective-permute-done | bytes 131104 | tf_op jit(solution)/shard_map/ppermute | solution.py:417
  125.0 0.0 copy-done
  125.0 0.0 copy-done.1
  125.0 1.1 head.1
  (1 shorter events, 0.0 us)
Async XLA Ops:
  0.0 2.9 %collective-permute-start.1 = (bf16[32,2048]{1,0:T(8,128)(2,1)}, bf16[32,2048]{1,0:T(8,128)(2,1)S(1)}, u32[]{:S(2)}, u32[]{:S(2)}) collective-permute-start(bf16[32,2048]{1,0:T(8,128)(2,1)} %table.1), channel_id=1, source_target_pairs={{0,64},{64,0},{1,65},{65,1},{2,66},{66,2},{3,67},{67,3},{4,68},{68... | collective-permute-start | bytes 393224 | tf_op jit(solution)/shard_map/ppermute | solution.py:417
  1.4 1.5 %collective-permute-start = (bf16[2,8,2048]{2,1,0:T(8,128)(2,1)}, bf16[2,8,2048]{2,1,0:T(8,128)(2,1)S(1)}, u32[]{:S(2)}, u32[]{:S(2)}) collective-permute-start(bf16[2,8,2048]{2,1,0:T(8,128)(2,1)} %param.16), channel_id=1, source_target_pairs={{0,64},{64,0},{1,65},{65,1},{2,66},{66,2},{3,67},{67,3},{4,68},{68... | collective-permute-start | bytes 196616 | tf_op jit(solution)/shard_map/ppermute | solution.py:417
  52.2 23.1 %collective-permute-start.2 = (bf16[32,2048]{1,0:T(8,128)(2,1)S(1)}, bf16[32,2048]{1,0:T(8,128)(2,1)S(1)}, u32[]{:S(2)}, u32[]{:S(2)}) collective-permute-start(bf16[32,2048]{1,0:T(8,128)(2,1)S(1)} %get-tuple-element.83), channel_id=1, source_target_pairs={{0,64},{64,0},{1,65},{65,1},{2,66},{66,2},{3,67},{67,3},{4,68},{68... | collective-permute-start | bytes 393224 | tf_op jit(solution)/shard_map/ppermute | solution.py:417
  75.3 49.7 %copy-start = (f32[2048]{0:T(1024)S(1)}, f32[2048]{0:T(1024)}, u32[]{:S(2)}) copy-start(f32[2048]{0:T(1024)} %param.27) | copy-start | bytes 24580
  75.3 49.7 %copy-start.1 = (bf16[32,2048]{1,0:T(8,128)(2,1)S(1)}, bf16[32,2048]{1,0:T(8,128)(2,1)}, u32[]{:S(2)}) copy-start(bf16[32,2048]{1,0:T(8,128)(2,1)} %table.1) | copy-start | bytes 393220
  123.6 1.4 %collective-permute-start.3 = (bf16[32,2048]{1,0:T(8,128)(2,1)S(1)}, bf16[32,2048]{1,0:T(8,128)(2,1)S(1)}, u32[]{:S(2)}, u32[]{:S(2)}) collective-permute-start(bf16[32,2048]{1,0:T(8,128)(2,1)S(1)} %get-tuple-element.90.mine), channel_id=1, source_target_pairs={{0,64},{64,0},{1,65},{65,1},{2,66},{66,2},{3,67},{67,3},{4,68},{68... | collective-permute-start | bytes 393224 | tf_op jit(solution)/shard_map/ppermute | solution.py:417

commit v5 on v4

--- a/solution.py
+++ b/solution.py
@@ -75,32 +75,38 @@
     return value * lax.rsqrt(jnp.mean(value * value, axis=1, keepdims=True) + EPS) * gain
 
 
-def placed_rows(ids, gates, mixing):
+def named_slots(ids, gates=None):
     width = DESTS * SLOTS
     column = iota((T, width), 1)
     row = iota((T, width), 0)
     same_step = (row // ROWS) == (column // CAP) % STEPS
     below, above = iota((T, T), 0), iota((T, T), 1)
     earlier = ((below // ROWS == above // ROWS) & (above < below)).astype(F32).astype(BF16)
-    order = row_order()
     ids = ids[0].reshape(T, TOP)
-    gates = gates[0].reshape(T, TOP)
-    shares = gates / jnp.sum(gates, axis=1, keepdims=True)
     named = jnp.zeros((T, width), F32)
     weight = jnp.zeros((T, width), F32)
+    if gates is not None:
+        gates = gates[0].reshape(T, TOP)
+        shares = gates / jnp.sum(gates, axis=1, keepdims=True)
     for k in range(TOP):
         match = (ids[:, k : k + 1] == column // SLOTS) & same_step
         named = jnp.where(match, 1.0, named)
-        weight = jnp.where(match, shares[:, k : k + 1], weight)
-    rank = dot(earlier, named.astype(BF16))
-    keep = rank == (column % CAP).astype(F32)
-    hit = jnp.where(keep, named, 0.0)
-    share = jnp.where(keep, weight, 0.0)
+        if gates is not None:
+            weight = jnp.where(match, shares[:, k : k + 1], weight)
+    keep = dot(earlier, named.astype(BF16)) == (column % CAP).astype(F32)
+    return jnp.where(keep, named if gates is None else weight, 0.0)
+
+
+def slot_rows(ids):
+    return dot(named_slots(ids).astype(BF16), row_order(), ((0,), (1,))).astype(BF16)
+
+
+def mix_rows(ids, gates, mixing):
+    share = named_slots(ids, gates)
     high = share.astype(BF16)
     low = (share - high.astype(F32)).astype(BF16)
-    mixing[:T] = dot(order, high).astype(BF16)
-    mixing[T:] = dot(order, low).astype(BF16)
-    return dot(hit.astype(BF16), order, ((0,), (1,))).astype(BF16)
+    mixing[:T] = dot(row_order(), high).astype(BF16)
+    mixing[T:] = dot(row_order(), low).astype(BF16)
 
 
 def codec_part(section, seq, books, tables):
@@ -204,9 +210,9 @@
 
 
 def enter_body(
-    ids_in, gates_in, lengths_in, gains_in, cache, entry_in, books_in, table_in, entry_got, table_got,
-    sent, mixing, unused,
-    ids, gates, lengths, gains, entry, books, table, kv, queries, values, stats, scores, weights, small_sems, sems,
+    ids_in, lengths_in, gains_in, cache, entry_in, books_in, table_in, gate_in, entry_got, table_got,
+    sent, gate, unused,
+    ids, lengths, gains, entry, books, table, kv, queries, values, stats, scores, weights, small_sems, sems, ahead_sem,
 ):
     section = lax.axis_index("section")
     seq = lax.axis_index("seq")
@@ -214,14 +220,14 @@
         (entry_in, entry),
         (gains_in, gains),
         (ids_in, ids),
-        (gates_in, gates),
         (lengths_in, lengths),
         (books_in, books),
         (table_in, table),
     )
     small = [pltpu.make_async_copy(source, target, small_sems.at[i]) for i, (source, target) in enumerate(pairs)]
     copies = cache_copies(cache, kv, sems)
-    for copy in small + copies:
+    ahead = pltpu.make_async_copy(gate_in.at[0, 0], gate, ahead_sem.at[0])
+    for copy in [*small, *copies, ahead]:
         copy.start()
     for copy in small:
         copy.wait()
@@ -229,7 +235,7 @@
     b = entry_got[...].astype(F32).reshape(T // 2, D)
     rows = jnp.where(section == 0, jnp.concatenate([a, b], axis=0), jnp.concatenate([b, a], axis=0))
     lay_queries(dot(row_order(), rows.astype(BF16)), gains[0, 0:1, :], queries, values)
-    pick = placed_rows(ids, gates, mixing)
+    pick = slot_rows(ids)
     codes = codec_part(section, seq, books, (table, table_got))
     tiles = [
         codes[x * SLOTS : (x + 1) * SLOTS, s * STAT : (s + 1) * STAT] for x in range(N_EXPERT) for s in range(N_SEQ)
@@ -237,6 +243,7 @@
     sent[:, PAY:] = jnp.concatenate(tiles, axis=0).astype(BF16)
     attend_rows(seq, lengths, kv, copies, queries, values, stats, scores, weights)
     spread_rows(values, stats, pick, sent)
+    ahead.wait()
 
 
 def trade_body(cache, out, held, parts, in_sems, out_sems):
@@ -256,12 +263,12 @@
 
 
 def attend_body(
-    ids_in, gates_in, lengths_in, gains_in, cache, rows,
-    sent, mixing,
-    ids, gates, lengths, gains, kv, normed, hidden, queries, values, stats, scores, weights, small_sems, sems,
+    ids_in, lengths_in, gains_in, cache, gate_in, rows,
+    sent, gate,
+    ids, lengths, gains, kv, normed, hidden, queries, values, stats, scores, weights, small_sems, sems, ahead_sem,
 ):
     seq = lax.axis_index("seq")
-    pairs = ((gains_in, gains), (ids_in, ids), (gates_in, gates), (lengths_in, lengths))
+    pairs = ((gains_in, gains), (ids_in, ids), (lengths_in, lengths))
     small = [pltpu.make_async_copy(source, target, small_sems.at[i]) for i, (source, target) in enumerate(pairs)]
     local = cache.shape[3]
     copies = [
@@ -269,7 +276,8 @@
         for i in range(2)
         for y in range(KV_HEADS)
     ]
-    for copy in small + copies:
+    ahead = pltpu.make_async_copy(gate_in.at[0, 0], gate, ahead_sem.at[0])
+    for copy in [*small, *copies, ahead]:
         copy.start()
     whole = rows[...].astype(F32)
     hidden[...] = whole
@@ -286,7 +294,7 @@
             queries[r, g * STEPS : (g + 1) * STEPS, :] = asked[
                 r * STEPS : (r + 1) * STEPS, g * HEAD_DIM : (g + 1) * HEAD_DIM
             ]
-    pick = placed_rows(ids, gates, mixing)
+    pick = slot_rows(ids)
     for copy in copies[:KV_HEADS]:
         copy.wait()
     for r in range(ROWS):
@@ -317,18 +325,20 @@
             lanes_at = slice(g * HEAD_DIM, (g + 1) * HEAD_DIM)
             values[rows_at, lanes_at] = values[rows_at, lanes_at] + out[g * STEPS : (g + 1) * STEPS]
     spread_rows(values, stats, pick, sent)
-
-
-def expert_body(width, got, gains_in, gate_in, up_in, down_in, sent, middle, gains, gate, up, down, sems):
+    ahead.wait()
+
+
+def expert_body(
+    width, got, ids_in, gates_in, gains_in, gate, up_in, down_in,
+    sent, mixing,
+    middle, ids, gates, gains, up, down, sems,
+):
     block = N_SEQ * SLOTS
     size = gate.shape[0] // CHUNKS
-    pairs = [(gains_in, gains)]
-    for j in range(CHUNKS):
-        at = slice(j * size, (j + 1) * size)
-        pairs += [(gate_in.at[0, 0, at], gate.at[at]), (up_in.at[0, 0, at], up.at[at])]
-    for j in range(CHUNKS):
-        at = slice(j * size, (j + 1) * size)
-        pairs.append((down_in.at[0, 0, at], down.at[at]))
+    pairs = [(gains_in, gains), (ids_in, ids), (gates_in, gates)]
+    for source, target in ((up_in, up), (down_in, down)):
+        for j in range(0, CHUNKS * size, size):
+            pairs.append((source.at[0, 0, j : j + size], target.at[j : j + size]))
     copies = [pltpu.make_async_copy(source, target, sems.at[i]) for i, (source, target) in enumerate(pairs)]
     for copy in copies:
         copy.start()
@@ -357,19 +367,20 @@
                     y * SLOTS : (y + 1) * SLOTS
                 ]
     rows = middle[...]
-    copies[0].wait()
+    for copy in copies[:3]:
+        copy.wait()
+    mix_rows(ids, gates, mixing)
     moe_in = rms(rows, gains[0, 1:2, :]).astype(BF16)
     activ = []
     for j in range(CHUNKS):
         at = slice(j * size, (j + 1) * size)
-        copies[1 + 2 * j].wait()
-        copies[2 + 2 * j].wait()
+        copies[3 + j].wait()
         gate_out = dot(moe_in, gate[at], ((1,), (1,)))
         up_out = dot(moe_in, up[at], ((1,), (1,)))
         activ.append((gate_out / (1.0 + jnp.exp(-gate_out)) * up_out).astype(BF16))
     total = jnp.zeros((T, D), F32)
     for j in range(CHUNKS):
-        copies[1 + 2 * CHUNKS + j].wait()
+        copies[3 + CHUNKS + j].wait()
         total = total + dot(activ[j], down[j * size : (j + 1) * size])
     result = total.astype(BF16).astype(F32) + rows
     coded = got.shape[1] > width + STAT
@@ -441,20 +452,22 @@
     return lax.all_to_all(parts, "seq", 0, 0, axis_index_groups=groups, tiled=True)
 
 
-def experts(width, sent, mixing, gains, gate, up, down):
+def experts(width, sent, ids, gates, gains, gate, up, down):
     coded = STAT if sent.shape[1] > width + STAT else 0
-    sent = call(
+    sent, mixing = call(
         functools.partial(expert_body, width),
         "experts",
-        [vmem()] + [hbm()] * 4,
-        shape(DESTS * SLOTS, D + coded),
+        [vmem()] + [hbm()] * 3 + [vmem()] + [hbm()] * 2,
+        (shape(DESTS * SLOTS, D + coded), shape(2 * T, DESTS * SLOTS)),
         [
             pltpu.VMEM((T, D), F32),
+            pltpu.VMEM(ids.shape, jnp.int32),
+            pltpu.VMEM(gates.shape, F32),
             pltpu.VMEM(gains.shape, F32),
-            *(pltpu.VMEM(weight.shape[2:], BF16) for weight in (gate, up, down)),
-            pltpu.SemaphoreType.DMA((1 + 3 * CHUNKS,)),
+            *(pltpu.VMEM(weight.shape[2:], BF16) for weight in (up, down)),
+            pltpu.SemaphoreType.DMA((3 + 2 * CHUNKS,)),
         ],
-    )(exchanged(sent), *(in_hbm(v) for v in (gains, gate, up, down)))
+    )(exchanged(sent), in_hbm(ids), in_hbm(gates), in_hbm(gains), gate, in_hbm(up), in_hbm(down))
     return call(mix_body, "mix", [vmem()] * 2, shape(T, D))(exchanged(sent), mixing)
 
 
@@ -478,23 +491,22 @@
     kv_width = cache_entries.shape[4]
     width = DESTS * SLOTS
 
-    def small(ids, gates, lengths, gains, *rest):
+    def small(ids, lengths, gains):
         return [
             pltpu.VMEM(ids.shape, jnp.int32),
-            pltpu.VMEM(gates.shape, F32),
             pltpu.SMEM(lengths.shape, jnp.int32),
             pltpu.VMEM(gains.shape, F32),
         ]
 
     def first(entry, entry_got, books, table, table_got, cache, weights, *held):
         lines = ROWS * HEADS * STEPS
-        sent, mixing, unused = call(
+        sent, gate, unused = call(
             enter_body,
             "enter",
             [hbm()] * 8 + [vmem()] * 2,
-            (shape(width, PAY + STAT), shape(2 * T, width), shape(KV_HEADS, ROWS, 2, ctx, HEAD_DIM)),
+            (shape(width, PAY + STAT), shape(*gate_weight.shape[2:]), shape(KV_HEADS, ROWS, 2, ctx, HEAD_DIM)),
             [
-                *small(*held),
+                *small(held[0], *held[2:]),
                 pltpu.VMEM(entry.shape, BF16),
                 pltpu.SMEM(books.shape, jnp.int32),
                 pltpu.VMEM(table.shape, BF16),
@@ -504,12 +516,13 @@
                 pltpu.VMEM((T, STAT), F32),
                 pltpu.VMEM((lines, ctx), F32),
                 pltpu.VMEM((lines, ctx), BF16),
-                pltpu.SemaphoreType.DMA((7,)),
+                pltpu.SemaphoreType.DMA((6,)),
                 pltpu.SemaphoreType.DMA((2, 2)),
+                pltpu.SemaphoreType.DMA((1,)),
             ],
             places=(vmem(), vmem(), hbm()),
-        )(*(in_hbm(v) for v in (*held, cache, entry, books, table)), entry_got, table_got)
-        return experts(D, sent, mixing, held[3], *weights), unused
+        )(*(in_hbm(v) for v in (held[0], *held[2:], cache, entry, books, table, weights[0])), entry_got, table_got)
+        return experts(D, sent, *held[:2], held[3], gate, *weights[1:]), unused
 
     def waiting(entry, entry_got, books, table, table_got, cache, weights, *held):
         return jnp.zeros((T, D), BF16), traded(cache)
@@ -518,13 +531,13 @@
         lines = ROWS * GROUPS * STEPS
         span = KV_HEADS * ctx
         share = GROUPS * HEAD_DIM
-        sent, mixing = call(
+        sent, gate = call(
             attend_body,
             "attend",
             [hbm()] * 5 + [vmem()],
-            (shape(width, share + STAT), shape(2 * T, width)),
+            (shape(width, share + STAT), shape(*gate_weight.shape[2:])),
             [
-                *small(*held),
+                *small(held[0], *held[2:]),
                 pltpu.VMEM((ROWS, 2, span, HEAD_DIM), BF16),
                 pltpu.VMEM((T, D), F32),
                 pltpu.VMEM((T, D), F32),
@@ -533,11 +546,12 @@
                 pltpu.VMEM((T, STAT), F32),
                 pltpu.VMEM((lines, span), F32),
                 pltpu.VMEM((lines, span), BF16),
-                pltpu.SemaphoreType.DMA((4,)),
+                pltpu.SemaphoreType.DMA((3,)),
                 pltpu.SemaphoreType.DMA((2, KV_HEADS)),
+                pltpu.SemaphoreType.DMA((1,)),
             ],
-        )(*(in_hbm(v) for v in (*held, cache)), rows)
-        return experts(share, sent, mixing, held[3], *weights)
+        )(*(in_hbm(v) for v in (held[0], *held[2:], cache, weights[0])), rows)
+        return experts(share, sent, *held[:2], held[3], gate, *weights[1:])
 
     held = (expert_ids, gate_weights, cache_lengths, norm_gains)
     weights = (gate_weight, up_weight, down_weight)

time: 126 us -> 126 us (level)
  no operation moved by 1% of the time
where the time goes in v5:
time: 126 us; the launch traced here: 125 us
  blocking collectives  83.8 us (67%)
  starting transfers between devices  23.6 us (19%)
  Pallas kernels  13.8 us (11%)
  waiting for transfers between devices  3.79 us (3%)
    all_to_all x1, blocking collectives, traded(): lax.all_to_all(parts, 'seq', 0, 0, axis_index_groups=groups, tiled=True)  45 us
    all_to_all x2, blocking collectives, exchanged(): return lax.all_to_all(value, ('expert', 'seq'), 0, 0, tiled=True)  38.8 us
    ppermute x4, starting transfers between devices, swapped(): return lax.ppermute(value, 'section', [(0, 1), (1, 0)])  23.6 us
    pallas_call x1, Pallas kernels, experts(): call(functools.partial(expert_body, width), 'experts', [vmem()] + [hbm()]...  4.44 us
    pallas_call x1, Pallas kernels, traded(): pl.pallas_call(trade_body, name='trade', in_specs=[hbm()], out_specs=hbm(...  4.29 us
    ppermute x4, waiting for transfers between devices, swapped(): return lax.ppermute(value, 'section', [(0, 1), (1, 0)])  3.79 us
    pallas_call x1, Pallas kernels, second(): call(attend_body, 'attend', [hbm()] * 5 + [vmem()], (shape(width, share +...  3.54 us
  transfers between devices with their start and end apart: 4, of which 3 were waited for; matrix products, arithmetic and copies ran while one was open for 0% of the time, Pallas kernels for 0%

profile of v5, /device:TPU:1, one launch (start us, length us, event | category | flops | bytes accessed | tf_op | source)
XLA Modules:
  0.0 125.3 jit_solution(10540528489134847046)
XLA Ops:
  0.0 1.4 %collective-permute-start.1 = (bf16[32,2048]{1,0:T(8,128)(2,1)}, bf16[32,2048]{1,0:T(8,128)(2,1)S(1)}, u32[]{:S(2)}, u32[]{:S(2)}) collective-permute-start(bf16[32,2048]{1,0:T(8,128)(2,1)} %table.1), channel_id=1, source_target_pairs={{0,64},{64,0},{1,65},{65,1},{2,66},{66,2},{3,67},{67,3},{4,68},{68... | collective-permute-start | bytes 393224 | tf_op jit(solution)/shard_map/ppermute | solution.py:428
  1.4 0.0 collective-permute-start
  1.4 1.5 %collective-permute-done = bf16[2,8,2048]{2,1,0:T(8,128)(2,1)S(1)} collective-permute-done((bf16[2,8,2048]{2,1,0:T(8,128)(2,1)}, bf16[2,8,2048]{2,1,0:T(8,128)(2,1)S(1)}, u32[]{:S(2)}, u32[]{:S(2)}) %collective-permute-start) | collective-permute-done | bytes 65568 | tf_op jit(solution)/shard_map/ppermute | solution.py:428
  2.9 0.0 collective-permute-done.1
  2.9 49.3 %conditional.2 = (bf16[32,2048]{1,0:T(8,128)(2,1)S(1)}, bf16[4,8,2,256,128]{4,3,2,1,0:T(8,128)(2,1)}) conditional(s32[]{:T(128)} %convert_element_type.7, bf16[1,8,2,256,512]{4,3,2,1,0:T(8,128)(2,1)} %param.17, (s32[1,4,8,8]{3,2,1,0:T(8,128)}, s32[4,8]{1,0:T(4,128)}, f32[1,2,2048]{2,1,0:T(2,128)}, bf16[1,8,2,256,512]{4,3,2,1,0:T(8,128)(2,1)}, ...), branch_computations={%region_0.0_spmd, %region_1.0_spmd} | conditional | bytes 9175056 | solution.py:558
  2.9 4.3 %trade.1 = bf16[4,8,2,256,128]{4,3,2,1,0:T(8,128)(2,1)} custom-call(bf16[1,8,2,256,512]{4,3,2,1,0:T(8,128)(2,1)} %cache), custom_call_target="tpu_custom_call" | custom-call | tf_op jit(solution)/shard_map/cond/branch_0_fun/trade/pallas_call | solution.py:437
  7.2 45.0 %all_to_all.36 = bf16[4,8,2,256,128]{4,3,2,1,0:T(8,128)(2,1)} all-to-all(bf16[4,8,2,256,128]{4,3,2,1,0:T(8,128)(2,1)} %trade.1), channel_id=1, replica_groups={{0,1,2,3},{4,5,6,7},{8,9,10,11},{12,13,14,15},{16,17,18,19},{20,21,22,2..., dimensions={0} | all-to-all | bytes 8388608 | tf_op jit(solution)/shard_map/cond/branch_0_fun/all_to_all | solution.py:452
  52.2 22.1 %collective-permute-start.2 = (bf16[32,2048]{1,0:T(8,128)(2,1)S(1)}, bf16[32,2048]{1,0:T(8,128)(2,1)S(1)}, u32[]{:S(2)}, u32[]{:S(2)}) collective-permute-start(bf16[32,2048]{1,0:T(8,128)(2,1)S(1)} %get-tuple-element.87), channel_id=1, source_target_pairs={{0,64},{64,0},{1,65},{65,1},{2,66},{66,2},{3,67},{67,3},{4,68},{68... | collective-permute-start | bytes 393224 | tf_op jit(solution)/shard_map/ppermute | solution.py:428
  74.3 1.0 collective-permute-done.2
  75.3 0.0 copy-start
  75.3 0.0 copy-start.1
  75.3 47.5 %conditional.3 = (bf16[32,2048]{1,0:T(8,128)(2,1)S(1)}) conditional(s32[]{:T(128)} %convert_element_type.6, () %tuple.19, (s32[1,4,8,8]{3,2,1,0:T(8,128)}, s32[4,8]{1,0:T(4,128)}, f32[1,2,2048]{2,1,0:T(2,128)}, bf16[4,8,2,256,128]{4,3,2,1,0:T(8,128)(2,1)}, bf16[1,1,768,2048]{3,2,1,0:T(8,128)(2,1)}, /*index=5*/bf16[32,2048]{1,0:T(8,128)(2,1)S(1)}, ...), branch_computations={%region_2.0_spmd, %region_3.0_spmd} | conditional | bytes 5505032 | solution.py:571
  75.3 3.5 %attend.1 = (bf16[512,640]{1,0:T(8,128)(2,1)S(1)}, bf16[768,2048]{1,0:T(8,128)(2,1)S(1)}) custom-call(s32[1,4,8,8]{3,2,1,0:T(8,128)} %get-tuple-element.71.ids_in, s32[4,8]{1,0:T(4,128)} %get-tuple-element.72.lengths_in, f32[1,2,2048]{2,1,0:T(2,128)} %get-tuple-element.73.gains_in, bf16[4,8,2,256,128]{4,3,2,1,0:T(8,128)(2,1)} %get-tuple-element.74.cache, ...), custom_call_target="tpu_custom_call" | custom-call | tf_op jit(solution)/shard_map/cond/branch_1_fun/attend/pallas_call | solution.py:534
  78.9 15.9 %all_to_all.39 = bf16[64,8,640]{2,1,0:T(8,128)(2,1)S(1)} all-to-all(bf16[64,8,640]{2,1,0:T(8,128)(2,1)S(1)} %bitcast.16), channel_id=1, replica_groups=mesh['section'=2,'expert'=4,'seq'=16] {'expert','seq'}, dimensions={0} | all-to-all | bytes 1310720 | tf_op jit(solution)/shard_map/cond/branch_1_fun/all_to_all | solution.py:432
  94.8 4.4 %experts.3 = (bf16[512,2048]{1,0:T(8,128)(2,1)S(1)}, bf16[64,512]{1,0:T(8,128)(2,1)S(1)}) custom-call(bf16[512,640]{1,0:T(8,128)(2,1)S(1)} %bitcast.12, s32[1,4,8,8]{3,2,1,0:T(8,128)} %get-tuple-element.71.ids_in, f32[1,4,8,8]{3,2,1,0:T(8,128)} %get-tuple-element.78.gates_in, f32[1,2,2048]{2,1,0:T(2,128)} %get-tuple-element.73.gains_in, ...), custom_call_target="tpu_custom_call" | custom-call | tf_op jit(solution)/shard_map/cond/branch_1_fun/experts/pallas_call | solution.py:457
  99.2 22.9 %all_to_all.40 = bf16[64,8,2048]{2,1,0:T(8,128)(2,1)S(1)} all-to-all(bf16[64,8,2048]{2,1,0:T(8,128)(2,1)S(1)} %bitcast.15), channel_id=1, replica_groups=mesh['section'=2,'expert'=4,'seq'=16] {'expert','seq'}, dimensions={0} | all-to-all | bytes 4194304 | tf_op jit(solution)/shard_map/cond/branch_1_fun/all_to_all | solution.py:432
  122.2 0.5 mix.3
  122.8 0.1 collective-permute-start.3
  122.9 1.3 %collective-permute-done.3.got = bf16[32,2048]{1,0:T(8,128)(2,1)S(1)} collective-permute-done((bf16[32,2048]{1,0:T(8,128)(2,1)S(1)}, bf16[32,2048]{1,0:T(8,128)(2,1)S(1)}, u32[]{:S(2)}, u32[]{:S(2)}) %collective-permute-start.3) | collective-permute-done | bytes 131104 | tf_op jit(solution)/shard_map/ppermute | solution.py:428
  124.2 0.0 copy-done
  124.2 0.0 copy-done.1
  124.2 1.1 head.1
  (1 shorter events, 0.0 us)
Async XLA Ops:
  0.0 2.9 %collective-permute-start.1 = (bf16[32,2048]{1,0:T(8,128)(2,1)}, bf16[32,2048]{1,0:T(8,128)(2,1)S(1)}, u32[]{:S(2)}, u32[]{:S(2)}) collective-permute-start(bf16[32,2048]{1,0:T(8,128)(2,1)} %table.1), channel_id=1, source_target_pairs={{0,64},{64,0},{1,65},{65,1},{2,66},{66,2},{3,67},{67,3},{4,68},{68... | collective-permute-start | bytes 393224 | tf_op jit(solution)/shard_map/ppermute | solution.py:428
  1.4 1.5 %collective-permute-start = (bf16[2,8,2048]{2,1,0:T(8,128)(2,1)}, bf16[2,8,2048]{2,1,0:T(8,128)(2,1)S(1)}, u32[]{:S(2)}, u32[]{:S(2)}) collective-permute-start(bf16[2,8,2048]{2,1,0:T(8,128)(2,1)} %param.16), channel_id=1, source_target_pairs={{0,64},{64,0},{1,65},{65,1},{2,66},{66,2},{3,67},{67,3},{4,68},{68... | collective-permute-start | bytes 196616 | tf_op jit(solution)/shard_map/ppermute | solution.py:428
  52.2 23.1 %collective-permute-start.2 = (bf16[32,2048]{1,0:T(8,128)(2,1)S(1)}, bf16[32,2048]{1,0:T(8,128)(2,1)S(1)}, u32[]{:S(2)}, u32[]{:S(2)}) collective-permute-start(bf16[32,2048]{1,0:T(8,128)(2,1)S(1)} %get-tuple-element.87), channel_id=1, source_target_pairs={{0,64},{64,0},{1,65},{65,1},{2,66},{66,2},{3,67},{67,3},{4,68},{68... | collective-permute-start | bytes 393224 | tf_op jit(solution)/shard_map/ppermute | solution.py:428
  75.3 48.9 %copy-start = (f32[2048]{0:T(1024)S(1)}, f32[2048]{0:T(1024)}, u32[]{:S(2)}) copy-start(f32[2048]{0:T(1024)} %param.27) | copy-start | bytes 24580
  75.3 48.9 %copy-start.1 = (bf16[32,2048]{1,0:T(8,128)(2,1)S(1)}, bf16[32,2048]{1,0:T(8,128)(2,1)}, u32[]{:S(2)}) copy-start(bf16[32,2048]{1,0:T(8,128)(2,1)} %table.1) | copy-start | bytes 393220
  122.8 1.4 %collective-permute-start.3 = (bf16[32,2048]{1,0:T(8,128)(2,1)S(1)}, bf16[32,2048]{1,0:T(8,128)(2,1)S(1)}, u32[]{:S(2)}, u32[]{:S(2)}) collective-permute-start(bf16[32,2048]{1,0:T(8,128)(2,1)S(1)} %get-tuple-element.94.mine), channel_id=1, source_target_pairs={{0,64},{64,0},{1,65},{65,1},{2,66},{66,2},{3,67},{67,3},{4,68},{68... | collective-permute-start | bytes 393224 | tf_op jit(solution)/shard_map/ppermute | solution.py:428

commit v6 on v5

--- a/solution.py
+++ b/solution.py
@@ -369,7 +369,6 @@
     rows = middle[...]
     for copy in copies[:3]:
         copy.wait()
-    mix_rows(ids, gates, mixing)
     moe_in = rms(rows, gains[0, 1:2, :]).astype(BF16)
     activ = []
     for j in range(CHUNKS):
@@ -378,6 +377,7 @@
         gate_out = dot(moe_in, gate[at], ((1,), (1,)))
         up_out = dot(moe_in, up[at], ((1,), (1,)))
         activ.append((gate_out / (1.0 + jnp.exp(-gate_out)) * up_out).astype(BF16))
+    mix_rows(ids, gates, mixing)
     total = jnp.zeros((T, D), F32)
     for j in range(CHUNKS):
         copies[3 + CHUNKS + j].wait()

time: 126 us -> 126 us (level)
  no operation moved by 1% of the time
where the time goes in v6:
time: 126 us
  blocking collectives  83.8 us (67%)
  starting transfers between devices  23.8 us (19%)
  Pallas kernels  14 us (11%)
  waiting for transfers between devices  3.79 us (3%)
    all_to_all x1, blocking collectives, traded(): lax.all_to_all(parts, 'seq', 0, 0, axis_index_groups=groups, tiled=True)  45 us
    all_to_all x2, blocking collectives, exchanged(): return lax.all_to_all(value, ('expert', 'seq'), 0, 0, tiled=True)  38.8 us
    ppermute x4, starting transfers between devices, swapped(): return lax.ppermute(value, 'section', [(0, 1), (1, 0)])  23.8 us
    pallas_call x1, Pallas kernels, experts(): call(functools.partial(expert_body, width), 'experts', [vmem()] + [hbm()]...  4.64 us
    pallas_call x1, Pallas kernels, traded(): pl.pallas_call(trade_body, name='trade', in_specs=[hbm()], out_specs=hbm(...  4.29 us
    ppermute x4, waiting for transfers between devices, swapped(): return lax.ppermute(value, 'section', [(0, 1), (1, 0)])  3.79 us
    pallas_call x1, Pallas kernels, second(): call(attend_body, 'attend', [hbm()] * 5 + [vmem()], (shape(width, share +...  3.54 us
  transfers between devices with their start and end apart: 4, of which 3 were waited for; matrix products, arithmetic and copies ran while one was open for 0% of the time, Pallas kernels for 0%

profile of v6, /device:TPU:1, one launch (start us, length us, event | category | flops | bytes accessed | tf_op | source)
XLA Modules:
  0.0 125.7 jit_solution(3616258859412104359)
XLA Ops:
  0.0 1.4 %collective-permute-start.1 = (bf16[32,2048]{1,0:T(8,128)(2,1)}, bf16[32,2048]{1,0:T(8,128)(2,1)S(1)}, u32[]{:S(2)}, u32[]{:S(2)}) collective-permute-start(bf16[32,2048]{1,0:T(8,128)(2,1)} %table.1), channel_id=1, source_target_pairs={{0,64},{64,0},{1,65},{65,1},{2,66},{66,2},{3,67},{67,3},{4,68},{68... | collective-permute-start | bytes 393224 | tf_op jit(solution)/shard_map/ppermute | solution.py:428
  1.4 0.0 collective-permute-start
  1.4 1.5 %collective-permute-done = bf16[2,8,2048]{2,1,0:T(8,128)(2,1)S(1)} collective-permute-done((bf16[2,8,2048]{2,1,0:T(8,128)(2,1)}, bf16[2,8,2048]{2,1,0:T(8,128)(2,1)S(1)}, u32[]{:S(2)}, u32[]{:S(2)}) %collective-permute-start) | collective-permute-done | bytes 65568 | tf_op jit(solution)/shard_map/ppermute | solution.py:428
  2.9 0.0 collective-permute-done.1
  2.9 49.3 %conditional.2 = (bf16[32,2048]{1,0:T(8,128)(2,1)S(1)}, bf16[4,8,2,256,128]{4,3,2,1,0:T(8,128)(2,1)}) conditional(s32[]{:T(128)} %convert_element_type.7, bf16[1,8,2,256,512]{4,3,2,1,0:T(8,128)(2,1)} %param.17, (s32[1,4,8,8]{3,2,1,0:T(8,128)}, s32[4,8]{1,0:T(4,128)}, f32[1,2,2048]{2,1,0:T(2,128)}, bf16[1,8,2,256,512]{4,3,2,1,0:T(8,128)(2,1)}, ...), branch_computations={%region_0.0_spmd, %region_1.0_spmd} | conditional | bytes 9175056 | solution.py:558
  2.9 4.3 %trade.1 = bf16[4,8,2,256,128]{4,3,2,1,0:T(8,128)(2,1)} custom-call(bf16[1,8,2,256,512]{4,3,2,1,0:T(8,128)(2,1)} %cache), custom_call_target="tpu_custom_call" | custom-call | tf_op jit(solution)/shard_map/cond/branch_0_fun/trade/pallas_call | solution.py:437
  7.2 45.0 %all_to_all.36 = bf16[4,8,2,256,128]{4,3,2,1,0:T(8,128)(2,1)} all-to-all(bf16[4,8,2,256,128]{4,3,2,1,0:T(8,128)(2,1)} %trade.1), channel_id=1, replica_groups={{0,1,2,3},{4,5,6,7},{8,9,10,11},{12,13,14,15},{16,17,18,19},{20,21,22,2..., dimensions={0} | all-to-all | bytes 8388608 | tf_op jit(solution)/shard_map/cond/branch_0_fun/all_to_all | solution.py:452
  52.2 22.3 %collective-permute-start.2 = (bf16[32,2048]{1,0:T(8,128)(2,1)S(1)}, bf16[32,2048]{1,0:T(8,128)(2,1)S(1)}, u32[]{:S(2)}, u32[]{:S(2)}) collective-permute-start(bf16[32,2048]{1,0:T(8,128)(2,1)S(1)} %get-tuple-element.87), channel_id=1, source_target_pairs={{0,64},{64,0},{1,65},{65,1},{2,66},{66,2},{3,67},{67,3},{4,68},{68... | collective-permute-start | bytes 393224 | tf_op jit(solution)/shard_map/ppermute | solution.py:428
  74.5 1.0 collective-permute-done.2
  75.5 0.0 copy-start
  75.5 0.0 copy-start.1
  75.5 47.7 %conditional.3 = (bf16[32,2048]{1,0:T(8,128)(2,1)S(1)}) conditional(s32[]{:T(128)} %convert_element_type.6, () %tuple.19, (s32[1,4,8,8]{3,2,1,0:T(8,128)}, s32[4,8]{1,0:T(4,128)}, f32[1,2,2048]{2,1,0:T(2,128)}, bf16[4,8,2,256,128]{4,3,2,1,0:T(8,128)(2,1)}, bf16[1,1,768,2048]{3,2,1,0:T(8,128)(2,1)}, /*index=5*/bf16[32,2048]{1,0:T(8,128)(2,1)S(1)}, ...), branch_computations={%region_2.0_spmd, %region_3.0_spmd} | conditional | bytes 5505032 | solution.py:571
  75.5 3.5 %attend.1 = (bf16[512,640]{1,0:T(8,128)(2,1)S(1)}, bf16[768,2048]{1,0:T(8,128)(2,1)S(1)}) custom-call(s32[1,4,8,8]{3,2,1,0:T(8,128)} %get-tuple-element.71.ids_in, s32[4,8]{1,0:T(4,128)} %get-tuple-element.72.lengths_in, f32[1,2,2048]{2,1,0:T(2,128)} %get-tuple-element.73.gains_in, bf16[4,8,2,256,128]{4,3,2,1,0:T(8,128)(2,1)} %get-tuple-element.74.cache, ...), custom_call_target="tpu_custom_call" | custom-call | tf_op jit(solution)/shard_map/cond/branch_1_fun/attend/pallas_call | solution.py:534
  79.1 15.9 %all_to_all.39 = bf16[64,8,640]{2,1,0:T(8,128)(2,1)S(1)} all-to-all(bf16[64,8,640]{2,1,0:T(8,128)(2,1)S(1)} %bitcast.16), channel_id=1, replica_groups=mesh['section'=2,'expert'=4,'seq'=16] {'expert','seq'}, dimensions={0} | all-to-all | bytes 1310720 | tf_op jit(solution)/shard_map/cond/branch_1_fun/all_to_all | solution.py:432
  95.0 4.6 %experts.3 = (bf16[512,2048]{1,0:T(8,128)(2,1)S(1)}, bf16[64,512]{1,0:T(8,128)(2,1)S(1)}) custom-call(bf16[512,640]{1,0:T(8,128)(2,1)S(1)} %bitcast.12, s32[1,4,8,8]{3,2,1,0:T(8,128)} %get-tuple-element.71.ids_in, f32[1,4,8,8]{3,2,1,0:T(8,128)} %get-tuple-element.78.gates_in, f32[1,2,2048]{2,1,0:T(2,128)} %get-tuple-element.73.gains_in, ...), custom_call_target="tpu_custom_call" | custom-call | tf_op jit(solution)/shard_map/cond/branch_1_fun/experts/pallas_call | solution.py:457
  99.6 22.9 %all_to_all.40 = bf16[64,8,2048]{2,1,0:T(8,128)(2,1)S(1)} all-to-all(bf16[64,8,2048]{2,1,0:T(8,128)(2,1)S(1)} %bitcast.15), channel_id=1, replica_groups=mesh['section'=2,'expert'=4,'seq'=16] {'expert','seq'}, dimensions={0} | all-to-all | bytes 4194304 | tf_op jit(solution)/shard_map/cond/branch_1_fun/all_to_all | solution.py:432
  122.6 0.5 mix.3
  123.2 0.1 collective-permute-start.3
  123.3 1.3 %collective-permute-done.3.got = bf16[32,2048]{1,0:T(8,128)(2,1)S(1)} collective-permute-done((bf16[32,2048]{1,0:T(8,128)(2,1)S(1)}, bf16[32,2048]{1,0:T(8,128)(2,1)S(1)}, u32[]{:S(2)}, u32[]{:S(2)}) %collective-permute-start.3) | collective-permute-done | bytes 131104 | tf_op jit(solution)/shard_map/ppermute | solution.py:428
  124.6 0.0 copy-done
  124.6 0.0 copy-done.1
  124.6 1.1 head.1
  (1 shorter events, 0.0 us)
Async XLA Ops:
  0.0 2.9 %collective-permute-start.1 = (bf16[32,2048]{1,0:T(8,128)(2,1)}, bf16[32,2048]{1,0:T(8,128)(2,1)S(1)}, u32[]{:S(2)}, u32[]{:S(2)}) collective-permute-start(bf16[32,2048]{1,0:T(8,128)(2,1)} %table.1), channel_id=1, source_target_pairs={{0,64},{64,0},{1,65},{65,1},{2,66},{66,2},{3,67},{67,3},{4,68},{68... | collective-permute-start | bytes 393224 | tf_op jit(solution)/shard_map/ppermute | solution.py:428
  1.4 1.5 %collective-permute-start = (bf16[2,8,2048]{2,1,0:T(8,128)(2,1)}, bf16[2,8,2048]{2,1,0:T(8,128)(2,1)S(1)}, u32[]{:S(2)}, u32[]{:S(2)}) collective-permute-start(bf16[2,8,2048]{2,1,0:T(8,128)(2,1)} %param.16), channel_id=1, source_target_pairs={{0,64},{64,0},{1,65},{65,1},{2,66},{66,2},{3,67},{67,3},{4,68},{68... | collective-permute-start | bytes 196616 | tf_op jit(solution)/shard_map/ppermute | solution.py:428
  52.2 23.3 %collective-permute-start.2 = (bf16[32,2048]{1,0:T(8,128)(2,1)S(1)}, bf16[32,2048]{1,0:T(8,128)(2,1)S(1)}, u32[]{:S(2)}, u32[]{:S(2)}) collective-permute-start(bf16[32,2048]{1,0:T(8,128)(2,1)S(1)} %get-tuple-element.87), channel_id=1, source_target_pairs={{0,64},{64,0},{1,65},{65,1},{2,66},{66,2},{3,67},{67,3},{4,68},{68... | collective-permute-start | bytes 393224 | tf_op jit(solution)/shard_map/ppermute | solution.py:428
  75.5 49.1 %copy-start = (f32[2048]{0:T(1024)S(1)}, f32[2048]{0:T(1024)}, u32[]{:S(2)}) copy-start(f32[2048]{0:T(1024)} %param.27) | copy-start | bytes 24580
  75.5 49.1 %copy-start.1 = (bf16[32,2048]{1,0:T(8,128)(2,1)S(1)}, bf16[32,2048]{1,0:T(8,128)(2,1)}, u32[]{:S(2)}) copy-start(bf16[32,2048]{1,0:T(8,128)(2,1)} %table.1) | copy-start | bytes 393220
  123.2 1.4 %collective-permute-start.3 = (bf16[32,2048]{1,0:T(8,128)(2,1)S(1)}, bf16[32,2048]{1,0:T(8,128)(2,1)S(1)}, u32[]{:S(2)}, u32[]{:S(2)}) collective-permute-start(bf16[32,2048]{1,0:T(8,128)(2,1)S(1)} %get-tuple-element.94.mine), channel_id=1, source_target_pairs={{0,64},{64,0},{1,65},{65,1},{2,66},{66,2},{3,67},{67,3},{4,68},{68... | collective-permute-start | bytes 393224 | tf_op jit(solution)/shard_map/ppermute | solution.py:428
